TPU v7x, 32 devices: a whole 2x2x4 slice. The times are simulated.
32 devices in a mesh: light: 4 (over y, x), view: 8 (over z, core).
Axes of the slice: x: 2, y: 2, z: 4, core: 2. Of those that a mesh axis runs over, the one named last changes fastest.
Arguments:
- density: float32 [64, 256, 4096], P('view', 'light'), may hold values from 0 to 1
- tables: float32 [8, 4, 16], replicated, may hold values from 0.2 to 2
- table_index: int32 [4, 8], P('light', 'view'), may hold values from 0 to 7
- light_code: int32 [4], replicated, may hold values from -1 to 1, as said below
- light_tint: float32 [4, 3], replicated, may hold values from 0.25 to 1
Outputs:
- image: float32 [4, 256, 4096], P(None, ('light', 'view'))
Inputs may be any that keep to these rules, and one draw needn't show every extreme that they name: `light_code`: each of -1, 0 and 1 occurs.
All inputs are finite; a program needn't handle non-finite values.
Results may differ from a plain program's by a relative error of at most 0.0003.
Values sent between devices are 32-bit elements; how exact they have to be, the bound alone decides.
No kernel may reach another device: no remote copies, remote signals or barrier semaphores. Data moves between devices by JAX's collectives and lax.ppermute only.
A program may use at most 256 MiB of HBM per device.

v0:
```python
import functools
import math

import jax
import jax.numpy as jnp
from jax import lax
from jax.experimental import pallas as pl
from jax.experimental.pallas import tpu as pltpu
from jax.sharding import PartitionSpec as P

LANE = 128
SUB = 8
DRIFTS = (-1, 0, 1)
VMEM_LIMIT = 48 * 2**20
F32 = jnp.float32


def params():
    return pltpu.CompilerParams(vmem_limit_bytes=VMEM_LIMIT)


def bit_reversed(value, bits):
    return sum((value >> at & 1) << bits - 1 - at for at in range(bits))


def rows_of(table, index):
    return jnp.take_along_axis(table, index, axis=0, mode="promise_in_bounds")


def fill_coefficients(which, tables_ref, coef, sigma_scale, properties):
    rows = tables_ref[which]
    knots = rows.shape[1]
    at_row = lax.broadcasted_iota(jnp.int32, (2 * SUB, knots), 0)
    at_col = lax.broadcasted_iota(jnp.int32, (2 * SUB, knots), 1)
    left_at = jnp.minimum(at_row, knots - 2)
    for q in range(properties):
        row = jnp.broadcast_to(rows[q : q + 1], (2 * SUB, knots))
        left = jnp.sum(jnp.where(at_col == left_at, row, 0.0), axis=1, keepdims=True)
        right = jnp.sum(jnp.where(at_col == left_at + 1, row, 0.0), axis=1, keepdims=True)
        step = right - left
        start = left - step * left_at[:, :1].astype(F32)
        scale = sigma_scale if q == 0 else 1.0
        start = jnp.broadcast_to(start * scale, (2 * SUB, LANE))
        step = jnp.broadcast_to(step * (scale * (knots - 1)), (2 * SUB, LANE))
        coef[4 * q] = start[:SUB]
        coef[4 * q + 1] = start[SUB:]
        coef[4 * q + 2] = step[:SUB]
        coef[4 * q + 3] = step[SUB:]


def place_of(cells, knots):
    knot = (cells * (knots - 1.0)).astype(jnp.int32)
    return knot & (SUB - 1), knot >= SUB


def value_at(coef, q, place, cells):
    low, high = place
    start = jnp.where(high, rows_of(coef[4 * q + 1], low), rows_of(coef[4 * q], low))
    step = jnp.where(high, rows_of(coef[4 * q + 3], low), rows_of(coef[4 * q + 2], low))
    return start + step * cells


def fetch_tile(density_ref, buffer, sems, first, tile):
    columns = pl.ds(pl.multiple_of(first + tile * LANE, LANE), LANE)
    return pltpu.make_async_copy(density_ref.at[:, :, columns], buffer.at[tile], sems.at[tile])


def sums_kernel(sigma_scale, ratio, first, bits, split, index_ref, tables_ref, density_ref, *rest):
    if split:
        leaving_ref, send_ref, keep_ref, coef, buffer, clear, sems = rest
    else:
        leaving_ref, coef, buffer, sems = rest
    tiles, layers, slices, _ = buffer.shape
    knots = tables_ref.shape[2]

    @pl.loop(0, tiles)
    def _(tile):
        fetch_tile(density_ref, buffer, sems, first, tile).start()

    fill_coefficients(index_ref[0, 0], tables_ref, coef, sigma_scale, 1)
    mine = lax.axis_index("view") & 1 if split else 0
    half = (1 << bits) // 2

    @pl.loop(0, tiles)
    def _(tile):
        fetch_tile(density_ref, buffer, sems, first, tile).wait()
        down = [jnp.zeros((SUB, LANE), F32) for _ in range(layers)]
        for block in range(slices // SUB):
            through = jnp.zeros((SUB, LANE), F32)
            for b in range(layers):
                cells = buffer[tile, b, block * SUB : block * SUB + SUB]
                sigma = value_at(coef, 0, place_of(cells, knots), cells)
                through = through + sigma
                down[b] = down[b] + sigma
            if split:
                clear[block] = jnp.exp2(through)
        columns = pl.ds(pl.multiple_of(tile * LANE, LANE), LANE)
        for b in range(layers):
            leaving_ref[b : b + 1, columns] = jnp.exp2(
                jnp.sum(down[b], axis=0, keepdims=True) * ratio
            )
        if split:
            for q in range(half):
                octet = 2 * bit_reversed(q, bits - 1)
                send_ref[q, tile] = clear[octet + 1 - mine]
                keep_ref[q, tile] = clear[octet + mine]


def fill_lighting(pieces, brick_refs, code_ref, tint_ref, lighting, first, total):
    layers, width = lighting.shape[1:]
    wide = width + 2 * LANE
    place = lax.broadcasted_iota(jnp.int32, (layers, wide), 1) + (first - LANE)
    inside = jnp.logical_and(place >= 0, place < total).astype(F32)
    mine = lax.axis_index("light")
    fronts = [inside] * len(DRIFTS)
    for apart in range(len(brick_refs), 0, -1):
        parts, at = [], first - LANE
        if at < 0:
            parts.append(jnp.zeros((layers, -at), F32))
            at = 0
        for (low, high), ref in zip(pieces, brick_refs[apart - 1]):
            stop = min(high, first + width + LANE)
            if at < stop and at >= low:
                parts.append(ref[:, at - low : stop - low])
                at = stop
        if at < first + width + LANE:
            parts.append(jnp.zeros((layers, first + width + LANE - at), F32))
        leaving = jnp.concatenate(parts, axis=1)
        active = mine >= apart
        result = []
        shared = None
        for drift, front in zip(DRIFTS, fronts):
            if shared is None or apart < len(brick_refs):
                row = front * leaving
                shared = 0.5 * row + 0.25 * (pltpu.roll(row, 1, 1) + pltpu.roll(row, wide - 1, 1))
            moved = shared if drift == 0 else pltpu.roll(shared, drift % wide, 1)
            result.append(jnp.where(active, moved * inside, front))
        fronts = result
    for k in range(lighting.shape[0]):
        shade = jnp.zeros((layers, wide), F32)
        for drift, front in zip(DRIFTS, fronts):
            tint = 0.0
            for light in range(tint_ref.shape[0]):
                tint = tint + jnp.where(code_ref[light] == drift, tint_ref[light, k], 0.0)
            shade = shade + tint * front
        lighting[k] = shade[:, LANE : LANE + width]


def shade_kernel(
    sigma_scale, ratio, first, total, bits, pieces, far, whole_out,
    index_ref, code_ref, tint_ref, tables_ref, density_ref, *rest,
):
    brick_refs = [rest[at * len(pieces) : (at + 1) * len(pieces)] for at in range(far)]
    rest = rest[far * len(pieces) :]
    if whole_out:
        out_ref, coef, buffer, lighting, sums, sems = rest
    else:
        send_ref, keep_ref, coef, buffer, lighting, sums, sems = rest
    tiles, layers, slices, _ = buffer.shape
    knots = tables_ref.shape[2]
    steps = slices // SUB
    channels = lighting.shape[0]

    @pl.loop(0, tiles)
    def _(tile):
        fetch_tile(density_ref, buffer, sems, first, tile).start()

    fill_coefficients(index_ref[0, 0], tables_ref, coef, sigma_scale, tables_ref.shape[1])
    fill_lighting(pieces, brick_refs, code_ref, tint_ref, lighting, first, total)
    mine = lax.axis_index("view") & 1
    sublane = lax.broadcasted_iota(jnp.int32, (SUB, LANE), 0)

    @pl.loop(0, tiles)
    def _(tile):
        fetch_tile(density_ref, buffer, sems, first, tile).wait()
        columns = pl.ds(pl.multiple_of(tile * LANE, LANE), LANE)
        ahead = [None] * steps
        for b in range(layers):
            lit = [
                jnp.broadcast_to(lighting[k, b : b + 1, columns], (SUB, LANE))
                for k in range(channels)
            ]
            cells, places, sigma = [], [], []
            for j in range(steps):
                cells.append(buffer[tile, b, pl.ds(j, SUB, stride=steps), :])
                places.append(place_of(cells[j], knots))
                sigma.append(value_at(coef, 0, places[j], cells[j]))
            before, running = [], None
            for j in range(steps):
                before.append(running)
                running = sigma[j] if running is None else running + sigma[j]
            earlier = running
            for hop in (1, 2, 4):
                earlier = earlier + jnp.where(sublane >= hop, pltpu.roll(earlier, hop, 0), 0.0)
            earlier = earlier - running
            for j in range(steps):
                inside = earlier if j == 0 else earlier + before[j]
                shadow = jnp.exp2(inside * ratio)
                passed = jnp.exp2(sigma[j])
                if b == 0:
                    after = passed
                    weight = (1.0 - passed) * shadow
                else:
                    after = ahead[j] * passed
                    weight = (ahead[j] - after) * shadow
                ahead[j] = after
                rows = pl.ds(j * SUB, SUB)
                for k in range(channels):
                    term = value_at(coef, k + 1, places[j], cells[j]) * (weight * lit[k])
                    if b == 0:
                        sums[k, rows] = term
                    else:
                        sums[k, rows] = sums[k, rows] + term
        if whole_out:
            for j in range(steps):
                sums[channels, pl.ds(j * SUB, SUB)] = ahead[j]
            for octet in range(SUB):
                for k in range(channels + 1):
                    for part in range(steps // SUB):
                        out_ref[k, tile, pl.ds(octet * steps + part * SUB, SUB)] = sums[
                            k, pl.ds(part * SUB * SUB + octet, SUB, stride=SUB), :
                        ]
        else:
            for q in range(1 << bits - 1):
                octet = 2 * bit_reversed(q, bits - 1)
                for k in range(channels):
                    send_ref[q, k, tile] = sums[k, pl.ds(octet + 1 - mine, SUB, stride=SUB), :]
                    keep_ref[q, k, tile] = sums[k, pl.ds(octet + mine, SUB, stride=SUB), :]


VMEM = functools.partial(pl.BlockSpec, memory_space=pltpu.VMEM)
SMEM = functools.partial(pl.BlockSpec, memory_space=pltpu.SMEM)
ANY = functools.partial(pl.BlockSpec, memory_space=pl.ANY)


def shape(*dims):
    return jax.ShapeDtypeStruct(dims, F32)


def cost(density, columns, per_cell):
    cells = density.shape[0] * density.shape[1] * columns
    return pl.CostEstimate(flops=cells * per_cell, bytes_accessed=4 * cells, transcendentals=0)


def sums(density, tables, index, low, high, sigma_scale, ratio, bits, split):
    layers, slices, _ = density.shape
    tiles = (high - low) // LANE
    half = (1 << bits) // 2
    outs = [shape(layers, high - low)]
    scratch = [pltpu.VMEM((4, SUB, LANE), F32), pltpu.VMEM((tiles, layers, slices, LANE), F32)]
    if split:
        outs += [shape(half, tiles, SUB, LANE)] * 2
        scratch.append(pltpu.VMEM((slices // SUB, SUB, LANE), F32))
    scratch.append(pltpu.SemaphoreType.DMA((tiles,)))
    return pl.pallas_call(
        functools.partial(sums_kernel, sigma_scale, ratio, low, bits, split),
        in_specs=[SMEM(), VMEM(), ANY()],
        out_specs=[VMEM()] * len(outs),
        out_shape=outs,
        scratch_shapes=scratch,
        compiler_params=params(),
        cost_estimate=cost(density, high - low, 16),
        name="sums",
    )(index, tables, density)


def shade(density, tables, index, code, tint, bricks, pieces, low, high, sigma_scale, ratio, bits, whole_out):
    layers, slices, total = density.shape
    channels = tint.shape[1]
    tiles = (high - low) // LANE
    half = (1 << bits) // 2
    if whole_out:
        outs = [shape(channels + 1, tiles, slices, LANE)]
    else:
        outs = [shape(half, channels, tiles, SUB, LANE)] * 2
    used = [at for at, (start, stop) in enumerate(pieces) if start < high + LANE and stop > low - LANE]
    operands = [rows[at] for rows in bricks for at in used]
    return pl.pallas_call(
        functools.partial(
            shade_kernel, sigma_scale, ratio, low, total, bits,
            tuple(pieces[at] for at in used), len(bricks), whole_out,
        ),
        in_specs=[SMEM()] * 3 + [VMEM(), ANY()] + [VMEM()] * len(operands),
        out_specs=[VMEM()] * len(outs),
        out_shape=outs,
        scratch_shapes=[
            pltpu.VMEM((4 * tables.shape[1], SUB, LANE), F32),
            pltpu.VMEM((tiles, layers, slices, LANE), F32),
            pltpu.VMEM((channels, layers, high - low), F32),
            pltpu.VMEM((channels + 1, slices, LANE), F32),
            pltpu.SemaphoreType.DMA((tiles,)),
        ],
        compiler_params=params(),
        cost_estimate=cost(density, high - low, 60),
        name="shade",
    )(index, code, tint, tables, density, *operands)


def merge_clear_kernel(bit, own_ref, other_ref, send_ref, keep_ref):
    half = send_ref.shape[0]
    mine = lax.axis_index("view") >> bit + 1 & 1
    for at in range(half):
        there, here = (1 - mine) * half + at, mine * half + at
        send_ref[at] = own_ref[there] * other_ref[there]
        keep_ref[at] = own_ref[here] * other_ref[here]


def merge_clear(own, other, bit):
    half = shape(own.shape[0] // 2, *own.shape[1:])
    return pl.pallas_call(
        functools.partial(merge_clear_kernel, bit),
        in_specs=[VMEM()] * 2,
        out_specs=[VMEM()] * 2,
        out_shape=[half] * 2,
        compiler_params=params(),
        name="merge_clear",
    )(own, other)


def merge_kernel(bit, own_ref, other_ref, own_clear_ref, other_clear_ref, send_ref, keep_ref):
    half = send_ref.shape[0]
    me = lax.axis_index("view")
    mine = me >> bit + 1 & 1

    def merged(front_ref, back_ref, clear_ref):
        for at in range(half):
            for to_ref, side in ((send_ref, 1 - mine), (keep_ref, mine)):
                source = side * half + at
                clear = clear_ref[source]
                for k in range(send_ref.shape[1]):
                    to_ref[at, k] = front_ref[source, k] + clear * back_ref[source, k]

    upper = me >> bit & 1 == 1

    @pl.when(upper)
    def _():
        merged(other_ref, own_ref, other_clear_ref)

    @pl.when(jnp.logical_not(upper))
    def _():
        merged(own_ref, other_ref, own_clear_ref)


def unit_of(low, high):
    return math.gcd(low // LANE, (high - low) // LANE)


def merge(own, other, own_clear, other_clear, bit, low, high):
    count, channels, tiles = own.shape[:3]
    unit = unit_of(low, high)
    start = low // LANE // unit
    half = count // 2
    data = lambda n: pl.BlockSpec((n, channels, unit, SUB, LANE), lambda i: (0, 0, i, 0, 0))
    clear = pl.BlockSpec((count, unit, SUB, LANE), lambda i: (0, start + i, 0, 0))
    return pl.pallas_call(
        functools.partial(merge_kernel, bit),
        grid=(tiles // unit,),
        in_specs=[data(count)] * 2 + [clear] * 2,
        out_specs=[data(half)] * 2,
        out_shape=[shape(half, *own.shape[1:])] * 2,
        compiler_params=params(),
        name="merge",
    )(own, other, own_clear, other_clear)


def last_kernel(bit, own_ref, other_ref, own_clear_ref, other_clear_ref, *rest):
    image_ref = rest[-1]
    channels, tiles = own_ref.shape[1:3]

    def merged(front_ref, back_ref, clear_ref):
        for tile in range(tiles):
            columns = slice(tile * LANE, tile * LANE + LANE)
            clear = clear_ref[0, tile]
            for k in range(channels):
                image_ref[k, :, columns] = front_ref[0, k, tile] + clear * back_ref[0, k, tile]
            image_ref[channels, :, columns] = own_clear_ref[0, tile] * other_clear_ref[0, tile]

    upper = lax.axis_index("view") >> bit & 1 == 1

    @pl.when(upper)
    def _():
        merged(other_ref, own_ref, other_clear_ref)

    @pl.when(jnp.logical_not(upper))
    def _():
        merged(own_ref, other_ref, own_clear_ref)


def last(own, other, own_clear, other_clear, bit, low, high, total, image):
    _, channels, tiles = own.shape[:3]
    unit = unit_of(low, high)
    start = low // LANE // unit
    data = pl.BlockSpec((1, channels, unit, SUB, LANE), lambda i: (0, 0, i, 0, 0))
    clear = pl.BlockSpec((1, unit, SUB, LANE), lambda i: (0, start + i, 0, 0))
    before = [] if image is None else [image]
    return pl.pallas_call(
        functools.partial(last_kernel, bit),
        grid=(tiles // unit,),
        in_specs=[data] * 2 + [clear] * 2 + [ANY()] * len(before),
        out_specs=pl.BlockSpec((channels + 1, SUB, unit * LANE), lambda i: (0, 0, start + i)),
        out_shape=shape(channels + 1, SUB, total),
        input_output_aliases={4: 0} if before else {},
        compiler_params=params(),
        name="last",
    )(own, other, own_clear, other_clear, *before)


def swap(block, bit):
    count = lax.axis_size("view")
    return lax.ppermute(block, "view", [(at, at ^ 1 << bit) for at in range(count)])


def from_earlier(leaving):
    count = lax.axis_size("light")
    return [
        lax.ppermute(leaving, "light", [(at, at + apart) for at in range(count - apart)])
        for apart in range(1, count)
    ]


def composite_over(front, back):
    clear = front[-1:]
    return jnp.concatenate([front[:-1] + clear * back[:-1], clear * back[-1:]])


def plain(density, tables, table_index, light_code, light_tint, sigma_scale, ratio, bits):
    slices, total = density.shape[1:]
    [leaving] = sums(density, tables, table_index, 0, total, sigma_scale, ratio, 0, False)
    bricks = [[row] for row in from_earlier(leaving)]
    parts = shade(
        density, tables, table_index, light_code, light_tint, bricks, [(0, total)], 0, total,
        sigma_scale, ratio, 0, True,
    )[0]
    rows = slices >> bits
    depth = parts.shape[0]
    current = parts.transpose(0, 2, 1, 3).reshape((depth,) + (2,) * bits + (rows, total))
    current = current.transpose((0,) + tuple(range(bits, 0, -1)) + (bits + 1, bits + 2))
    for bit in range(bits):
        upper = lax.axis_index("view") >> bit & 1 == 1
        first, second = current[:, 0], current[:, 1]
        kept = jnp.where(upper, second, first)
        arrived = swap(jnp.where(upper, first, second), bit)
        current = composite_over(jnp.where(upper, arrived, kept), jnp.where(upper, kept, arrived))
    return current.reshape(depth, rows, total)


LIGHT_CUTS = (0.28125,)
CUTS = (0.25, 0.625)


def ranges(cuts, total):
    ends = [0] + [round(total * cut / LANE) * LANE for cut in cuts] + [total]
    return list(zip(ends[:-1], ends[1:]))


def local(density, tables, table_index, light_code, light_tint):
    layers, slices, total = density.shape
    views = lax.axis_size("view")
    bits = views.bit_length() - 1
    sigma_scale = -math.log2(math.e) / (layers * views)
    ratio = layers * views / (slices * lax.axis_size("light"))
    if views * SUB != slices:
        return plain(
            density, tables, table_index, light_code, light_tint, sigma_scale, ratio, bits
        )
    pieces = ranges(LIGHT_CUTS, total)
    bricks = [[] for _ in range(lax.axis_size("light") - 1)]
    clears = []
    for low, high in pieces:
        leaving, *halves = sums(
            density, tables, table_index, low, high, sigma_scale, ratio, bits, True
        )
        clears.append(halves)
        for rows, row in zip(bricks, from_earlier(leaving)):
            rows.append(row)
    send, keep = (jnp.concatenate(parts, axis=1) for parts in zip(*clears))
    clear = []
    for bit in range(bits):
        clear.append((keep, swap(send, bit)))
        if bit < bits - 1:
            send, keep = merge_clear(*clear[bit], bit)
    image = None
    for low, high in ranges(CUTS, total):
        send, keep = shade(
            density, tables, table_index, light_code, light_tint, bricks, pieces, low, high,
            sigma_scale, ratio, bits, False,
        )
        for bit in range(bits - 1):
            send, keep = merge(keep, swap(send, bit), *clear[bit], bit, low, high)
        bit = bits - 1
        image = last(keep, swap(send, bit), *clear[bit], bit, low, high, total, image)
    return image


def solution(mesh):
    return jax.shard_map(
        local,
        mesh=mesh,
        in_specs=(P("view", "light", None), P(), P("light", "view"), P(), P()),
        out_specs=P(None, ("light", "view"), None),
        check_vma=False,
    )
```

profile of v0, /device:TPU:0, one launch (start us, length us, event | category | flops | bytes accessed | tf_op | source)
XLA Modules:
  0.0 98.3 jit_solution(10293912516362054365)
XLA Ops:
  0.7 0.7 copy-done
  1.4 5.4 %sums.2 = (f32[8,2944]{1,0:T(8,128)S(1)}, f32[4,23,8,128]{3,2,1,0:T(8,128)S(1)}, f32[4,23,8,128]{3,2,1,0:T(8,128)S(1)}) custom-call(s32[1,1]{1,0:T(1,128)S(6)} %copy.11.index_ref, f32[8,4,16]{2,1,0:T(4,128)S(1)} %copy-done, f32[8,64,4096]{2,1,0:T(8,128)} %density_ref.9), custom_call_target="tpu_custom_call" | custom-call | flops 24117248 | bytes 6029312 | tf_op jit(solution)/shard_map/sums/pallas_call | solution.py:255
  6.8 4.8 %collective-permute-start = (f32[8,2944]{1,0:T(8,128)S(1)}, f32[8,2944]{1,0:T(8,128)S(1)}, u32[]{:S(2)}, u32[]{:S(2)}) collective-permute-start(f32[8,2944]{1,0:T(8,128)S(1)} %get-tuple-element.33), channel_id=1, source_target_pairs={{0,8},{8,16},{16,24},{1,9},{9,17},{17,25},{2,10},{10,18},{18,26},{... | collective-permute-start | bytes 282632 | tf_op jit(solution)/shard_map/ppermute | solution.py:416
  11.6 3.4 %collective-permute-start.1 = (f32[8,2944]{1,0:T(8,128)S(1)}, f32[8,2944]{1,0:T(8,128)S(1)}, u32[]{:S(2)}, u32[]{:S(2)}) collective-permute-start(f32[8,2944]{1,0:T(8,128)S(1)} %get-tuple-element.33), channel_id=1, source_target_pairs={{0,16},{8,24},{1,17},{9,25},{2,18},{10,26},{3,19},{11,27},{4,20},{... | collective-permute-start | bytes 282632 | tf_op jit(solution)/shard_map/ppermute | solution.py:416
  15.1 1.3 %collective-permute-start.2 = (f32[8,2944]{1,0:T(8,128)S(1)}, f32[8,2944]{1,0:T(8,128)S(1)}, u32[]{:S(2)}, u32[]{:S(2)}) collective-permute-start(f32[8,2944]{1,0:T(8,128)S(1)} %get-tuple-element.33), channel_id=1, source_target_pairs={{0,24},{1,25},{2,26},{3,27},{4,28},{5,29},{6,30},{7,31}} | collective-permute-start | bytes 282632 | tf_op jit(solution)/shard_map/ppermute | solution.py:416
  16.4 2.7 %sums.3 = (f32[8,1152]{1,0:T(8,128)S(1)}, f32[4,9,8,128]{3,2,1,0:T(8,128)S(1)}, f32[4,9,8,128]{3,2,1,0:T(8,128)S(1)}) custom-call(s32[1,1]{1,0:T(1,128)S(6)} %copy.11.index_ref, f32[8,4,16]{2,1,0:T(4,128)S(1)} %copy-done, f32[8,64,4096]{2,1,0:T(8,128)} %density_ref.9), custom_call_target="tpu_custom_call" | custom-call | flops 9437184 | bytes 2359296 | tf_op jit(solution)/shard_map/sums/pallas_call | solution.py:255
  19.1 1.3 %collective-permute-start.9 = (f32[8,1152]{1,0:T(8,128)S(1)}, f32[8,1152]{1,0:T(8,128)S(1)}, u32[]{:S(2)}, u32[]{:S(2)}) collective-permute-start(f32[8,1152]{1,0:T(8,128)S(1)} %get-tuple-element.48), channel_id=1, source_target_pairs={{0,8},{8,16},{16,24},{1,9},{9,17},{17,25},{2,10},{10,18},{18,26},{... | collective-permute-start | bytes 110600 | tf_op jit(solution)/shard_map/ppermute | solution.py:416
  20.4 1.3 %collective-permute-start.10 = (f32[8,1152]{1,0:T(8,128)S(1)}, f32[8,1152]{1,0:T(8,128)S(1)}, u32[]{:S(2)}, u32[]{:S(2)}) collective-permute-start(f32[8,1152]{1,0:T(8,128)S(1)} %get-tuple-element.48), channel_id=1, source_target_pairs={{0,16},{8,24},{1,17},{9,25},{2,18},{10,26},{3,19},{11,27},{4,20},{... | collective-permute-start | bytes 110600 | tf_op jit(solution)/shard_map/ppermute | solution.py:416
  21.7 1.3 %collective-permute-start.11 = (f32[8,1152]{1,0:T(8,128)S(1)}, f32[8,1152]{1,0:T(8,128)S(1)}, u32[]{:S(2)}, u32[]{:S(2)}) collective-permute-start(f32[8,1152]{1,0:T(8,128)S(1)} %get-tuple-element.48), channel_id=1, source_target_pairs={{0,24},{1,25},{2,26},{3,27},{4,28},{5,29},{6,30},{7,31}} | collective-permute-start | bytes 110600 | tf_op jit(solution)/shard_map/ppermute | solution.py:416
  23.0 8.3 %shade.3 = (f32[4,3,12,8,128]{4,3,2,1,0:T(8,128)S(1)}, f32[4,3,12,8,128]{4,3,2,1,0:T(8,128)S(1)}) custom-call(s32[1,1]{1,0:T(1,128)S(6)} %copy.11.index_ref, s32[4]{0:T(128)S(1)} %copy-done.2, f32[4,3]{1,0:T(4,128)S(1)} %copy-done.1, f32[8,4,16]{2,1,0:T(4,128)S(1)} %copy-done, f32[8,64,4096]{2,1,0:T(8,128)} %density_ref.9, ...), custom_call_target="tpu_custom_call" | custom-call | flops 47185920 | bytes 3145728 | tf_op jit(solution)/shard_map/shade/pallas_call | solution.py:278
  31.5 8.3 %shade.4 = (f32[4,3,12,8,128]{4,3,2,1,0:T(8,128)S(1)}, f32[4,3,12,8,128]{4,3,2,1,0:T(8,128)S(1)}) custom-call(s32[1,1]{1,0:T(1,128)S(6)} %copy.11.index_ref, s32[4]{0:T(128)S(1)} %copy-done.2, f32[4,3]{1,0:T(4,128)S(1)} %copy-done.1, f32[8,4,16]{2,1,0:T(4,128)S(1)} %copy-done, f32[8,64,4096]{2,1,0:T(8,128)} %density_ref.9, ...), custom_call_target="tpu_custom_call" | custom-call | flops 47185920 | bytes 3145728 | tf_op jit(solution)/shard_map/shade/pallas_call | solution.py:278
  39.8 0.5 collective-permute-start.12
  40.4 0.1 collective-permute-start.4
  40.5 6.0 %shade.5 = (f32[4,3,8,8,128]{4,3,2,1,0:T(8,128)S(1)}, f32[4,3,8,8,128]{4,3,2,1,0:T(8,128)S(1)}) custom-call(s32[1,1]{1,0:T(1,128)S(6)} %copy.11.index_ref, s32[4]{0:T(128)S(1)} %copy-done.2, f32[4,3]{1,0:T(4,128)S(1)} %copy-done.1, f32[8,4,16]{2,1,0:T(4,128)S(1)} %copy-done, f32[8,64,4096]{2,1,0:T(8,128)} %density_ref.9, ...), custom_call_target="tpu_custom_call" | custom-call | flops 31457280 | bytes 2097152 | tf_op jit(solution)/shard_map/shade/pallas_call | solution.py:278
  46.5 0.5 collective-permute-start.15
  47.2 0.4 merge.8
  47.6 1.6 %collective-permute-start.13 = (f32[2,3,12,8,128]{4,3,2,1,0:T(8,128)S(1)}, f32[2,3,12,8,128]{4,3,2,1,0:T(8,128)S(1)}, u32[]{:S(2)}, u32[]{:S(2)}) collective-permute-start(f32[2,3,12,8,128]{4,3,2,1,0:T(8,128)S(1)} %get-tuple-element.52), channel_id=1, source_target_pairs={{0,2},{1,3},{2,0},{3,1},{4,6},{5,7},{6,4},{7,5},{8,10},{9,11},{10,... | collective-permute-start | bytes 884744 | tf_op jit(solution)/shard_map/ppermute | solution.py:410
  49.2 0.4 merge.6
  49.6 0.5 collective-permute-start.5
  50.1 1.6 %collective-permute-start.6 = (f32[2,32,8,128]{3,2,1,0:T(8,128)S(1)}, f32[2,32,8,128]{3,2,1,0:T(8,128)S(1)}, u32[]{:S(2)}, u32[]{:S(2)}) collective-permute-start(f32[2,32,8,128]{3,2,1,0:T(8,128)S(1)} %get-tuple-element.43), channel_id=1, source_target_pairs={{0,2},{1,3},{2,0},{3,1},{4,6},{5,7},{6,4},{7,5},{8,10},{9,11},{10,... | collective-permute-start | bytes 786440 | tf_op jit(solution)/shard_map/ppermute | solution.py:410
  51.9 0.5 collective-permute-start.16
  52.4 17.0 %collective-permute-done.6.other_clear_ref.other_ref = f32[2,32,8,128]{3,2,1,0:T(8,128)S(1)} collective-permute-done((f32[2,32,8,128]{3,2,1,0:T(8,128)S(1)}, f32[2,32,8,128]{3,2,1,0:T(8,128)S(1)}, u32[]{:S(2)}, u32[]{:S(2)}) %collective-permute-start.6) | collective-permute-done | bytes 262176 | tf_op jit(solution)/shard_map/ppermute | solution.py:410
  69.4 0.3 merge.9
  69.7 2.7 %collective-permute-start.14 = (f32[1,3,12,8,128]{4,3,2,1,0:T(8,128)S(1)}, f32[1,3,12,8,128]{4,3,2,1,0:T(8,128)S(1)}, u32[]{:S(2)}, u32[]{:S(2)}) collective-permute-start(f32[1,3,12,8,128]{4,3,2,1,0:T(8,128)S(1)} %get-tuple-element.54), channel_id=1, source_target_pairs={{0,4},{1,5},{2,6},{3,7},{4,0},{5,1},{6,2},{7,3},{8,12},{9,13},{10,... | collective-permute-start | bytes 442376 | tf_op jit(solution)/shard_map/ppermute | solution.py:410
  72.4 0.3 merge.7
  72.7 0.4 collective-permute-start.7
  73.1 2.6 %collective-permute-start.8 = (f32[1,32,8,128]{3,2,1,0:T(8,128)S(1)}, f32[1,32,8,128]{3,2,1,0:T(8,128)S(1)}, u32[]{:S(2)}, u32[]{:S(2)}) collective-permute-start(f32[1,32,8,128]{3,2,1,0:T(8,128)S(1)} %get-tuple-element.47), channel_id=1, source_target_pairs={{0,4},{1,5},{2,6},{3,7},{4,0},{5,1},{6,2},{7,3},{8,12},{9,13},{10,... | collective-permute-start | bytes 393224 | tf_op jit(solution)/shard_map/ppermute | solution.py:410
  75.8 0.5 collective-permute-start.17
  76.3 18.6 %collective-permute-done.17.other_ref = f32[1,3,8,8,128]{4,3,2,1,0:T(8,128)S(1)} collective-permute-done((f32[1,3,8,8,128]{4,3,2,1,0:T(8,128)S(1)}, f32[1,3,8,8,128]{4,3,2,1,0:T(8,128)S(1)}, u32[]{:S(2)}, u32[]{:S(2)}) %collective-permute-start.17) | collective-permute-done | bytes 98336 | tf_op jit(solution)/shard_map/ppermute | solution.py:410
  94.9 0.7 last.3.rest_0_
  95.6 1.3 %last.4.rest_0_ = f32[4,8,4096]{2,1,0:T(8,128)} custom-call(f32[1,3,12,8,128]{4,3,2,1,0:T(8,128)S(1)} %get-tuple-element.53.own_ref, f32[1,3,12,8,128]{4,3,2,1,0:T(8,128)S(1)} %collective-permute-done.14.other_ref, f32[1,32,8,128]{3,2,1,0:T(8,128)S(1)} %get-tuple-element.46.own_clear_ref, ...), custom_call_target="tpu_custom_call", output_to_operand_aliasing={{}: (4, {})} | custom-call | tf_op jit(solution)/shard_map/last/pallas_call | solution.py:396
  96.9 1.3 %last.5 = f32[4,8,4096]{2,1,0:T(8,128)} custom-call(f32[1,3,12,8,128]{4,3,2,1,0:T(8,128)S(1)} %get-tuple-element.44.own_ref, f32[1,3,12,8,128]{4,3,2,1,0:T(8,128)S(1)} %collective-permute-done.7.other_ref, f32[1,32,8,128]{3,2,1,0:T(8,128)S(1)} %get-tuple-element.46.own_clear_ref, ...), custom_call_target="tpu_custom_call", output_to_operand_aliasing={{}: (4, {})} | custom-call | tf_op jit(solution)/shard_map/last/pallas_call | solution.py:396
  (29 shorter events, 0.4 us)
Async XLA Ops:
  0.7 0.7 copy-start
  1.4 21.6 %copy-start.1 = (f32[4,3]{1,0:T(4,128)S(1)}, f32[4,3]{1,0:T(4,128)}, u32[]{:S(2)}) copy-start(f32[4,3]{1,0:T(4,128)} %tint_ref.5) | copy-start | bytes 148
  1.4 21.7 %copy-start.2 = (s32[4]{0:T(128)S(1)}, s32[4]{0:T(128)}, u32[]{:S(2)}) copy-start(s32[4]{0:T(128)} %code_ref.5) | copy-start | bytes 52
  6.8 14.9 %collective-permute-start = (f32[8,2944]{1,0:T(8,128)S(1)}, f32[8,2944]{1,0:T(8,128)S(1)}, u32[]{:S(2)}, u32[]{:S(2)}) collective-permute-start(f32[8,2944]{1,0:T(8,128)S(1)} %get-tuple-element.33), channel_id=1, source_target_pairs={{0,8},{8,16},{16,24},{1,9},{9,17},{17,25},{2,10},{10,18},{18,26},{... | collective-permute-start | bytes 282632 | tf_op jit(solution)/shard_map/ppermute | solution.py:416
  11.6 11.3 %collective-permute-start.1 = (f32[8,2944]{1,0:T(8,128)S(1)}, f32[8,2944]{1,0:T(8,128)S(1)}, u32[]{:S(2)}, u32[]{:S(2)}) collective-permute-start(f32[8,2944]{1,0:T(8,128)S(1)} %get-tuple-element.33), channel_id=1, source_target_pairs={{0,16},{8,24},{1,17},{9,25},{2,18},{10,26},{3,19},{11,27},{4,20},{... | collective-permute-start | bytes 282632 | tf_op jit(solution)/shard_map/ppermute | solution.py:416
  15.1 7.9 %collective-permute-start.2 = (f32[8,2944]{1,0:T(8,128)S(1)}, f32[8,2944]{1,0:T(8,128)S(1)}, u32[]{:S(2)}, u32[]{:S(2)}) collective-permute-start(f32[8,2944]{1,0:T(8,128)S(1)} %get-tuple-element.33), channel_id=1, source_target_pairs={{0,24},{1,25},{2,26},{3,27},{4,28},{5,29},{6,30},{7,31}} | collective-permute-start | bytes 282632 | tf_op jit(solution)/shard_map/ppermute | solution.py:416
  19.1 12.4 %collective-permute-start.9 = (f32[8,1152]{1,0:T(8,128)S(1)}, f32[8,1152]{1,0:T(8,128)S(1)}, u32[]{:S(2)}, u32[]{:S(2)}) collective-permute-start(f32[8,1152]{1,0:T(8,128)S(1)} %get-tuple-element.48), channel_id=1, source_target_pairs={{0,8},{8,16},{16,24},{1,9},{9,17},{17,25},{2,10},{10,18},{18,26},{... | collective-permute-start | bytes 110600 | tf_op jit(solution)/shard_map/ppermute | solution.py:416
  20.4 11.1 %collective-permute-start.10 = (f32[8,1152]{1,0:T(8,128)S(1)}, f32[8,1152]{1,0:T(8,128)S(1)}, u32[]{:S(2)}, u32[]{:S(2)}) collective-permute-start(f32[8,1152]{1,0:T(8,128)S(1)} %get-tuple-element.48), channel_id=1, source_target_pairs={{0,16},{8,24},{1,17},{9,25},{2,18},{10,26},{3,19},{11,27},{4,20},{... | collective-permute-start | bytes 110600 | tf_op jit(solution)/shard_map/ppermute | solution.py:416
  21.7 9.8 %collective-permute-start.11 = (f32[8,1152]{1,0:T(8,128)S(1)}, f32[8,1152]{1,0:T(8,128)S(1)}, u32[]{:S(2)}, u32[]{:S(2)}) collective-permute-start(f32[8,1152]{1,0:T(8,128)S(1)} %get-tuple-element.48), channel_id=1, source_target_pairs={{0,24},{1,25},{2,26},{3,27},{4,28},{5,29},{6,30},{7,31}} | collective-permute-start | bytes 110600 | tf_op jit(solution)/shard_map/ppermute | solution.py:416
  31.4 17.8 %collective-permute-start.3 = (f32[4,3,12,8,128]{4,3,2,1,0:T(8,128)S(1)}, f32[4,3,12,8,128]{4,3,2,1,0:T(8,128)S(1)}, u32[]{:S(2)}, u32[]{:S(2)}) collective-permute-start(f32[4,3,12,8,128]{4,3,2,1,0:T(8,128)S(1)} %get-tuple-element.35), channel_id=1, source_target_pairs={{0,1},{1,0},{2,3},{3,2},{4,5},{5,4},{6,7},{7,6},{8,9},{9,8},{10,11... | collective-permute-start | bytes 1769480 | tf_op jit(solution)/shard_map/ppermute | solution.py:410
  39.8 7.3 %collective-permute-start.12 = (f32[4,3,12,8,128]{4,3,2,1,0:T(8,128)S(1)}, f32[4,3,12,8,128]{4,3,2,1,0:T(8,128)S(1)}, u32[]{:S(2)}, u32[]{:S(2)}) collective-permute-start(f32[4,3,12,8,128]{4,3,2,1,0:T(8,128)S(1)} %get-tuple-element.50), channel_id=1, source_target_pairs={{0,1},{1,0},{2,3},{3,2},{4,5},{5,4},{6,7},{7,6},{8,9},{9,8},{10,11... | collective-permute-start | bytes 1769480 | tf_op jit(solution)/shard_map/ppermute | solution.py:410
  40.4 6.7 %collective-permute-start.4 = (f32[4,32,8,128]{3,2,1,0:T(8,128)S(1)}, f32[4,32,8,128]{3,2,1,0:T(8,128)S(1)}, u32[]{:S(2)}, u32[]{:S(2)}) collective-permute-start(f32[4,32,8,128]{3,2,1,0:T(8,128)S(1)} %pad_maximum_fusion), channel_id=1, source_target_pairs={{0,1},{1,0},{2,3},{3,2},{4,5},{5,4},{6,7},{7,6},{8,9},{9,8},{10,11... | collective-permute-start | bytes 1572872 | tf_op jit(solution)/shard_map/ppermute | solution.py:410
  46.5 5.2 %collective-permute-start.15 = (f32[4,3,8,8,128]{4,3,2,1,0:T(8,128)S(1)}, f32[4,3,8,8,128]{4,3,2,1,0:T(8,128)S(1)}, u32[]{:S(2)}, u32[]{:S(2)}) collective-permute-start(f32[4,3,8,8,128]{4,3,2,1,0:T(8,128)S(1)} %get-tuple-element.56), channel_id=1, source_target_pairs={{0,1},{1,0},{2,3},{3,2},{4,5},{5,4},{6,7},{7,6},{8,9},{9,8},{10,11... | collective-permute-start | bytes 1179656 | tf_op jit(solution)/shard_map/ppermute | solution.py:410
  47.6 21.9 %collective-permute-start.13 = (f32[2,3,12,8,128]{4,3,2,1,0:T(8,128)S(1)}, f32[2,3,12,8,128]{4,3,2,1,0:T(8,128)S(1)}, u32[]{:S(2)}, u32[]{:S(2)}) collective-permute-start(f32[2,3,12,8,128]{4,3,2,1,0:T(8,128)S(1)} %get-tuple-element.52), channel_id=1, source_target_pairs={{0,2},{1,3},{2,0},{3,1},{4,6},{5,7},{6,4},{7,5},{8,10},{9,11},{10,... | collective-permute-start | bytes 884744 | tf_op jit(solution)/shard_map/ppermute | solution.py:410
  49.6 22.8 %collective-permute-start.5 = (f32[2,3,12,8,128]{4,3,2,1,0:T(8,128)S(1)}, f32[2,3,12,8,128]{4,3,2,1,0:T(8,128)S(1)}, u32[]{:S(2)}, u32[]{:S(2)}) collective-permute-start(f32[2,3,12,8,128]{4,3,2,1,0:T(8,128)S(1)} %get-tuple-element.41), channel_id=1, source_target_pairs={{0,2},{1,3},{2,0},{3,1},{4,6},{5,7},{6,4},{7,5},{8,10},{9,11},{10,... | collective-permute-start | bytes 884744 | tf_op jit(solution)/shard_map/ppermute | solution.py:410
  50.1 19.3 %collective-permute-start.6 = (f32[2,32,8,128]{3,2,1,0:T(8,128)S(1)}, f32[2,32,8,128]{3,2,1,0:T(8,128)S(1)}, u32[]{:S(2)}, u32[]{:S(2)}) collective-permute-start(f32[2,32,8,128]{3,2,1,0:T(8,128)S(1)} %get-tuple-element.43), channel_id=1, source_target_pairs={{0,2},{1,3},{2,0},{3,1},{4,6},{5,7},{6,4},{7,5},{8,10},{9,11},{10,... | collective-permute-start | bytes 786440 | tf_op jit(solution)/shard_map/ppermute | solution.py:410
  51.9 23.9 %collective-permute-start.16 = (f32[2,3,8,8,128]{4,3,2,1,0:T(8,128)S(1)}, f32[2,3,8,8,128]{4,3,2,1,0:T(8,128)S(1)}, u32[]{:S(2)}, u32[]{:S(2)}) collective-permute-start(f32[2,3,8,8,128]{4,3,2,1,0:T(8,128)S(1)} %get-tuple-element.58), channel_id=1, source_target_pairs={{0,2},{1,3},{2,0},{3,1},{4,6},{5,7},{6,4},{7,5},{8,10},{9,11},{10,... | collective-permute-start | bytes 589832 | tf_op jit(solution)/shard_map/ppermute | solution.py:410
  69.7 25.9 %collective-permute-start.14 = (f32[1,3,12,8,128]{4,3,2,1,0:T(8,128)S(1)}, f32[1,3,12,8,128]{4,3,2,1,0:T(8,128)S(1)}, u32[]{:S(2)}, u32[]{:S(2)}) collective-permute-start(f32[1,3,12,8,128]{4,3,2,1,0:T(8,128)S(1)} %get-tuple-element.54), channel_id=1, source_target_pairs={{0,4},{1,5},{2,6},{3,7},{4,0},{5,1},{6,2},{7,3},{8,12},{9,13},{10,... | collective-permute-start | bytes 442376 | tf_op jit(solution)/shard_map/ppermute | solution.py:410
  72.7 24.3 %collective-permute-start.7 = (f32[1,3,12,8,128]{4,3,2,1,0:T(8,128)S(1)}, f32[1,3,12,8,128]{4,3,2,1,0:T(8,128)S(1)}, u32[]{:S(2)}, u32[]{:S(2)}) collective-permute-start(f32[1,3,12,8,128]{4,3,2,1,0:T(8,128)S(1)} %get-tuple-element.45), channel_id=1, source_target_pairs={{0,4},{1,5},{2,6},{3,7},{4,0},{5,1},{6,2},{7,3},{8,12},{9,13},{10,... | collective-permute-start | bytes 442376 | tf_op jit(solution)/shard_map/ppermute | solution.py:410
  73.1 21.8 %collective-permute-start.8 = (f32[1,32,8,128]{3,2,1,0:T(8,128)S(1)}, f32[1,32,8,128]{3,2,1,0:T(8,128)S(1)}, u32[]{:S(2)}, u32[]{:S(2)}) collective-permute-start(f32[1,32,8,128]{3,2,1,0:T(8,128)S(1)} %get-tuple-element.47), channel_id=1, source_target_pairs={{0,4},{1,5},{2,6},{3,7},{4,0},{5,1},{6,2},{7,3},{8,12},{9,13},{10,... | collective-permute-start | bytes 393224 | tf_op jit(solution)/shard_map/ppermute | solution.py:410
  75.8 19.1 %collective-permute-start.17 = (f32[1,3,8,8,128]{4,3,2,1,0:T(8,128)S(1)}, f32[1,3,8,8,128]{4,3,2,1,0:T(8,128)S(1)}, u32[]{:S(2)}, u32[]{:S(2)}) collective-permute-start(f32[1,3,8,8,128]{4,3,2,1,0:T(8,128)S(1)} %get-tuple-element.60), channel_id=1, source_target_pairs={{0,4},{1,5},{2,6},{3,7},{4,0},{5,1},{6,2},{7,3},{8,12},{9,13},{10,... | collective-permute-start | bytes 294920 | tf_op jit(solution)/shard_map/ppermute | solution.py:410
where the time goes:
time: 98.6 us; the launch traced here: 98.3 us
  Pallas kernels  35.7 us (36%)
  waiting for transfers between devices  35.6 us (36%)
  starting transfers between devices  25.3 us (26%)
    ppermute x12, waiting for transfers between devices, swap(): lax.ppermute(block, 'view', [(at, at ^ 1 << bit) for at in range(count)])  35.6 us
    pallas_call x3, Pallas kernels, shade(): pl.pallas_call(functools.partial(shade_kernel, sigma_scale, ratio, low, t...  22.7 us
    ppermute x6, starting transfers between devices, from_earlier(): lax.ppermute(leaving, 'light', [(at, at + apart) for at in range(count -...  13.4 us
    ppermute x12, starting transfers between devices, swap(): lax.ppermute(block, 'view', [(at, at ^ 1 << bit) for at in range(count)])  11.8 us
    pallas_call x2, Pallas kernels, sums(): pl.pallas_call(functools.partial(sums_kernel, sigma_scale, ratio, low, bi...  8.09 us
    pallas_call x3, Pallas kernels, last(): pl.pallas_call(functools.partial(last_kernel, bit), grid=(tiles // unit,)...  3.37 us
  transfers between devices with their start and end apart: 18, of which 2 were waited for; matrix products, arithmetic and copies ran while one was open for 0% of the time, Pallas kernels for 29%

commit v1 on v0

--- a/solution.py
+++ b/solution.py
@@ -11,12 +11,13 @@
 LANE = 128
 SUB = 8
 DRIFTS = (-1, 0, 1)
-VMEM_LIMIT = 48 * 2**20
+VMEM_LIMIT = 24 * 2**20
+STREAM_LIMIT = 52 * 2**20
 F32 = jnp.float32
 
 
-def params():
-    return pltpu.CompilerParams(vmem_limit_bytes=VMEM_LIMIT)
+def params(limit=VMEM_LIMIT):
+    return pltpu.CompilerParams(vmem_limit_bytes=limit)
 
 
 def bit_reversed(value, bits):
@@ -53,11 +54,15 @@
     return knot & (SUB - 1), knot >= SUB
 
 
-def value_at(coef, q, place, cells):
+def value_at(table, place, cells):
     low, high = place
-    start = jnp.where(high, rows_of(coef[4 * q + 1], low), rows_of(coef[4 * q], low))
-    step = jnp.where(high, rows_of(coef[4 * q + 3], low), rows_of(coef[4 * q + 2], low))
+    start = jnp.where(high, rows_of(table[1], low), rows_of(table[0], low))
+    step = jnp.where(high, rows_of(table[3], low), rows_of(table[2], low))
     return start + step * cells
+
+
+def table_of(coef, q):
+    return [coef[4 * q + at] for at in range(4)]
 
 
 def fetch_tile(density_ref, buffer, sems, first, tile):
@@ -84,12 +89,13 @@
     @pl.loop(0, tiles)
     def _(tile):
         fetch_tile(density_ref, buffer, sems, first, tile).wait()
+        table = table_of(coef, 0)
         down = [jnp.zeros((SUB, LANE), F32) for _ in range(layers)]
         for block in range(slices // SUB):
             through = jnp.zeros((SUB, LANE), F32)
             for b in range(layers):
                 cells = buffer[tile, b, block * SUB : block * SUB + SUB]
-                sigma = value_at(coef, 0, place_of(cells, knots), cells)
+                sigma = value_at(table, place_of(cells, knots), cells)
                 through = through + sigma
                 down[b] = down[b] + sigma
             if split:
@@ -146,12 +152,52 @@
         lighting[k] = shade[:, LANE : LANE + width]
 
 
+def weights_of(coef, buffer, tile, b, ahead, ratio, knots):
+    steps = len(ahead)
+    sublane = lax.broadcasted_iota(jnp.int32, (SUB, LANE), 0)
+    table = table_of(coef, 0)
+    cells, places, sigma = [], [], []
+    before, running = [], None
+    for j in range(steps):
+        cells.append(buffer[tile, b, pl.ds(j, SUB, stride=steps), :])
+        places.append(place_of(cells[j], knots))
+        sigma.append(value_at(table, places[j], cells[j]))
+        before.append(running)
+        running = sigma[j] if running is None else running + sigma[j]
+    earlier = running
+    for hop in (1, 2, 4):
+        earlier = earlier + jnp.where(sublane >= hop, pltpu.roll(earlier, hop, 0), 0.0)
+    earlier = earlier - running
+    weights = []
+    for j in range(steps):
+        inside = earlier if j == 0 else earlier + before[j]
+        shadow = jnp.exp2(inside * ratio)
+        passed = jnp.exp2(sigma[j])
+        if ahead[j] is None:
+            after = passed
+            weights.append((1.0 - passed) * shadow)
+        else:
+            after = ahead[j] * passed
+            weights.append((ahead[j] - after) * shadow)
+        ahead[j] = after
+    return cells, places, weights
+
+
+def put_halves(send_ref, keep_ref, sums, tile, bits):
+    mine = lax.axis_index("view") & 1
+    for q in range(1 << bits - 1):
+        octet = 2 * bit_reversed(q, bits - 1)
+        for k in range(send_ref.shape[1]):
+            send_ref[q, k, tile] = sums[k, pl.ds(octet + 1 - mine, SUB, stride=SUB), :]
+            keep_ref[q, k, tile] = sums[k, pl.ds(octet + mine, SUB, stride=SUB), :]
+
+
 def shade_kernel(
-    sigma_scale, ratio, first, total, bits, pieces, far, whole_out,
+    sigma_scale, ratio, first, total, bits, pieces, far, late, whole_out,
     index_ref, code_ref, tint_ref, tables_ref, density_ref, *rest,
 ):
     brick_refs = [rest[at * len(pieces) : (at + 1) * len(pieces)] for at in range(far)]
-    rest = rest[far * len(pieces) :]
+    rest = rest[far * len(pieces) + late :]
     if whole_out:
         out_ref, coef, buffer, lighting, sums, sems = rest
     else:
@@ -167,8 +213,6 @@
 
     fill_coefficients(index_ref[0, 0], tables_ref, coef, sigma_scale, tables_ref.shape[1])
     fill_lighting(pieces, brick_refs, code_ref, tint_ref, lighting, first, total)
-    mine = lax.axis_index("view") & 1
-    sublane = lax.broadcasted_iota(jnp.int32, (SUB, LANE), 0)
 
     @pl.loop(0, tiles)
     def _(tile):
@@ -176,37 +220,13 @@
         columns = pl.ds(pl.multiple_of(tile * LANE, LANE), LANE)
         ahead = [None] * steps
         for b in range(layers):
-            lit = [
-                jnp.broadcast_to(lighting[k, b : b + 1, columns], (SUB, LANE))
-                for k in range(channels)
-            ]
-            cells, places, sigma = [], [], []
-            for j in range(steps):
-                cells.append(buffer[tile, b, pl.ds(j, SUB, stride=steps), :])
-                places.append(place_of(cells[j], knots))
-                sigma.append(value_at(coef, 0, places[j], cells[j]))
-            before, running = [], None
-            for j in range(steps):
-                before.append(running)
-                running = sigma[j] if running is None else running + sigma[j]
-            earlier = running
-            for hop in (1, 2, 4):
-                earlier = earlier + jnp.where(sublane >= hop, pltpu.roll(earlier, hop, 0), 0.0)
-            earlier = earlier - running
-            for j in range(steps):
-                inside = earlier if j == 0 else earlier + before[j]
-                shadow = jnp.exp2(inside * ratio)
-                passed = jnp.exp2(sigma[j])
-                if b == 0:
-                    after = passed
-                    weight = (1.0 - passed) * shadow
-                else:
-                    after = ahead[j] * passed
-                    weight = (ahead[j] - after) * shadow
-                ahead[j] = after
-                rows = pl.ds(j * SUB, SUB)
-                for k in range(channels):
-                    term = value_at(coef, k + 1, places[j], cells[j]) * (weight * lit[k])
+            cells, places, weights = weights_of(coef, buffer, tile, b, ahead, ratio, knots)
+            for k in range(channels):
+                lit = jnp.broadcast_to(lighting[k, b : b + 1, columns], (SUB, LANE))
+                table = [entry * lit for entry in table_of(coef, k + 1)]
+                for j in range(steps):
+                    rows = pl.ds(j * SUB, SUB)
+                    term = value_at(table, places[j], cells[j]) * weights[j]
                     if b == 0:
                         sums[k, rows] = term
                     else:
@@ -221,16 +241,59 @@
                             k, pl.ds(part * SUB * SUB + octet, SUB, stride=SUB), :
                         ]
         else:
-            for q in range(1 << bits - 1):
-                octet = 2 * bit_reversed(q, bits - 1)
-                for k in range(channels):
-                    send_ref[q, k, tile] = sums[k, pl.ds(octet + 1 - mine, SUB, stride=SUB), :]
-                    keep_ref[q, k, tile] = sums[k, pl.ds(octet + mine, SUB, stride=SUB), :]
+            put_halves(send_ref, keep_ref, sums, tile, bits)
+
+
+def unlit_kernel(sigma_scale, ratio, first, late, index_ref, tables_ref, density_ref, *rest):
+    out_ref, coef, buffer, sems = rest[late:]
+    tiles, layers, slices, _ = buffer.shape
+    knots = tables_ref.shape[2]
+    steps = slices // SUB
+
+    @pl.loop(0, tiles)
+    def _(tile):
+        fetch_tile(density_ref, buffer, sems, first, tile).start()
+
+    fill_coefficients(index_ref[0, 0], tables_ref, coef, sigma_scale, tables_ref.shape[1])
+
+    @pl.loop(0, tiles)
+    def _(tile):
+        fetch_tile(density_ref, buffer, sems, first, tile).wait()
+        ahead = [None] * steps
+        for b in range(layers):
+            cells, places, weights = weights_of(coef, buffer, tile, b, ahead, ratio, knots)
+            for k in range(out_ref.shape[2]):
+                table = table_of(coef, k + 1)
+                for j in range(steps):
+                    term = value_at(table, places[j], cells[j]) * weights[j]
+                    out_ref[tile, b, k, j * SUB : j * SUB + SUB] = term
+
+
+def lit_kernel(first, total, bits, pieces, far, late, code_ref, tint_ref, unlit_ref, *rest):
+    brick_refs = [rest[at * len(pieces) : (at + 1) * len(pieces)] for at in range(far)]
+    send_ref, keep_ref, lighting, sums = rest[far * len(pieces) + late :]
+    tiles, layers, channels, slices, _ = unlit_ref.shape
+    fill_lighting(pieces, brick_refs, code_ref, tint_ref, lighting, first, total)
+
+    @pl.loop(0, tiles)
+    def _(tile):
+        columns = pl.ds(pl.multiple_of(tile * LANE, LANE), LANE)
+        for k in range(channels):
+            lit = [
+                jnp.broadcast_to(lighting[k, b : b + 1, columns], (SUB, LANE))
+                for b in range(layers)
+            ]
+            for j in range(slices // SUB):
+                rows = slice(j * SUB, j * SUB + SUB)
+                terms = [unlit_ref[tile, b, k, rows] * lit[b] for b in range(layers)]
+                sums[k, rows] = functools.reduce(jnp.add, terms)
+        put_halves(send_ref, keep_ref, sums, tile, bits)
 
 
 VMEM = functools.partial(pl.BlockSpec, memory_space=pltpu.VMEM)
 SMEM = functools.partial(pl.BlockSpec, memory_space=pltpu.SMEM)
 ANY = functools.partial(pl.BlockSpec, memory_space=pl.ANY)
+HBM = functools.partial(pl.BlockSpec, memory_space=pltpu.HBM)
 
 
 def shape(*dims):
@@ -240,6 +303,9 @@
 def cost(density, columns, per_cell):
     cells = density.shape[0] * density.shape[1] * columns
     return pl.CostEstimate(flops=cells * per_cell, bytes_accessed=4 * cells, transcendentals=0)
+
+
+MERGE_COST = pl.CostEstimate(flops=2 * 10**10, bytes_accessed=2**20, transcendentals=0)
 
 
 def sums(density, tables, index, low, high, sigma_scale, ratio, bits, split):
@@ -254,17 +320,20 @@
     scratch.append(pltpu.SemaphoreType.DMA((tiles,)))
     return pl.pallas_call(
         functools.partial(sums_kernel, sigma_scale, ratio, low, bits, split),
-        in_specs=[SMEM(), VMEM(), ANY()],
+        in_specs=[SMEM(), VMEM(), HBM()],
         out_specs=[VMEM()] * len(outs),
         out_shape=outs,
         scratch_shapes=scratch,
-        compiler_params=params(),
-        cost_estimate=cost(density, high - low, 16),
+        compiler_params=params(STREAM_LIMIT),
+        cost_estimate=cost(density, high - low, 4000),
         name="sums",
     )(index, tables, density)
 
 
-def shade(density, tables, index, code, tint, bricks, pieces, low, high, sigma_scale, ratio, bits, whole_out):
+def shade(
+    density, tables, index, code, tint, bricks, pieces, low, high, sigma_scale, ratio, bits,
+    whole_out, after=(),
+):
     layers, slices, total = density.shape
     channels = tint.shape[1]
     tiles = (high - low) // LANE
@@ -273,14 +342,13 @@
         outs = [shape(channels + 1, tiles, slices, LANE)]
     else:
         outs = [shape(half, channels, tiles, SUB, LANE)] * 2
-    used = [at for at, (start, stop) in enumerate(pieces) if start < high + LANE and stop > low - LANE]
-    operands = [rows[at] for rows in bricks for at in used]
+    operands = [row for rows in bricks for row in rows]
     return pl.pallas_call(
         functools.partial(
-            shade_kernel, sigma_scale, ratio, low, total, bits,
-            tuple(pieces[at] for at in used), len(bricks), whole_out,
+            shade_kernel, sigma_scale, ratio, low, total, bits, pieces, len(bricks), len(after),
+            whole_out,
         ),
-        in_specs=[SMEM()] * 3 + [VMEM(), ANY()] + [VMEM()] * len(operands),
+        in_specs=[SMEM()] * 3 + [VMEM(), HBM()] + [VMEM()] * len(operands) + [ANY()] * len(after),
         out_specs=[VMEM()] * len(outs),
         out_shape=outs,
         scratch_shapes=[
@@ -291,12 +359,52 @@
             pltpu.SemaphoreType.DMA((tiles,)),
         ],
         compiler_params=params(),
-        cost_estimate=cost(density, high - low, 60),
+        cost_estimate=cost(density, high - low, 10000),
         name="shade",
-    )(index, code, tint, tables, density, *operands)
-
-
-def merge_clear_kernel(bit, own_ref, other_ref, send_ref, keep_ref):
+    )(index, code, tint, tables, density, *operands, *after)
+
+
+def unlit(density, tables, index, low, high, sigma_scale, ratio, after=()):
+    layers, slices, _ = density.shape
+    tiles = (high - low) // LANE
+    return pl.pallas_call(
+        functools.partial(unlit_kernel, sigma_scale, ratio, low, len(after)),
+        in_specs=[SMEM(), VMEM(), HBM()] + [ANY()] * len(after),
+        out_specs=VMEM(),
+        out_shape=shape(tiles, layers, tables.shape[1] - 1, slices, LANE),
+        scratch_shapes=[
+            pltpu.VMEM((4 * tables.shape[1], SUB, LANE), F32),
+            pltpu.VMEM((tiles, layers, slices, LANE), F32),
+            pltpu.SemaphoreType.DMA((tiles,)),
+        ],
+        compiler_params=params(),
+        cost_estimate=cost(density, high - low, 10000),
+        name="unlit",
+    )(index, tables, density, *after)
+
+
+def lit(cells, code, tint, bricks, pieces, low, high, total, bits, after=()):
+    tiles, layers, channels, slices, _ = cells.shape
+    half = (1 << bits) // 2
+    operands = [row for rows in bricks for row in rows]
+    return pl.pallas_call(
+        functools.partial(
+            lit_kernel, low, total, bits, pieces, len(bricks), len(after)
+        ),
+        in_specs=[SMEM()] * 2 + [VMEM()] * (1 + len(operands)) + [ANY()] * len(after),
+        out_specs=[VMEM()] * 2,
+        out_shape=[shape(half, channels, tiles, SUB, LANE)] * 2,
+        scratch_shapes=[
+            pltpu.VMEM((channels, layers, high - low), F32),
+            pltpu.VMEM((channels, slices, LANE), F32),
+        ],
+        compiler_params=params(),
+        name="lit",
+    )(code, tint, cells, *operands, *after)
+
+
+def merge_clear_kernel(bit, own_ref, other_ref, *rest):
+    send_ref, keep_ref = rest[-2:]
     half = send_ref.shape[0]
     mine = lax.axis_index("view") >> bit + 1 & 1
     for at in range(half):
@@ -305,19 +413,22 @@
         keep_ref[at] = own_ref[here] * other_ref[here]
 
 
-def merge_clear(own, other, bit):
+def merge_clear(own, other, bit, after=()):
     half = shape(own.shape[0] // 2, *own.shape[1:])
     return pl.pallas_call(
         functools.partial(merge_clear_kernel, bit),
-        in_specs=[VMEM()] * 2,
+        in_specs=[VMEM()] * 2 + [ANY()] * len(after),
         out_specs=[VMEM()] * 2,
         out_shape=[half] * 2,
         compiler_params=params(),
+        cost_estimate=MERGE_COST,
         name="merge_clear",
-    )(own, other)
-
-
-def merge_kernel(bit, own_ref, other_ref, own_clear_ref, other_clear_ref, send_ref, keep_ref):
+    )(own, other, *after)
+
+
+def merge_kernel(bit, start, own_ref, other_ref, own_clear_ref, other_clear_ref, *rest):
+    send_ref, keep_ref = rest[-2:]
+    tiles = pl.ds(start, own_ref.shape[2])
     half = send_ref.shape[0]
     me = lax.axis_index("view")
     mine = me >> bit + 1 & 1
@@ -326,7 +437,7 @@
         for at in range(half):
             for to_ref, side in ((send_ref, 1 - mine), (keep_ref, mine)):
                 source = side * half + at
-                clear = clear_ref[source]
+                clear = clear_ref[source, tiles]
                 for k in range(send_ref.shape[1]):
                     to_ref[at, k] = front_ref[source, k] + clear * back_ref[source, k]
 
@@ -341,68 +452,56 @@
         merged(own_ref, other_ref, own_clear_ref)
 
 
-def unit_of(low, high):
-    return math.gcd(low // LANE, (high - low) // LANE)
-
-
-def merge(own, other, own_clear, other_clear, bit, low, high):
-    count, channels, tiles = own.shape[:3]
-    unit = unit_of(low, high)
-    start = low // LANE // unit
-    half = count // 2
-    data = lambda n: pl.BlockSpec((n, channels, unit, SUB, LANE), lambda i: (0, 0, i, 0, 0))
-    clear = pl.BlockSpec((count, unit, SUB, LANE), lambda i: (0, start + i, 0, 0))
+def merge(own, other, own_clear, other_clear, bit, low, after=()):
+    half = shape(own.shape[0] // 2, *own.shape[1:])
     return pl.pallas_call(
-        functools.partial(merge_kernel, bit),
-        grid=(tiles // unit,),
-        in_specs=[data(count)] * 2 + [clear] * 2,
-        out_specs=[data(half)] * 2,
-        out_shape=[shape(half, *own.shape[1:])] * 2,
+        functools.partial(merge_kernel, bit, low // LANE),
+        in_specs=[VMEM()] * 4 + [ANY()] * len(after),
+        out_specs=[VMEM()] * 2,
+        out_shape=[half] * 2,
         compiler_params=params(),
+        cost_estimate=MERGE_COST,
         name="merge",
-    )(own, other, own_clear, other_clear)
-
-
-def last_kernel(bit, own_ref, other_ref, own_clear_ref, other_clear_ref, *rest):
-    image_ref = rest[-1]
-    channels, tiles = own_ref.shape[1:3]
-
-    def merged(front_ref, back_ref, clear_ref):
-        for tile in range(tiles):
-            columns = slice(tile * LANE, tile * LANE + LANE)
-            clear = clear_ref[0, tile]
-            for k in range(channels):
-                image_ref[k, :, columns] = front_ref[0, k, tile] + clear * back_ref[0, k, tile]
-            image_ref[channels, :, columns] = own_clear_ref[0, tile] * other_clear_ref[0, tile]
-
+    )(own, other, own_clear, other_clear, *after)
+
+
+def last_kernel(bit, firsts, *refs):
+    chunks = len(firsts)
+    own_clear_ref, other_clear_ref = refs[2 * chunks : 2 * chunks + 2]
+    image_ref = refs[-1]
     upper = lax.axis_index("view") >> bit & 1 == 1
+
+    def merged(fronts, backs, clear_ref):
+        for first, front_ref, back_ref in zip(firsts, fronts, backs):
+            channels, tiles = front_ref.shape[1:3]
+            for tile in range(tiles):
+                columns = slice(first + tile * LANE, first + tile * LANE + LANE)
+                clear = clear_ref[0, first // LANE + tile]
+                for k in range(channels):
+                    image_ref[k, :, columns] = front_ref[0, k, tile] + clear * back_ref[0, k, tile]
+
+    for tile in range(own_clear_ref.shape[1]):
+        columns = slice(tile * LANE, tile * LANE + LANE)
+        image_ref[image_ref.shape[0] - 1, :, columns] = own_clear_ref[0, tile] * other_clear_ref[0, tile]
 
     @pl.when(upper)
     def _():
-        merged(other_ref, own_ref, other_clear_ref)
+        merged(refs[chunks : 2 * chunks], refs[:chunks], other_clear_ref)
 
     @pl.when(jnp.logical_not(upper))
     def _():
-        merged(own_ref, other_ref, own_clear_ref)
-
-
-def last(own, other, own_clear, other_clear, bit, low, high, total, image):
-    _, channels, tiles = own.shape[:3]
-    unit = unit_of(low, high)
-    start = low // LANE // unit
-    data = pl.BlockSpec((1, channels, unit, SUB, LANE), lambda i: (0, 0, i, 0, 0))
-    clear = pl.BlockSpec((1, unit, SUB, LANE), lambda i: (0, start + i, 0, 0))
-    before = [] if image is None else [image]
+        merged(refs[:chunks], refs[chunks : 2 * chunks], own_clear_ref)
+
+
+def last(owns, others, own_clear, other_clear, bit, firsts, total):
     return pl.pallas_call(
-        functools.partial(last_kernel, bit),
-        grid=(tiles // unit,),
-        in_specs=[data] * 2 + [clear] * 2 + [ANY()] * len(before),
-        out_specs=pl.BlockSpec((channels + 1, SUB, unit * LANE), lambda i: (0, 0, start + i)),
-        out_shape=shape(channels + 1, SUB, total),
-        input_output_aliases={4: 0} if before else {},
+        functools.partial(last_kernel, bit, firsts),
+        in_specs=[VMEM()] * (2 * len(owns) + 2),
+        out_specs=VMEM(),
+        out_shape=shape(owns[0].shape[1] + 1, SUB, total),
         compiler_params=params(),
         name="last",
-    )(own, other, own_clear, other_clear, *before)
+    )(*owns, *others, own_clear, other_clear)
 
 
 def swap(block, bit):
@@ -444,7 +543,6 @@
     return current.reshape(depth, rows, total)
 
 
-LIGHT_CUTS = (0.28125,)
 CUTS = (0.25, 0.625)
 
 
@@ -459,37 +557,49 @@
     bits = views.bit_length() - 1
     sigma_scale = -math.log2(math.e) / (layers * views)
     ratio = layers * views / (slices * lax.axis_size("light"))
-    if views * SUB != slices:
+    if views * SUB != slices or bits != 3:
         return plain(
             density, tables, table_index, light_code, light_tint, sigma_scale, ratio, bits
         )
-    pieces = ranges(LIGHT_CUTS, total)
-    bricks = [[] for _ in range(lax.axis_size("light") - 1)]
-    clears = []
-    for low, high in pieces:
-        leaving, *halves = sums(
-            density, tables, table_index, low, high, sigma_scale, ratio, bits, True
-        )
-        clears.append(halves)
-        for rows, row in zip(bricks, from_earlier(leaving)):
-            rows.append(row)
-    send, keep = (jnp.concatenate(parts, axis=1) for parts in zip(*clears))
-    clear = []
-    for bit in range(bits):
-        clear.append((keep, swap(send, bit)))
-        if bit < bits - 1:
-            send, keep = merge_clear(*clear[bit], bit)
-    image = None
-    for low, high in ranges(CUTS, total):
-        send, keep = shade(
-            density, tables, table_index, light_code, light_tint, bricks, pieces, low, high,
-            sigma_scale, ratio, bits, False,
-        )
-        for bit in range(bits - 1):
-            send, keep = merge(keep, swap(send, bit), *clear[bit], bit, low, high)
-        bit = bits - 1
-        image = last(keep, swap(send, bit), *clear[bit], bit, low, high, total, image)
-    return image
+    pieces = [(0, total)]
+    chunks = ranges(CUTS, total)
+    leaving, send, keep = sums(
+        density, tables, table_index, 0, total, sigma_scale, ratio, bits, True
+    )
+    bricks = [[row] for row in from_earlier(leaving)]
+    clear = [(keep, swap(send, 0))]
+    send, keep = merge_clear(*clear[0], 0)
+    clear.append((keep, swap(send, 1)))
+    first = unlit(
+        density, tables, table_index, *chunks[0], sigma_scale, ratio, after=(send,)
+    )
+    state = [None] * len(chunks)
+    state[0] = lit(first, light_code, light_tint, bricks, pieces, *chunks[0], total, bits)
+    send, keep = merge_clear(*clear[1], 1, after=(state[0][0],))
+    clear.append((keep, swap(send, 2)))
+    done = send
+    for at, (low, high) in enumerate(chunks):
+        if at:
+            state[at] = shade(
+                density, tables, table_index, light_code, light_tint, bricks, pieces, low, high,
+                sigma_scale, ratio, bits, False, after=(done,),
+            )
+            done = state[at][0]
+        send, keep = state[at]
+        arrived = swap(send, 0)
+        if at:
+            before = chunks[at - 1][0]
+            settled = state[at - 2][1] if at > 1 else clear[2][1]
+            late = merge(*state[at - 1], *clear[1], 1, before, after=(done, settled))
+            state[at - 1] = (late[1], swap(late[0], 2))
+            done = late[0]
+        send, keep = merge(keep, arrived, *clear[0], 0, low, after=(done,))
+        done = send
+        state[at] = (keep, swap(send, 1))
+    late = merge(*state[-1], *clear[1], 1, chunks[-1][0], after=(state[-2][1],))
+    state[-1] = (late[1], swap(late[0], 2))
+    owns, others = zip(*state)
+    return last(owns, others, *clear[2], 2, [low for low, _ in chunks], total)
 
 
 def solution(mesh):

time: 98.6 us -> 75.9 us (0.77)
  waiting for transfers between devices: 35.6 us -> 19.1 us
  Pallas kernels: 35.7 us -> 31.3 us
  starting transfers between devices: 25.3 us -> 23.1 us
    ppermute x12, waiting for transfers between devices: 35.6 us -> 19.1 us  [swap(): lax.ppermute(block, 'view', [(at, at ^ 1 << bit) for at in range(count)])]
    pallas_call x3 -> x2, Pallas kernels: 22.7 us -> 16.6 us  [shade(): pl.pallas_call(functools.partial(shade_kernel, sigma_scale, ratio, low, t...]
    ppermute x6 -> x3, starting transfers between devices: 13.4 us -> 9.15 us  [from_earlier(): lax.ppermute(leaving, 'light', [(at, at + apart) for at in range(count -...]
    pallas_call x9, Pallas kernels: 4.78 us -> 7.32 us  [the longest x1 4.39 us: unlit(): pl.pallas_call(functools.partial(unlit_kernel, sigma_scale, ratio, low, l...]
    ppermute x12, starting transfers between devices: 11.8 us -> 14 us  [swap(): lax.ppermute(block, 'view', [(at, at ^ 1 << bit) for at in range(count)])]
    pallas_call x2 -> x1, Pallas kernels: 8.09 us -> 7.28 us  [sums(): pl.pallas_call(functools.partial(sums_kernel, sigma_scale, ratio, low, bi...]
  transfers between devices with their start and end apart: 18 -> 15, of which waited for: 2 -> 6; matrix products, arithmetic and copies ran while one was open for 0% -> 0% of each run, Pallas kernels for 29% -> 30%
where the time goes in v1:
time: 75.9 us; the launch traced here: 75.6 us
  Pallas kernels  31.3 us (41%)
  starting transfers between devices  23.1 us (30%)
  waiting for transfers between devices  19.1 us (25%)
  local copies, waits for them, and re-layouts  1.16 us (2%)
  between operations  0.89 us (1%)
    ppermute x12, waiting for transfers between devices, swap(): lax.ppermute(block, 'view', [(at, at ^ 1 << bit) for at in range(count)])  19.1 us
    pallas_call x2, Pallas kernels, shade(): pl.pallas_call(functools.partial(shade_kernel, sigma_scale, ratio, low, t...  16.6 us
    ppermute x12, starting transfers between devices, swap(): lax.ppermute(block, 'view', [(at, at ^ 1 << bit) for at in range(count)])  14 us
    ppermute x3, starting transfers between devices, from_earlier(): lax.ppermute(leaving, 'light', [(at, at + apart) for at in range(count -...  9.15 us
    pallas_call x1, Pallas kernels, sums(): pl.pallas_call(functools.partial(sums_kernel, sigma_scale, ratio, low, bi...  7.28 us
    pallas_call x1, Pallas kernels, unlit(): pl.pallas_call(functools.partial(unlit_kernel, sigma_scale, ratio, low, l...  4.39 us
    pallas_call x1, Pallas kernels, lit(): pl.pallas_call(functools.partial(lit_kernel, low, total, bits, pieces, le...  1.69 us
  transfers between devices with their start and end apart: 15, of which 6 were waited for; matrix products, arithmetic and copies ran while one was open for 0% of the time, Pallas kernels for 30%

profile of v1, /device:TPU:0, one launch (start us, length us, event | category | flops | bytes accessed | tf_op | source)
XLA Modules:
  0.0 75.6 jit_solution(8459946246455725088)
XLA Ops:
  0.7 0.7 copy-done.2
  1.4 7.3 %sums.1 = (f32[8,4096]{1,0:T(8,128)S(1)}, f32[4,32,8,128]{3,2,1,0:T(8,128)S(1)}, f32[4,32,8,128]{3,2,1,0:T(8,128)S(1)}) custom-call(s32[1,1]{1,0:T(1,128)S(6)} %copy.6.index_ref, f32[8,4,16]{2,1,0:T(4,128)S(1)} %copy-done.2, f32[8,64,4096]{2,1,0:T(8,128)} %density_ref.7), custom_call_target="tpu_custom_call" | custom-call | flops 8388608000 | bytes 8388608 | tf_op jit(solution)/shard_map/sums/pallas_call | solution.py:321
  8.7 0.5 collective-permute-start
  9.2 5.4 %collective-permute-start.3 = (f32[8,4096]{1,0:T(8,128)S(1)}, f32[8,4096]{1,0:T(8,128)S(1)}, u32[]{:S(2)}, u32[]{:S(2)}) collective-permute-start(f32[8,4096]{1,0:T(8,128)S(1)} %get-tuple-element.33), channel_id=1, source_target_pairs={{0,24},{1,25},{2,26},{3,27},{4,28},{5,29},{6,30},{7,31}} | collective-permute-start | bytes 393224 | tf_op jit(solution)/shard_map/ppermute | solution.py:515
  14.6 1.3 %collective-permute-start.2 = (f32[8,4096]{1,0:T(8,128)S(1)}, f32[8,4096]{1,0:T(8,128)S(1)}, u32[]{:S(2)}, u32[]{:S(2)}) collective-permute-start(f32[8,4096]{1,0:T(8,128)S(1)} %get-tuple-element.33), channel_id=1, source_target_pairs={{0,16},{8,24},{1,17},{9,25},{2,18},{10,26},{3,19},{11,27},{4,20},{... | collective-permute-start | bytes 393224 | tf_op jit(solution)/shard_map/ppermute | solution.py:515
  15.9 2.5 %collective-permute-start.1 = (f32[8,4096]{1,0:T(8,128)S(1)}, f32[8,4096]{1,0:T(8,128)S(1)}, u32[]{:S(2)}, u32[]{:S(2)}) collective-permute-start(f32[8,4096]{1,0:T(8,128)S(1)} %get-tuple-element.33), channel_id=1, source_target_pairs={{0,8},{8,16},{16,24},{1,9},{9,17},{17,25},{2,10},{10,18},{18,26},{... | collective-permute-start | bytes 393224 | tf_op jit(solution)/shard_map/ppermute | solution.py:515
  18.4 0.1 merge_clear.2
  18.5 1.6 %collective-permute-start.5 = (f32[2,32,8,128]{3,2,1,0:T(8,128)S(1)}, f32[2,32,8,128]{3,2,1,0:T(8,128)S(1)}, u32[]{:S(2)}, u32[]{:S(2)}) collective-permute-start(f32[2,32,8,128]{3,2,1,0:T(8,128)S(1)} %get-tuple-element.32.rest_0_), channel_id=1, source_target_pairs={{0,2},{1,3},{2,0},{3,1},{4,6},{5,7},{6,4},{7,5},{8,10},{9,11},{10,... | collective-permute-start | bytes 786440 | tf_op jit(solution)/shard_map/ppermute | solution.py:509
  20.1 0.4 slice-done.1
  20.5 4.4 %unlit.1.unlit_ref = f32[8,8,3,64,128]{4,3,2,1,0:T(8,128)S(1)} custom-call(s32[1,1]{1,0:T(1,128)S(6)} %copy.6.index_ref, f32[8,4,16]{2,1,0:T(4,128)S(1)} %copy-done.3, f32[8,64,4096]{2,1,0:T(8,128)S(1)} %bitcast.1, f32[2,32,8,128]{3,2,1,0:T(8,128)S(1)} %get-tuple-element.32.rest_0_), custom_call_target="tpu_custom_call" | custom-call | flops 5242880000 | bytes 2097152 | tf_op jit(solution)/shard_map/unlit/pallas_call | solution.py:370
  25.0 1.7 %lit.1 = (f32[4,3,8,8,128]{4,3,2,1,0:T(8,128)S(1)}, f32[4,3,8,8,128]{4,3,2,1,0:T(8,128)S(1)}) custom-call(s32[4]{0:T(128)S(1)} %copy-done.1, f32[4,3]{1,0:T(4,128)S(1)} %copy-done, f32[8,8,3,64,128]{4,3,2,1,0:T(8,128)S(1)} %unlit.1.unlit_ref, f32[8,4096]{1,0:T(8,128)S(1)} %collective-permute-done.1.rest_0_, f32[8,4096]{1,0:T(8,128)S(1)} %collective-permute-done.2.rest_1_, ...), custom_call_target="tpu_custom_call" | custom-call | tf_op jit(solution)/shard_map/lit/pallas_call | solution.py:390
  26.7 0.1 collective-permute-start.4
  26.8 2.7 %collective-permute-start.7 = (f32[1,32,8,128]{3,2,1,0:T(8,128)S(1)}, f32[1,32,8,128]{3,2,1,0:T(8,128)S(1)}, u32[]{:S(2)}, u32[]{:S(2)}) collective-permute-start(f32[1,32,8,128]{3,2,1,0:T(8,128)S(1)} %get-tuple-element.37.rest_0_), channel_id=1, source_target_pairs={{0,4},{1,5},{2,6},{3,7},{4,0},{5,1},{6,2},{7,3},{8,12},{9,13},{10,... | collective-permute-start | bytes 393224 | tf_op jit(solution)/shard_map/ppermute | solution.py:509
  29.6 1.6 %collective-permute-start.6 = (f32[2,3,8,8,128]{4,3,2,1,0:T(8,128)S(1)}, f32[2,3,8,8,128]{4,3,2,1,0:T(8,128)S(1)}, u32[]{:S(2)}, u32[]{:S(2)}) collective-permute-start(f32[2,3,8,8,128]{4,3,2,1,0:T(8,128)S(1)} %get-tuple-element.39.rest_3_), channel_id=1, source_target_pairs={{0,2},{1,3},{2,0},{3,1},{4,6},{5,7},{6,4},{7,5},{8,10},{9,11},{10,... | collective-permute-start | bytes 589832 | tf_op jit(solution)/shard_map/ppermute | solution.py:509
  31.2 8.3 %shade.2 = (f32[4,3,12,8,128]{4,3,2,1,0:T(8,128)S(1)}, f32[4,3,12,8,128]{4,3,2,1,0:T(8,128)S(1)}) custom-call(s32[1,1]{1,0:T(1,128)S(6)} %copy.6.index_ref, s32[4]{0:T(128)S(1)} %copy-done.1, f32[4,3]{1,0:T(4,128)S(1)} %copy-done, f32[8,4,16]{2,1,0:T(4,128)S(1)} %copy-done.3, f32[8,64,4096]{2,1,0:T(8,128)S(1)} %bitcast.1, ...), custom_call_target="tpu_custom_call" | custom-call | flops 7864320000 | bytes 3145728 | tf_op jit(solution)/shard_map/shade/pallas_call | solution.py:346
  39.5 0.1 collective-permute-start.8
  39.6 1.6 %collective-permute-start.10 = (f32[1,3,8,8,128]{4,3,2,1,0:T(8,128)S(1)}, f32[1,3,8,8,128]{4,3,2,1,0:T(8,128)S(1)}, u32[]{:S(2)}, u32[]{:S(2)}) collective-permute-start(f32[1,3,8,8,128]{4,3,2,1,0:T(8,128)S(1)} %get-tuple-element.43.rest_0_), channel_id=1, source_target_pairs={{0,4},{1,5},{2,6},{3,7},{4,0},{5,1},{6,2},{7,3},{8,12},{9,13},{10,... | collective-permute-start | bytes 294920 | tf_op jit(solution)/shard_map/ppermute | solution.py:509
  41.3 0.3 collective-permute-done.8.other_ref
  41.6 0.1 merge.8
  41.6 1.1 %collective-permute-start.9 = (f32[2,3,12,8,128]{4,3,2,1,0:T(8,128)S(1)}, f32[2,3,12,8,128]{4,3,2,1,0:T(8,128)S(1)}, u32[]{:S(2)}, u32[]{:S(2)}) collective-permute-start(f32[2,3,12,8,128]{4,3,2,1,0:T(8,128)S(1)} %get-tuple-element.45.rest_3_), channel_id=1, source_target_pairs={{0,2},{1,3},{2,0},{3,1},{4,6},{5,7},{6,4},{7,5},{8,10},{9,11},{10,... | collective-permute-start | bytes 884744 | tf_op jit(solution)/shard_map/ppermute | solution.py:509
  42.8 8.3 %shade.3 = (f32[4,3,12,8,128]{4,3,2,1,0:T(8,128)S(1)}, f32[4,3,12,8,128]{4,3,2,1,0:T(8,128)S(1)}) custom-call(s32[1,1]{1,0:T(1,128)S(6)} %copy.6.index_ref, s32[4]{0:T(128)S(1)} %copy-done.1, f32[4,3]{1,0:T(4,128)S(1)} %copy-done, f32[8,4,16]{2,1,0:T(4,128)S(1)} %copy-done.3, f32[8,64,4096]{2,1,0:T(8,128)S(1)} %bitcast.1, ...), custom_call_target="tpu_custom_call" | custom-call | flops 7864320000 | bytes 3145728 | tf_op jit(solution)/shard_map/shade/pallas_call | solution.py:346
  51.1 0.1 collective-permute-start.11
  51.1 1.6 %collective-permute-done.9.other_ref = f32[2,3,12,8,128]{4,3,2,1,0:T(8,128)S(1)} collective-permute-done((f32[2,3,12,8,128]{4,3,2,1,0:T(8,128)S(1)}, f32[2,3,12,8,128]{4,3,2,1,0:T(8,128)S(1)}, u32[]{:S(2)}, u32[]{:S(2)}) %collective-permute-start.9) | collective-permute-done | bytes 294944 | tf_op jit(solution)/shard_map/ppermute | solution.py:509
  52.8 0.3 collective-permute-done.11.other_ref
  53.1 0.1 merge.10
  53.2 1.0 %collective-permute-start.12 = (f32[2,3,12,8,128]{4,3,2,1,0:T(8,128)S(1)}, f32[2,3,12,8,128]{4,3,2,1,0:T(8,128)S(1)}, u32[]{:S(2)}, u32[]{:S(2)}) collective-permute-start(f32[2,3,12,8,128]{4,3,2,1,0:T(8,128)S(1)} %get-tuple-element.51), channel_id=1, source_target_pairs={{0,2},{1,3},{2,0},{3,1},{4,6},{5,7},{6,4},{7,5},{8,10},{9,11},{10,... | collective-permute-start | bytes 884744 | tf_op jit(solution)/shard_map/ppermute | solution.py:509
  54.3 1.6 %collective-permute-start.13 = (f32[1,3,12,8,128]{4,3,2,1,0:T(8,128)S(1)}, f32[1,3,12,8,128]{4,3,2,1,0:T(8,128)S(1)}, u32[]{:S(2)}, u32[]{:S(2)}) collective-permute-start(f32[1,3,12,8,128]{4,3,2,1,0:T(8,128)S(1)} %get-tuple-element.49.rest_0_), channel_id=1, source_target_pairs={{0,4},{1,5},{2,6},{3,7},{4,0},{5,1},{6,2},{7,3},{8,12},{9,13},{10,... | collective-permute-start | bytes 442376 | tf_op jit(solution)/shard_map/ppermute | solution.py:509
  55.8 8.1 %collective-permute-done.13.rest_0_.refs_4_ = f32[1,3,12,8,128]{4,3,2,1,0:T(8,128)S(1)} collective-permute-done((f32[1,3,12,8,128]{4,3,2,1,0:T(8,128)S(1)}, f32[1,3,12,8,128]{4,3,2,1,0:T(8,128)S(1)}, u32[]{:S(2)}, u32[]{:S(2)}) %collective-permute-start.13) | collective-permute-done | bytes 147488 | tf_op jit(solution)/shard_map/ppermute | solution.py:509
  64.0 1.5 %collective-permute-done.12.other_ref = f32[2,3,12,8,128]{4,3,2,1,0:T(8,128)S(1)} collective-permute-done((f32[2,3,12,8,128]{4,3,2,1,0:T(8,128)S(1)}, f32[2,3,12,8,128]{4,3,2,1,0:T(8,128)S(1)}, u32[]{:S(2)}, u32[]{:S(2)}) %collective-permute-start.12) | collective-permute-done | bytes 294944 | tf_op jit(solution)/shard_map/ppermute | solution.py:509
  65.5 2.0 %collective-permute-start.14 = (f32[1,3,12,8,128]{4,3,2,1,0:T(8,128)S(1)}, f32[1,3,12,8,128]{4,3,2,1,0:T(8,128)S(1)}, u32[]{:S(2)}, u32[]{:S(2)}) collective-permute-start(f32[1,3,12,8,128]{4,3,2,1,0:T(8,128)S(1)} %get-tuple-element.53), channel_id=1, source_target_pairs={{0,4},{1,5},{2,6},{3,7},{4,0},{5,1},{6,2},{7,3},{8,12},{9,13},{10,... | collective-permute-start | bytes 442376 | tf_op jit(solution)/shard_map/ppermute | solution.py:509
  67.5 7.2 %collective-permute-done.14.refs_5_ = f32[1,3,12,8,128]{4,3,2,1,0:T(8,128)S(1)} collective-permute-done((f32[1,3,12,8,128]{4,3,2,1,0:T(8,128)S(1)}, f32[1,3,12,8,128]{4,3,2,1,0:T(8,128)S(1)}, u32[]{:S(2)}, u32[]{:S(2)}) %collective-permute-start.14) | collective-permute-done | bytes 147488 | tf_op jit(solution)/shard_map/ppermute | solution.py:509
  74.7 0.9 %last.1 = f32[4,8,4096]{2,1,0:T(8,128)} custom-call(f32[1,3,8,8,128]{4,3,2,1,0:T(8,128)S(1)} %get-tuple-element.41.refs_0_, f32[1,3,12,8,128]{4,3,2,1,0:T(8,128)S(1)} %get-tuple-element.47.refs_1_, f32[1,3,12,8,128]{4,3,2,1,0:T(8,128)S(1)} %get-tuple-element.52.refs_2_, f32[1,3,8,8,128]{4,3,2,1,0:T(8,128)S(1)} %collective-permute-done.10.rest_1_.refs_3_, ...), custom_call_target="tpu_custom_call" | custom-call | tf_op jit(solution)/shard_map/last/pallas_call | solution.py:497
  (25 shorter events, 0.3 us)
Async XLA Ops:
  0.7 0.7 copy-start.2
  1.4 18.7 %slice-start = ((s8[8388608]{0:T(1024)(128)(4,1)}), s8[4194304]{0:T(1024)(128)(4,1)S(1)}, s32[]{:S(2)}) async-start(s8[8388608]{0:T(1024)(128)(4,1)} %bitcast), calls=%async_computation | async-start | bytes 8388608
  8.7 9.7 %collective-permute-start = (f32[4,32,8,128]{3,2,1,0:T(8,128)S(1)}, f32[4,32,8,128]{3,2,1,0:T(8,128)S(1)}, u32[]{:S(2)}, u32[]{:S(2)}) collective-permute-start(f32[4,32,8,128]{3,2,1,0:T(8,128)S(1)} %get-tuple-element.31), channel_id=1, source_target_pairs={{0,1},{1,0},{2,3},{3,2},{4,5},{5,4},{6,7},{7,6},{8,9},{9,8},{10,11... | collective-permute-start | bytes 1572872 | tf_op jit(solution)/shard_map/ppermute | solution.py:509
  9.2 15.8 %collective-permute-start.3 = (f32[8,4096]{1,0:T(8,128)S(1)}, f32[8,4096]{1,0:T(8,128)S(1)}, u32[]{:S(2)}, u32[]{:S(2)}) collective-permute-start(f32[8,4096]{1,0:T(8,128)S(1)} %get-tuple-element.33), channel_id=1, source_target_pairs={{0,24},{1,25},{2,26},{3,27},{4,28},{5,29},{6,30},{7,31}} | collective-permute-start | bytes 393224 | tf_op jit(solution)/shard_map/ppermute | solution.py:515
  14.6 10.4 %collective-permute-start.2 = (f32[8,4096]{1,0:T(8,128)S(1)}, f32[8,4096]{1,0:T(8,128)S(1)}, u32[]{:S(2)}, u32[]{:S(2)}) collective-permute-start(f32[8,4096]{1,0:T(8,128)S(1)} %get-tuple-element.33), channel_id=1, source_target_pairs={{0,16},{8,24},{1,17},{9,25},{2,18},{10,26},{3,19},{11,27},{4,20},{... | collective-permute-start | bytes 393224 | tf_op jit(solution)/shard_map/ppermute | solution.py:515
  15.9 9.1 %collective-permute-start.1 = (f32[8,4096]{1,0:T(8,128)S(1)}, f32[8,4096]{1,0:T(8,128)S(1)}, u32[]{:S(2)}, u32[]{:S(2)}) collective-permute-start(f32[8,4096]{1,0:T(8,128)S(1)} %get-tuple-element.33), channel_id=1, source_target_pairs={{0,8},{8,16},{16,24},{1,9},{9,17},{17,25},{2,10},{10,18},{18,26},{... | collective-permute-start | bytes 393224 | tf_op jit(solution)/shard_map/ppermute | solution.py:515
  18.3 2.2 %slice-start.1 = ((s8[8388608]{0:T(1024)(128)(4,1)}), s8[4194304]{0:T(1024)(128)(4,1)S(1)}, s32[]{:S(2)}) async-start(s8[8388608]{0:T(1024)(128)(4,1)} %bitcast), calls=%async_computation.1 | async-start | bytes 8388608
  18.4 2.2 %copy-start.3 = (f32[8,4,16]{2,1,0:T(4,128)S(1)}, f32[8,4,16]{2,1,0:T(4,128)}, u32[]{:S(2)}) copy-start(f32[8,4,16]{2,1,0:T(4,128)} %tables_ref.7) | copy-start | bytes 6148
  18.5 6.5 %copy-start = (f32[4,3]{1,0:T(4,128)S(1)}, f32[4,3]{1,0:T(4,128)}, u32[]{:S(2)}) copy-start(f32[4,3]{1,0:T(4,128)} %tint_ref.5) | copy-start | bytes 148
  18.5 6.5 %copy-start.1 = (s32[4]{0:T(128)S(1)}, s32[4]{0:T(128)}, u32[]{:S(2)}) copy-start(s32[4]{0:T(128)} %code_ref.5) | copy-start | bytes 52
  18.5 8.3 %collective-permute-start.5 = (f32[2,32,8,128]{3,2,1,0:T(8,128)S(1)}, f32[2,32,8,128]{3,2,1,0:T(8,128)S(1)}, u32[]{:S(2)}, u32[]{:S(2)}) collective-permute-start(f32[2,32,8,128]{3,2,1,0:T(8,128)S(1)} %get-tuple-element.32.rest_0_), channel_id=1, source_target_pairs={{0,2},{1,3},{2,0},{3,1},{4,6},{5,7},{6,4},{7,5},{8,10},{9,11},{10,... | collective-permute-start | bytes 786440 | tf_op jit(solution)/shard_map/ppermute | solution.py:509
  26.7 2.8 %collective-permute-start.4 = (f32[4,3,8,8,128]{4,3,2,1,0:T(8,128)S(1)}, f32[4,3,8,8,128]{4,3,2,1,0:T(8,128)S(1)}, u32[]{:S(2)}, u32[]{:S(2)}) collective-permute-start(f32[4,3,8,8,128]{4,3,2,1,0:T(8,128)S(1)} %get-tuple-element.35.rest_0_), channel_id=1, source_target_pairs={{0,1},{1,0},{2,3},{3,2},{4,5},{5,4},{6,7},{7,6},{8,9},{9,8},{10,11... | collective-permute-start | bytes 1179656 | tf_op jit(solution)/shard_map/ppermute | solution.py:509
  26.8 12.7 %collective-permute-start.7 = (f32[1,32,8,128]{3,2,1,0:T(8,128)S(1)}, f32[1,32,8,128]{3,2,1,0:T(8,128)S(1)}, u32[]{:S(2)}, u32[]{:S(2)}) collective-permute-start(f32[1,32,8,128]{3,2,1,0:T(8,128)S(1)} %get-tuple-element.37.rest_0_), channel_id=1, source_target_pairs={{0,4},{1,5},{2,6},{3,7},{4,0},{5,1},{6,2},{7,3},{8,12},{9,13},{10,... | collective-permute-start | bytes 393224 | tf_op jit(solution)/shard_map/ppermute | solution.py:509
  29.6 10.0 %collective-permute-start.6 = (f32[2,3,8,8,128]{4,3,2,1,0:T(8,128)S(1)}, f32[2,3,8,8,128]{4,3,2,1,0:T(8,128)S(1)}, u32[]{:S(2)}, u32[]{:S(2)}) collective-permute-start(f32[2,3,8,8,128]{4,3,2,1,0:T(8,128)S(1)} %get-tuple-element.39.rest_3_), channel_id=1, source_target_pairs={{0,2},{1,3},{2,0},{3,1},{4,6},{5,7},{6,4},{7,5},{8,10},{9,11},{10,... | collective-permute-start | bytes 589832 | tf_op jit(solution)/shard_map/ppermute | solution.py:509
  39.5 2.1 %collective-permute-start.8 = (f32[4,3,12,8,128]{4,3,2,1,0:T(8,128)S(1)}, f32[4,3,12,8,128]{4,3,2,1,0:T(8,128)S(1)}, u32[]{:S(2)}, u32[]{:S(2)}) collective-permute-start(f32[4,3,12,8,128]{4,3,2,1,0:T(8,128)S(1)} %get-tuple-element.40.rest_0_), channel_id=1, source_target_pairs={{0,1},{1,0},{2,3},{3,2},{4,5},{5,4},{6,7},{7,6},{8,9},{9,8},{10,11... | collective-permute-start | bytes 1769480 | tf_op jit(solution)/shard_map/ppermute | solution.py:509
  39.6 11.5 %collective-permute-start.10 = (f32[1,3,8,8,128]{4,3,2,1,0:T(8,128)S(1)}, f32[1,3,8,8,128]{4,3,2,1,0:T(8,128)S(1)}, u32[]{:S(2)}, u32[]{:S(2)}) collective-permute-start(f32[1,3,8,8,128]{4,3,2,1,0:T(8,128)S(1)} %get-tuple-element.43.rest_0_), channel_id=1, source_target_pairs={{0,4},{1,5},{2,6},{3,7},{4,0},{5,1},{6,2},{7,3},{8,12},{9,13},{10,... | collective-permute-start | bytes 294920 | tf_op jit(solution)/shard_map/ppermute | solution.py:509
  41.6 11.1 %collective-permute-start.9 = (f32[2,3,12,8,128]{4,3,2,1,0:T(8,128)S(1)}, f32[2,3,12,8,128]{4,3,2,1,0:T(8,128)S(1)}, u32[]{:S(2)}, u32[]{:S(2)}) collective-permute-start(f32[2,3,12,8,128]{4,3,2,1,0:T(8,128)S(1)} %get-tuple-element.45.rest_3_), channel_id=1, source_target_pairs={{0,2},{1,3},{2,0},{3,1},{4,6},{5,7},{6,4},{7,5},{8,10},{9,11},{10,... | collective-permute-start | bytes 884744 | tf_op jit(solution)/shard_map/ppermute | solution.py:509
  51.1 2.1 %collective-permute-start.11 = (f32[4,3,12,8,128]{4,3,2,1,0:T(8,128)S(1)}, f32[4,3,12,8,128]{4,3,2,1,0:T(8,128)S(1)}, u32[]{:S(2)}, u32[]{:S(2)}) collective-permute-start(f32[4,3,12,8,128]{4,3,2,1,0:T(8,128)S(1)} %get-tuple-element.46.rest_0_), channel_id=1, source_target_pairs={{0,1},{1,0},{2,3},{3,2},{4,5},{5,4},{6,7},{7,6},{8,9},{9,8},{10,11... | collective-permute-start | bytes 1769480 | tf_op jit(solution)/shard_map/ppermute | solution.py:509
  53.2 12.3 %collective-permute-start.12 = (f32[2,3,12,8,128]{4,3,2,1,0:T(8,128)S(1)}, f32[2,3,12,8,128]{4,3,2,1,0:T(8,128)S(1)}, u32[]{:S(2)}, u32[]{:S(2)}) collective-permute-start(f32[2,3,12,8,128]{4,3,2,1,0:T(8,128)S(1)} %get-tuple-element.51), channel_id=1, source_target_pairs={{0,2},{1,3},{2,0},{3,1},{4,6},{5,7},{6,4},{7,5},{8,10},{9,11},{10,... | collective-permute-start | bytes 884744 | tf_op jit(solution)/shard_map/ppermute | solution.py:509
  54.3 9.7 %collective-permute-start.13 = (f32[1,3,12,8,128]{4,3,2,1,0:T(8,128)S(1)}, f32[1,3,12,8,128]{4,3,2,1,0:T(8,128)S(1)}, u32[]{:S(2)}, u32[]{:S(2)}) collective-permute-start(f32[1,3,12,8,128]{4,3,2,1,0:T(8,128)S(1)} %get-tuple-element.49.rest_0_), channel_id=1, source_target_pairs={{0,4},{1,5},{2,6},{3,7},{4,0},{5,1},{6,2},{7,3},{8,12},{9,13},{10,... | collective-permute-start | bytes 442376 | tf_op jit(solution)/shard_map/ppermute | solution.py:509
  65.5 9.2 %collective-permute-start.14 = (f32[1,3,12,8,128]{4,3,2,1,0:T(8,128)S(1)}, f32[1,3,12,8,128]{4,3,2,1,0:T(8,128)S(1)}, u32[]{:S(2)}, u32[]{:S(2)}) collective-permute-start(f32[1,3,12,8,128]{4,3,2,1,0:T(8,128)S(1)} %get-tuple-element.53), channel_id=1, source_target_pairs={{0,4},{1,5},{2,6},{3,7},{4,0},{5,1},{6,2},{7,3},{8,12},{9,13},{10,... | collective-permute-start | bytes 442376 | tf_op jit(solution)/shard_map/ppermute | solution.py:509

commit v2 on v1

--- a/solution.py
+++ b/solution.py
@@ -12,7 +12,7 @@
 SUB = 8
 DRIFTS = (-1, 0, 1)
 VMEM_LIMIT = 24 * 2**20
-STREAM_LIMIT = 52 * 2**20
+STREAM_LIMIT = 44 * 2**20
 F32 = jnp.float32
 
 
@@ -28,13 +28,13 @@
     return jnp.take_along_axis(table, index, axis=0, mode="promise_in_bounds")
 
 
-def fill_coefficients(which, tables_ref, coef, sigma_scale, properties):
-    rows = tables_ref[which]
+def fill_coefficients(table_ref, coef, sigma_scale):
+    rows = table_ref[...]
     knots = rows.shape[1]
     at_row = lax.broadcasted_iota(jnp.int32, (2 * SUB, knots), 0)
     at_col = lax.broadcasted_iota(jnp.int32, (2 * SUB, knots), 1)
     left_at = jnp.minimum(at_row, knots - 2)
-    for q in range(properties):
+    for q in range(rows.shape[0]):
         row = jnp.broadcast_to(rows[q : q + 1], (2 * SUB, knots))
         left = jnp.sum(jnp.where(at_col == left_at, row, 0.0), axis=1, keepdims=True)
         right = jnp.sum(jnp.where(at_col == left_at + 1, row, 0.0), axis=1, keepdims=True)
@@ -65,36 +65,36 @@
     return [coef[4 * q + at] for at in range(4)]
 
 
-def fetch_tile(density_ref, buffer, sems, first, tile):
-    columns = pl.ds(pl.multiple_of(first + tile * LANE, LANE), LANE)
-    return pltpu.make_async_copy(density_ref.at[:, :, columns], buffer.at[tile], sems.at[tile])
-
-
-def sums_kernel(sigma_scale, ratio, first, bits, split, index_ref, tables_ref, density_ref, *rest):
+def fetch_tile(density_ref, cells_ref, sems, tile):
+    columns = pl.ds(pl.multiple_of(tile * LANE, LANE), LANE)
+    return pltpu.make_async_copy(density_ref.at[:, :, columns], cells_ref.at[tile], sems.at[tile])
+
+
+def sums_kernel(sigma_scale, ratio, bits, split, table_ref, density_ref, *rest):
     if split:
-        leaving_ref, send_ref, keep_ref, coef, buffer, clear, sems = rest
+        leaving_ref, cells_ref, coef, send_ref, keep_ref, clear, sems = rest
     else:
-        leaving_ref, coef, buffer, sems = rest
-    tiles, layers, slices, _ = buffer.shape
-    knots = tables_ref.shape[2]
+        leaving_ref, cells_ref, coef, sems = rest
+    tiles, layers, slices, _ = cells_ref.shape
+    knots = table_ref.shape[1]
 
     @pl.loop(0, tiles)
     def _(tile):
-        fetch_tile(density_ref, buffer, sems, first, tile).start()
-
-    fill_coefficients(index_ref[0, 0], tables_ref, coef, sigma_scale, 1)
+        fetch_tile(density_ref, cells_ref, sems, tile).start()
+
+    fill_coefficients(table_ref, coef, sigma_scale)
     mine = lax.axis_index("view") & 1 if split else 0
     half = (1 << bits) // 2
 
     @pl.loop(0, tiles)
     def _(tile):
-        fetch_tile(density_ref, buffer, sems, first, tile).wait()
+        fetch_tile(density_ref, cells_ref, sems, tile).wait()
         table = table_of(coef, 0)
         down = [jnp.zeros((SUB, LANE), F32) for _ in range(layers)]
         for block in range(slices // SUB):
             through = jnp.zeros((SUB, LANE), F32)
             for b in range(layers):
-                cells = buffer[tile, b, block * SUB : block * SUB + SUB]
+                cells = cells_ref[tile, b, block * SUB : block * SUB + SUB]
                 sigma = value_at(table, place_of(cells, knots), cells)
                 through = through + sigma
                 down[b] = down[b] + sigma
@@ -152,14 +152,14 @@
         lighting[k] = shade[:, LANE : LANE + width]
 
 
-def weights_of(coef, buffer, tile, b, ahead, ratio, knots):
+def weights_of(coef, cells_ref, tile, b, ahead, ratio, knots):
     steps = len(ahead)
     sublane = lax.broadcasted_iota(jnp.int32, (SUB, LANE), 0)
     table = table_of(coef, 0)
     cells, places, sigma = [], [], []
     before, running = [], None
     for j in range(steps):
-        cells.append(buffer[tile, b, pl.ds(j, SUB, stride=steps), :])
+        cells.append(cells_ref[tile, b, pl.ds(j, SUB, stride=steps), :])
         places.append(place_of(cells[j], knots))
         sigma.append(value_at(table, places[j], cells[j]))
         before.append(running)
@@ -193,34 +193,28 @@
 
 
 def shade_kernel(
-    sigma_scale, ratio, first, total, bits, pieces, far, late, whole_out,
-    index_ref, code_ref, tint_ref, tables_ref, density_ref, *rest,
+    ratio, knots, first, total, bits, pieces, far, late, whole_out,
+    code_ref, tint_ref, coef, cells_ref, *rest,
 ):
     brick_refs = [rest[at * len(pieces) : (at + 1) * len(pieces)] for at in range(far)]
     rest = rest[far * len(pieces) + late :]
     if whole_out:
-        out_ref, coef, buffer, lighting, sums, sems = rest
+        out_ref, lighting, sums = rest
     else:
-        send_ref, keep_ref, coef, buffer, lighting, sums, sems = rest
-    tiles, layers, slices, _ = buffer.shape
-    knots = tables_ref.shape[2]
+        send_ref, keep_ref, lighting, sums = rest
+    layers, slices = cells_ref.shape[1:3]
     steps = slices // SUB
     channels = lighting.shape[0]
-
-    @pl.loop(0, tiles)
+    fill_lighting(pieces, brick_refs, code_ref, tint_ref, lighting, first, total)
+
+    @pl.loop(0, lighting.shape[2] // LANE)
     def _(tile):
-        fetch_tile(density_ref, buffer, sems, first, tile).start()
-
-    fill_coefficients(index_ref[0, 0], tables_ref, coef, sigma_scale, tables_ref.shape[1])
-    fill_lighting(pieces, brick_refs, code_ref, tint_ref, lighting, first, total)
-
-    @pl.loop(0, tiles)
-    def _(tile):
-        fetch_tile(density_ref, buffer, sems, first, tile).wait()
         columns = pl.ds(pl.multiple_of(tile * LANE, LANE), LANE)
         ahead = [None] * steps
         for b in range(layers):
-            cells, places, weights = weights_of(coef, buffer, tile, b, ahead, ratio, knots)
+            cells, places, weights = weights_of(
+                coef, cells_ref, first // LANE + tile, b, ahead, ratio, knots
+            )
             for k in range(channels):
                 lit = jnp.broadcast_to(lighting[k, b : b + 1, columns], (SUB, LANE))
                 table = [entry * lit for entry in table_of(coef, k + 1)]
@@ -244,25 +238,19 @@
             put_halves(send_ref, keep_ref, sums, tile, bits)
 
 
-def unlit_kernel(sigma_scale, ratio, first, late, index_ref, tables_ref, density_ref, *rest):
-    out_ref, coef, buffer, sems = rest[late:]
-    tiles, layers, slices, _ = buffer.shape
-    knots = tables_ref.shape[2]
+def unlit_kernel(ratio, knots, first, late, coef, cells_ref, *rest):
+    out_ref = rest[late]
+    tiles, layers, channels, slices, _ = out_ref.shape
     steps = slices // SUB
 
     @pl.loop(0, tiles)
     def _(tile):
-        fetch_tile(density_ref, buffer, sems, first, tile).start()
-
-    fill_coefficients(index_ref[0, 0], tables_ref, coef, sigma_scale, tables_ref.shape[1])
-
-    @pl.loop(0, tiles)
-    def _(tile):
-        fetch_tile(density_ref, buffer, sems, first, tile).wait()
         ahead = [None] * steps
         for b in range(layers):
-            cells, places, weights = weights_of(coef, buffer, tile, b, ahead, ratio, knots)
-            for k in range(out_ref.shape[2]):
+            cells, places, weights = weights_of(
+                coef, cells_ref, first // LANE + tile, b, ahead, ratio, knots
+            )
+            for k in range(channels):
                 table = table_of(coef, k + 1)
                 for j in range(steps):
                     term = value_at(table, places[j], cells[j]) * weights[j]
@@ -300,87 +288,79 @@
     return jax.ShapeDtypeStruct(dims, F32)
 
 
-def cost(density, columns, per_cell):
-    cells = density.shape[0] * density.shape[1] * columns
-    return pl.CostEstimate(flops=cells * per_cell, bytes_accessed=4 * cells, transcendentals=0)
+def cost(cells, columns, per_cell):
+    count = cells.shape[1] * cells.shape[2] * columns
+    return pl.CostEstimate(flops=count * per_cell, bytes_accessed=4 * count, transcendentals=0)
 
 
 MERGE_COST = pl.CostEstimate(flops=2 * 10**10, bytes_accessed=2**20, transcendentals=0)
 
 
-def sums(density, tables, index, low, high, sigma_scale, ratio, bits, split):
-    layers, slices, _ = density.shape
-    tiles = (high - low) // LANE
+def sums(density, table, sigma_scale, ratio, bits, split):
+    layers, slices, total = density.shape
+    tiles = total // LANE
     half = (1 << bits) // 2
-    outs = [shape(layers, high - low)]
-    scratch = [pltpu.VMEM((4, SUB, LANE), F32), pltpu.VMEM((tiles, layers, slices, LANE), F32)]
+    outs = [
+        shape(layers, total),
+        shape(tiles, layers, slices, LANE),
+        shape(4 * table.shape[0], SUB, LANE),
+    ]
+    cells_shape = outs[1]
+    scratch = []
     if split:
         outs += [shape(half, tiles, SUB, LANE)] * 2
         scratch.append(pltpu.VMEM((slices // SUB, SUB, LANE), F32))
     scratch.append(pltpu.SemaphoreType.DMA((tiles,)))
     return pl.pallas_call(
-        functools.partial(sums_kernel, sigma_scale, ratio, low, bits, split),
-        in_specs=[SMEM(), VMEM(), HBM()],
+        functools.partial(sums_kernel, sigma_scale, ratio, bits, split),
+        in_specs=[VMEM(), HBM()],
         out_specs=[VMEM()] * len(outs),
         out_shape=outs,
         scratch_shapes=scratch,
         compiler_params=params(STREAM_LIMIT),
-        cost_estimate=cost(density, high - low, 4000),
+        cost_estimate=cost(cells_shape, total, 4000),
         name="sums",
-    )(index, tables, density)
-
-
-def shade(
-    density, tables, index, code, tint, bricks, pieces, low, high, sigma_scale, ratio, bits,
-    whole_out, after=(),
-):
-    layers, slices, total = density.shape
+    )(table, density)
+
+
+def shade(coef, cells, knots, code, tint, bricks, pieces, low, high, ratio, bits, whole_out, after=()):
+    tiles, layers, slices, _ = cells.shape
     channels = tint.shape[1]
-    tiles = (high - low) // LANE
     half = (1 << bits) // 2
     if whole_out:
-        outs = [shape(channels + 1, tiles, slices, LANE)]
+        outs = [shape(channels + 1, (high - low) // LANE, slices, LANE)]
     else:
-        outs = [shape(half, channels, tiles, SUB, LANE)] * 2
+        outs = [shape(half, channels, (high - low) // LANE, SUB, LANE)] * 2
     operands = [row for rows in bricks for row in rows]
     return pl.pallas_call(
         functools.partial(
-            shade_kernel, sigma_scale, ratio, low, total, bits, pieces, len(bricks), len(after),
+            shade_kernel, ratio, knots, low, tiles * LANE, bits, pieces, len(bricks), len(after),
             whole_out,
         ),
-        in_specs=[SMEM()] * 3 + [VMEM(), HBM()] + [VMEM()] * len(operands) + [ANY()] * len(after),
+        in_specs=[SMEM()] * 2 + [VMEM()] * (2 + len(operands)) + [ANY()] * len(after),
         out_specs=[VMEM()] * len(outs),
         out_shape=outs,
         scratch_shapes=[
-            pltpu.VMEM((4 * tables.shape[1], SUB, LANE), F32),
-            pltpu.VMEM((tiles, layers, slices, LANE), F32),
             pltpu.VMEM((channels, layers, high - low), F32),
             pltpu.VMEM((channels + 1, slices, LANE), F32),
-            pltpu.SemaphoreType.DMA((tiles,)),
         ],
         compiler_params=params(),
-        cost_estimate=cost(density, high - low, 10000),
+        cost_estimate=cost(cells, high - low, 10000),
         name="shade",
-    )(index, code, tint, tables, density, *operands, *after)
-
-
-def unlit(density, tables, index, low, high, sigma_scale, ratio, after=()):
-    layers, slices, _ = density.shape
-    tiles = (high - low) // LANE
+    )(code, tint, coef, cells, *operands, *after)
+
+
+def unlit(coef, cells, knots, channels, low, high, ratio, after=()):
+    layers, slices = cells.shape[1:3]
     return pl.pallas_call(
-        functools.partial(unlit_kernel, sigma_scale, ratio, low, len(after)),
-        in_specs=[SMEM(), VMEM(), HBM()] + [ANY()] * len(after),
+        functools.partial(unlit_kernel, ratio, knots, low, len(after)),
+        in_specs=[VMEM()] * 2 + [ANY()] * len(after),
         out_specs=VMEM(),
-        out_shape=shape(tiles, layers, tables.shape[1] - 1, slices, LANE),
-        scratch_shapes=[
-            pltpu.VMEM((4 * tables.shape[1], SUB, LANE), F32),
-            pltpu.VMEM((tiles, layers, slices, LANE), F32),
-            pltpu.SemaphoreType.DMA((tiles,)),
-        ],
+        out_shape=shape((high - low) // LANE, layers, channels, slices, LANE),
         compiler_params=params(),
-        cost_estimate=cost(density, high - low, 10000),
+        cost_estimate=cost(cells, high - low, 10000),
         name="unlit",
-    )(index, tables, density, *after)
+    )(coef, cells, *after)
 
 
 def lit(cells, code, tint, bricks, pieces, low, high, total, bits, after=()):
@@ -426,10 +406,10 @@
     )(own, other, *after)
 
 
-def merge_kernel(bit, start, own_ref, other_ref, own_clear_ref, other_clear_ref, *rest):
+def merge_kernel(bit, start, joined, own_ref, other_ref, own_clear_ref, other_clear_ref, *rest):
     send_ref, keep_ref = rest[-2:]
-    tiles = pl.ds(start, own_ref.shape[2])
-    half = send_ref.shape[0]
+    half, channels, count = keep_ref.shape[:3]
+    tiles = pl.ds(start, count)
     me = lax.axis_index("view")
     mine = me >> bit + 1 & 1
 
@@ -438,8 +418,12 @@
             for to_ref, side in ((send_ref, 1 - mine), (keep_ref, mine)):
                 source = side * half + at
                 clear = clear_ref[source, tiles]
-                for k in range(send_ref.shape[1]):
-                    to_ref[at, k] = front_ref[source, k] + clear * back_ref[source, k]
+                for k in range(channels):
+                    value = front_ref[source, k] + clear * back_ref[source, k]
+                    if joined and to_ref is send_ref:
+                        send_ref[k * count : (k + 1) * count] = value
+                    else:
+                        to_ref[at, k] = value
 
     upper = me >> bit & 1 == 1
 
@@ -451,57 +435,71 @@
     def _():
         merged(own_ref, other_ref, own_clear_ref)
 
-
-def merge(own, other, own_clear, other_clear, bit, low, after=()):
-    half = shape(own.shape[0] // 2, *own.shape[1:])
+    if joined:
+        send_ref[channels * count :] = rest[0][0]
+
+
+def merge(own, other, own_clear, other_clear, bit, low, joined=(), after=()):
+    count, channels, tiles = own.shape[:3]
+    half = shape(count // 2, *own.shape[1:])
+    outs = [half] * 2
+    if joined:
+        outs = [shape(channels * tiles + joined[0].shape[1], SUB, LANE), half]
     return pl.pallas_call(
-        functools.partial(merge_kernel, bit, low // LANE),
-        in_specs=[VMEM()] * 4 + [ANY()] * len(after),
-        out_specs=[VMEM()] * 2,
-        out_shape=[half] * 2,
+        functools.partial(merge_kernel, bit, low // LANE, bool(joined)),
+        in_specs=[VMEM()] * (4 + len(joined)) + [ANY()] * len(after),
+        out_specs=[VMEM()] * len(outs),
+        out_shape=outs,
         compiler_params=params(),
         cost_estimate=MERGE_COST,
         name="merge",
-    )(own, other, own_clear, other_clear, *after)
+    )(own, other, own_clear, other_clear, *joined, *after)
 
 
 def last_kernel(bit, firsts, *refs):
     chunks = len(firsts)
-    own_clear_ref, other_clear_ref = refs[2 * chunks : 2 * chunks + 2]
-    image_ref = refs[-1]
+    owns, others = refs[:chunks], refs[chunks : 2 * chunks]
+    own_clear_ref, image_ref = refs[2 * chunks :]
+    channels, joined_tiles = owns[0].shape[1:3]
     upper = lax.axis_index("view") >> bit & 1 == 1
 
-    def merged(fronts, backs, clear_ref):
-        for first, front_ref, back_ref in zip(firsts, fronts, backs):
-            channels, tiles = front_ref.shape[1:3]
-            for tile in range(tiles):
+    def other_clear(tile):
+        return others[0][channels * joined_tiles + tile]
+
+    def merged(swapped):
+        for at, first in enumerate(firsts):
+            for tile in range(owns[at].shape[2]):
                 columns = slice(first + tile * LANE, first + tile * LANE + LANE)
-                clear = clear_ref[0, first // LANE + tile]
+                whole = first // LANE + tile
+                clear = other_clear(whole) if swapped else own_clear_ref[0, whole]
                 for k in range(channels):
-                    image_ref[k, :, columns] = front_ref[0, k, tile] + clear * back_ref[0, k, tile]
+                    own = owns[at][0, k, tile]
+                    other = others[at][k * joined_tiles + tile] if at == 0 else others[at][0, k, tile]
+                    front, back = (other, own) if swapped else (own, other)
+                    image_ref[k, :, columns] = front + clear * back
 
     for tile in range(own_clear_ref.shape[1]):
         columns = slice(tile * LANE, tile * LANE + LANE)
-        image_ref[image_ref.shape[0] - 1, :, columns] = own_clear_ref[0, tile] * other_clear_ref[0, tile]
+        image_ref[channels, :, columns] = own_clear_ref[0, tile] * other_clear(tile)
 
     @pl.when(upper)
     def _():
-        merged(refs[chunks : 2 * chunks], refs[:chunks], other_clear_ref)
+        merged(True)
 
     @pl.when(jnp.logical_not(upper))
     def _():
-        merged(refs[:chunks], refs[chunks : 2 * chunks], own_clear_ref)
-
-
-def last(owns, others, own_clear, other_clear, bit, firsts, total):
+        merged(False)
+
+
+def last(owns, others, own_clear, bit, firsts, total):
     return pl.pallas_call(
         functools.partial(last_kernel, bit, firsts),
-        in_specs=[VMEM()] * (2 * len(owns) + 2),
+        in_specs=[VMEM()] * (2 * len(owns) + 1),
         out_specs=VMEM(),
         out_shape=shape(owns[0].shape[1] + 1, SUB, total),
         compiler_params=params(),
         name="last",
-    )(*owns, *others, own_clear, other_clear)
+    )(*owns, *others, own_clear)
 
 
 def swap(block, bit):
@@ -522,13 +520,13 @@
     return jnp.concatenate([front[:-1] + clear * back[:-1], clear * back[-1:]])
 
 
-def plain(density, tables, table_index, light_code, light_tint, sigma_scale, ratio, bits):
+def plain(density, table, light_code, light_tint, sigma_scale, ratio, bits):
     slices, total = density.shape[1:]
-    [leaving] = sums(density, tables, table_index, 0, total, sigma_scale, ratio, 0, False)
+    leaving, cells, coef = sums(density, table, sigma_scale, ratio, 0, False)
     bricks = [[row] for row in from_earlier(leaving)]
     parts = shade(
-        density, tables, table_index, light_code, light_tint, bricks, [(0, total)], 0, total,
-        sigma_scale, ratio, 0, True,
+        coef, cells, table.shape[1], light_code, light_tint, bricks, [(0, total)], 0, total, ratio,
+        0, True,
     )[0]
     rows = slices >> bits
     depth = parts.shape[0]
@@ -543,7 +541,7 @@
     return current.reshape(depth, rows, total)
 
 
-CUTS = (0.25, 0.625)
+CUTS = (0.25, 0.6875)
 
 
 def ranges(cuts, total):
@@ -557,40 +555,41 @@
     bits = views.bit_length() - 1
     sigma_scale = -math.log2(math.e) / (layers * views)
     ratio = layers * views / (slices * lax.axis_size("light"))
+    chosen = jnp.arange(tables.shape[0], dtype=jnp.int32) == table_index[0, 0]
+    table = jnp.sum(jnp.where(chosen[:, None, None], tables, 0.0), axis=0)
     if views * SUB != slices or bits != 3:
-        return plain(
-            density, tables, table_index, light_code, light_tint, sigma_scale, ratio, bits
-        )
+        return plain(density, table, light_code, light_tint, sigma_scale, ratio, bits)
     pieces = [(0, total)]
     chunks = ranges(CUTS, total)
-    leaving, send, keep = sums(
-        density, tables, table_index, 0, total, sigma_scale, ratio, bits, True
+    knots = table.shape[1]
+    leaving, cells, coef, send, keep = sums(
+        density, table, sigma_scale, ratio, bits, True
     )
     bricks = [[row] for row in from_earlier(leaving)]
     clear = [(keep, swap(send, 0))]
     send, keep = merge_clear(*clear[0], 0)
     clear.append((keep, swap(send, 1)))
-    first = unlit(
-        density, tables, table_index, *chunks[0], sigma_scale, ratio, after=(send,)
-    )
-    state = [None] * len(chunks)
-    state[0] = lit(first, light_code, light_tint, bricks, pieces, *chunks[0], total, bits)
-    send, keep = merge_clear(*clear[1], 1, after=(state[0][0],))
-    clear.append((keep, swap(send, 2)))
-    done = send
+    first = unlit(coef, cells, knots, light_tint.shape[1], *chunks[0], ratio, after=(send,))
+    state = [lit(first, light_code, light_tint, bricks, pieces, *chunks[0], total, bits)]
+    clear_send, own_clear = merge_clear(*clear[1], 1, after=(state[0][0],))
+    done = clear_send
     for at, (low, high) in enumerate(chunks):
         if at:
-            state[at] = shade(
-                density, tables, table_index, light_code, light_tint, bricks, pieces, low, high,
-                sigma_scale, ratio, bits, False, after=(done,),
+            state.append(
+                shade(
+                    coef, cells, knots, light_code, light_tint, bricks, pieces, low, high, ratio,
+                    bits, False, after=(done,),
+                )
             )
             done = state[at][0]
         send, keep = state[at]
         arrived = swap(send, 0)
         if at:
-            before = chunks[at - 1][0]
-            settled = state[at - 2][1] if at > 1 else clear[2][1]
-            late = merge(*state[at - 1], *clear[1], 1, before, after=(done, settled))
+            settled = (done,) if at == 1 else (done, state[at - 2][1])
+            late = merge(
+                *state[at - 1], *clear[1], 1, chunks[at - 1][0],
+                joined=(clear_send,) if at == 1 else (), after=settled,
+            )
             state[at - 1] = (late[1], swap(late[0], 2))
             done = late[0]
         send, keep = merge(keep, arrived, *clear[0], 0, low, after=(done,))
@@ -599,7 +598,7 @@
     late = merge(*state[-1], *clear[1], 1, chunks[-1][0], after=(state[-2][1],))
     state[-1] = (late[1], swap(late[0], 2))
     owns, others = zip(*state)
-    return last(owns, others, *clear[2], 2, [low for low, _ in chunks], total)
+    return last(owns, others, own_clear, 2, [low for low, _ in chunks], total)
 
 
 def solution(mesh):

time: 75.9 us -> 74.2 us (0.978)
  Pallas kernels: 31.3 us -> 29.4 us
  waiting for transfers between devices: 19.1 us -> 20.7 us
  local copies, waits for them, and re-layouts: 1.16 us -> 0.01 us
  starting transfers between devices: 23.1 us -> 22.1 us
  other arithmetic: 0.01 us -> 0.81 us
    pallas_call x10, Pallas kernels: 28.6 us -> 26.8 us  [the longest x2 15.3 us: shade(): pl.pallas_call(functools.partial(shade_kernel, ratio, knots, low, tiles *...]
    ppermute x12 -> x11, waiting for transfers between devices: 19.1 us -> 20.7 us  [swap(): lax.ppermute(block, 'view', [(at, at ^ 1 << bit) for at in range(count)])]
    unnamed x12 -> x4, local copies, waits for them, and re-layouts: 1.16 us -> 0.01 us
    ppermute x12 -> x11, starting transfers between devices: 14 us -> 13 us  [swap(): lax.ppermute(block, 'view', [(at, at ^ 1 << bit) for at in range(count)])]
    reduce_sum x0 -> x1, other arithmetic: none -> 0.8 us  [local(): table = jnp.sum(jnp.where(chosen[:, None, None], tables, 0.0), axis=0)]
  transfers between devices with their start and end apart: 15 -> 14, of which waited for: 6 -> 7; matrix products, arithmetic and copies ran while one was open for 0% -> 0% of each run, Pallas kernels for 30% -> 29%
where the time goes in v2:
time: 74.2 us; the launch traced here: 73.9 us
  Pallas kernels  29.4 us (40%)
  starting transfers between devices  22.1 us (30%)
  waiting for transfers between devices  20.7 us (28%)
  between operations  0.82 us (1%)
  other arithmetic  0.81 us (1%)
    ppermute x11, waiting for transfers between devices, swap(): lax.ppermute(block, 'view', [(at, at ^ 1 << bit) for at in range(count)])  20.7 us
    pallas_call x2, Pallas kernels, shade(): pl.pallas_call(functools.partial(shade_kernel, ratio, knots, low, tiles *...  15.3 us
    ppermute x11, starting transfers between devices, swap(): lax.ppermute(block, 'view', [(at, at ^ 1 << bit) for at in range(count)])  13 us
    ppermute x3, starting transfers between devices, from_earlier(): lax.ppermute(leaving, 'light', [(at, at + apart) for at in range(count -...  9.17 us
    pallas_call x1, Pallas kernels, sums(): pl.pallas_call(functools.partial(sums_kernel, sigma_scale, ratio, bits, s...  7.15 us
    pallas_call x1, Pallas kernels, unlit(): pl.pallas_call(functools.partial(unlit_kernel, ratio, knots, low, len(aft...  3.85 us
    pallas_call x1, Pallas kernels, lit(): pl.pallas_call(functools.partial(lit_kernel, low, total, bits, pieces, le...  1.69 us
  transfers between devices with their start and end apart: 14, of which 7 were waited for; matrix products, arithmetic and copies ran while one was open for 0% of the time, Pallas kernels for 29%

profile of v2, /device:TPU:0, one launch (start us, length us, event | category | flops | bytes accessed | tf_op | source)
XLA Modules:
  0.0 73.9 jit_solution(15677904113590494948)
XLA Ops:
  0.7 0.8 %select_reduce_fusion.table_ref = f32[4,16]{1,0:T(4,128)S(1)} fusion(f32[8,4,16]{2,1,0:T(4,128)} %param.6, pred[8]{0:T(512)(128)(4,1)S(1)} %iota_compare_fusion), kind=kLoop, calls=%fused_computation | loop fusion | flops 960 | bytes 2312 | tf_op jit(solution)/shard_map/reduce_sum | solution.py:559
  1.5 7.2 %sums.1 = (f32[8,4096]{1,0:T(8,128)S(1)}, f32[32,8,64,128]{3,2,1,0:T(8,128)S(1)}, f32[16,8,128]{2,1,0:T(8,128)S(1)}, f32[4,32,8,128]{3,2,1,0:T(8,128)S(1)}, f32[4,32,8,128]{3,2,1,0:T(8,128)S(1)}) custom-call(f32[4,16]{1,0:T(4,128)S(1)} %select_reduce_fusion.table_ref, f32[8,64,4096]{2,1,0:T(8,128)} %density_ref.1), custom_call_target="tpu_custom_call" | custom-call | flops 8388608000 | bytes 8388608 | tf_op jit(solution)/shard_map/sums/pallas_call | solution.py:314
  8.6 0.5 collective-permute-start
  9.1 5.4 %collective-permute-start.3 = (f32[8,4096]{1,0:T(8,128)S(1)}, f32[8,4096]{1,0:T(8,128)S(1)}, u32[]{:S(2)}, u32[]{:S(2)}) collective-permute-start(f32[8,4096]{1,0:T(8,128)S(1)} %get-tuple-element.37), channel_id=1, source_target_pairs={{0,24},{1,25},{2,26},{3,27},{4,28},{5,29},{6,30},{7,31}} | collective-permute-start | bytes 393224 | tf_op jit(solution)/shard_map/ppermute | solution.py:513
  14.5 1.3 %collective-permute-start.2 = (f32[8,4096]{1,0:T(8,128)S(1)}, f32[8,4096]{1,0:T(8,128)S(1)}, u32[]{:S(2)}, u32[]{:S(2)}) collective-permute-start(f32[8,4096]{1,0:T(8,128)S(1)} %get-tuple-element.37), channel_id=1, source_target_pairs={{0,16},{8,24},{1,17},{9,25},{2,18},{10,26},{3,19},{11,27},{4,20},{... | collective-permute-start | bytes 393224 | tf_op jit(solution)/shard_map/ppermute | solution.py:513
  15.8 2.5 %collective-permute-start.1 = (f32[8,4096]{1,0:T(8,128)S(1)}, f32[8,4096]{1,0:T(8,128)S(1)}, u32[]{:S(2)}, u32[]{:S(2)}) collective-permute-start(f32[8,4096]{1,0:T(8,128)S(1)} %get-tuple-element.37), channel_id=1, source_target_pairs={{0,8},{8,16},{16,24},{1,9},{9,17},{17,25},{2,10},{10,18},{18,26},{... | collective-permute-start | bytes 393224 | tf_op jit(solution)/shard_map/ppermute | solution.py:513
  18.3 0.1 merge_clear.2
  18.4 1.6 %collective-permute-start.5 = (f32[2,32,8,128]{3,2,1,0:T(8,128)S(1)}, f32[2,32,8,128]{3,2,1,0:T(8,128)S(1)}, u32[]{:S(2)}, u32[]{:S(2)}) collective-permute-start(f32[2,32,8,128]{3,2,1,0:T(8,128)S(1)} %get-tuple-element.36.rest_0_), channel_id=1, source_target_pairs={{0,2},{1,3},{2,0},{3,1},{4,6},{5,7},{6,4},{7,5},{8,10},{9,11},{10,... | collective-permute-start | bytes 786440 | tf_op jit(solution)/shard_map/ppermute | solution.py:507
  20.0 3.9 %unlit.1.unlit_ref = f32[8,8,3,64,128]{4,3,2,1,0:T(8,128)S(1)} custom-call(f32[16,8,128]{2,1,0:T(8,128)S(1)} %get-tuple-element.32.coef, f32[32,8,64,128]{3,2,1,0:T(8,128)S(1)} %get-tuple-element.33.cells_ref, f32[2,32,8,128]{3,2,1,0:T(8,128)S(1)} %get-tuple-element.36.rest_0_), custom_call_target="tpu_custom_call" | custom-call | flops 5242880000 | bytes 2097152 | tf_op jit(solution)/shard_map/unlit/pallas_call | solution.py:355
  24.0 1.7 %lit.1 = (f32[4,3,8,8,128]{4,3,2,1,0:T(8,128)S(1)}, f32[4,3,8,8,128]{4,3,2,1,0:T(8,128)S(1)}) custom-call(s32[4]{0:T(128)S(1)} %copy-done.1, f32[4,3]{1,0:T(4,128)S(1)} %copy-done, f32[8,8,3,64,128]{4,3,2,1,0:T(8,128)S(1)} %unlit.1.unlit_ref, f32[8,4096]{1,0:T(8,128)S(1)} %collective-permute-done.1.rest_0_, f32[8,4096]{1,0:T(8,128)S(1)} %collective-permute-done.2.rest_1_, ...), custom_call_target="tpu_custom_call" | custom-call | tf_op jit(solution)/shard_map/lit/pallas_call | solution.py:370
  25.7 0.1 collective-permute-start.4
  25.7 0.9 %collective-permute-done.5.other_ref.other_clear_ref = f32[2,32,8,128]{3,2,1,0:T(8,128)S(1)} collective-permute-done((f32[2,32,8,128]{3,2,1,0:T(8,128)S(1)}, f32[2,32,8,128]{3,2,1,0:T(8,128)S(1)}, u32[]{:S(2)}, u32[]{:S(2)}) %collective-permute-start.5) | collective-permute-done | bytes 262176 | tf_op jit(solution)/shard_map/ppermute | solution.py:507
  26.6 0.8 %collective-permute-done.4.other_ref = f32[4,3,8,8,128]{4,3,2,1,0:T(8,128)S(1)} collective-permute-done((f32[4,3,8,8,128]{4,3,2,1,0:T(8,128)S(1)}, f32[4,3,8,8,128]{4,3,2,1,0:T(8,128)S(1)}, u32[]{:S(2)}, u32[]{:S(2)}) %collective-permute-start.4) | collective-permute-done | bytes 393248 | tf_op jit(solution)/shard_map/ppermute | solution.py:507
  27.4 0.1 merge.6
  27.5 0.9 %collective-permute-start.6 = (f32[2,3,8,8,128]{4,3,2,1,0:T(8,128)S(1)}, f32[2,3,8,8,128]{4,3,2,1,0:T(8,128)S(1)}, u32[]{:S(2)}, u32[]{:S(2)}) collective-permute-start(f32[2,3,8,8,128]{4,3,2,1,0:T(8,128)S(1)} %get-tuple-element.43.rest_3_), channel_id=1, source_target_pairs={{0,2},{1,3},{2,0},{3,1},{4,6},{5,7},{6,4},{7,5},{8,10},{9,11},{10,... | collective-permute-start | bytes 589832 | tf_op jit(solution)/shard_map/ppermute | solution.py:507
  28.4 8.8 %shade.2 = (f32[4,3,14,8,128]{4,3,2,1,0:T(8,128)S(1)}, f32[4,3,14,8,128]{4,3,2,1,0:T(8,128)S(1)}) custom-call(s32[4]{0:T(128)S(1)} %copy-done.1, f32[4,3]{1,0:T(4,128)S(1)} %copy-done, f32[16,8,128]{2,1,0:T(8,128)S(1)} %get-tuple-element.32.coef, f32[32,8,64,128]{3,2,1,0:T(8,128)S(1)} %get-tuple-element.33.cells_ref, ...), custom_call_target="tpu_custom_call" | custom-call | flops 9175040000 | bytes 3670016 | tf_op jit(solution)/shard_map/shade/pallas_call | solution.py:335
  37.1 0.1 collective-permute-start.7
  37.3 2.7 %collective-permute-start.9 = (f32[56,8,128]{2,1,0:T(8,128)S(1)}, f32[56,8,128]{2,1,0:T(8,128)S(1)}, u32[]{:S(2)}, u32[]{:S(2)}) collective-permute-start(f32[56,8,128]{2,1,0:T(8,128)S(1)} %get-tuple-element.47.rest_0_), channel_id=1, source_target_pairs={{0,4},{1,5},{2,6},{3,7},{4,0},{5,1},{6,2},{7,3},{8,12},{9,13},{10,... | collective-permute-start | bytes 688136 | tf_op jit(solution)/shard_map/ppermute | solution.py:507
  40.0 0.1 merge.8
  40.1 1.3 %collective-permute-start.8 = (f32[2,3,14,8,128]{4,3,2,1,0:T(8,128)S(1)}, f32[2,3,14,8,128]{4,3,2,1,0:T(8,128)S(1)}, u32[]{:S(2)}, u32[]{:S(2)}) collective-permute-start(f32[2,3,14,8,128]{4,3,2,1,0:T(8,128)S(1)} %get-tuple-element.49.rest_3_), channel_id=1, source_target_pairs={{0,2},{1,3},{2,0},{3,1},{4,6},{5,7},{6,4},{7,5},{8,10},{9,11},{10,... | collective-permute-start | bytes 1032200 | tf_op jit(solution)/shard_map/ppermute | solution.py:507
  41.4 6.6 %shade.3 = (f32[4,3,10,8,128]{4,3,2,1,0:T(8,128)S(1)}, f32[4,3,10,8,128]{4,3,2,1,0:T(8,128)S(1)}) custom-call(s32[4]{0:T(128)S(1)} %copy-done.1, f32[4,3]{1,0:T(4,128)S(1)} %copy-done, f32[16,8,128]{2,1,0:T(8,128)S(1)} %get-tuple-element.32.coef, f32[32,8,64,128]{3,2,1,0:T(8,128)S(1)} %get-tuple-element.33.cells_ref, ...), custom_call_target="tpu_custom_call" | custom-call | flops 6553600000 | bytes 2621440 | tf_op jit(solution)/shard_map/shade/pallas_call | solution.py:335
  47.9 0.1 collective-permute-start.10
  48.0 3.3 %collective-permute-done.9.rest_1_.refs_3_ = f32[56,8,128]{2,1,0:T(8,128)S(1)} collective-permute-done((f32[56,8,128]{2,1,0:T(8,128)S(1)}, f32[56,8,128]{2,1,0:T(8,128)S(1)}, u32[]{:S(2)}, u32[]{:S(2)}) %collective-permute-start.9) | collective-permute-done | bytes 229408 | tf_op jit(solution)/shard_map/ppermute | solution.py:507
  51.3 3.2 %collective-permute-done.8.other_ref = f32[2,3,14,8,128]{4,3,2,1,0:T(8,128)S(1)} collective-permute-done((f32[2,3,14,8,128]{4,3,2,1,0:T(8,128)S(1)}, f32[2,3,14,8,128]{4,3,2,1,0:T(8,128)S(1)}, u32[]{:S(2)}, u32[]{:S(2)}) %collective-permute-start.8) | collective-permute-done | bytes 344096 | tf_op jit(solution)/shard_map/ppermute | solution.py:507
  54.5 0.1 merge.10
  54.6 1.0 %collective-permute-start.11 = (f32[2,3,10,8,128]{4,3,2,1,0:T(8,128)S(1)}, f32[2,3,10,8,128]{4,3,2,1,0:T(8,128)S(1)}, u32[]{:S(2)}, u32[]{:S(2)}) collective-permute-start(f32[2,3,10,8,128]{4,3,2,1,0:T(8,128)S(1)} %get-tuple-element.55), channel_id=1, source_target_pairs={{0,2},{1,3},{2,0},{3,1},{4,6},{5,7},{6,4},{7,5},{8,10},{9,11},{10,... | collective-permute-start | bytes 737288 | tf_op jit(solution)/shard_map/ppermute | solution.py:507
  55.6 2.7 %collective-permute-start.12 = (f32[1,3,14,8,128]{4,3,2,1,0:T(8,128)S(1)}, f32[1,3,14,8,128]{4,3,2,1,0:T(8,128)S(1)}, u32[]{:S(2)}, u32[]{:S(2)}) collective-permute-start(f32[1,3,14,8,128]{4,3,2,1,0:T(8,128)S(1)} %get-tuple-element.53.rest_0_), channel_id=1, source_target_pairs={{0,4},{1,5},{2,6},{3,7},{4,0},{5,1},{6,2},{7,3},{8,12},{9,13},{10,... | collective-permute-start | bytes 516104 | tf_op jit(solution)/shard_map/ppermute | solution.py:507
  58.2 6.1 %collective-permute-done.12.rest_0_.refs_4_ = f32[1,3,14,8,128]{4,3,2,1,0:T(8,128)S(1)} collective-permute-done((f32[1,3,14,8,128]{4,3,2,1,0:T(8,128)S(1)}, f32[1,3,14,8,128]{4,3,2,1,0:T(8,128)S(1)}, u32[]{:S(2)}, u32[]{:S(2)}) %collective-permute-start.12) | collective-permute-done | bytes 172064 | tf_op jit(solution)/shard_map/ppermute | solution.py:507
  64.3 1.3 %collective-permute-done.11.other_ref = f32[2,3,10,8,128]{4,3,2,1,0:T(8,128)S(1)} collective-permute-done((f32[2,3,10,8,128]{4,3,2,1,0:T(8,128)S(1)}, f32[2,3,10,8,128]{4,3,2,1,0:T(8,128)S(1)}, u32[]{:S(2)}, u32[]{:S(2)}) %collective-permute-start.11) | collective-permute-done | bytes 245792 | tf_op jit(solution)/shard_map/ppermute | solution.py:507
  65.6 2.2 %collective-permute-start.13 = (f32[1,3,10,8,128]{4,3,2,1,0:T(8,128)S(1)}, f32[1,3,10,8,128]{4,3,2,1,0:T(8,128)S(1)}, u32[]{:S(2)}, u32[]{:S(2)}) collective-permute-start(f32[1,3,10,8,128]{4,3,2,1,0:T(8,128)S(1)} %get-tuple-element.57), channel_id=1, source_target_pairs={{0,4},{1,5},{2,6},{3,7},{4,0},{5,1},{6,2},{7,3},{8,12},{9,13},{10,... | collective-permute-start | bytes 368648 | tf_op jit(solution)/shard_map/ppermute | solution.py:507
  67.8 5.2 %collective-permute-done.13.refs_5_ = f32[1,3,10,8,128]{4,3,2,1,0:T(8,128)S(1)} collective-permute-done((f32[1,3,10,8,128]{4,3,2,1,0:T(8,128)S(1)}, f32[1,3,10,8,128]{4,3,2,1,0:T(8,128)S(1)}, u32[]{:S(2)}, u32[]{:S(2)}) %collective-permute-start.13) | collective-permute-done | bytes 122912 | tf_op jit(solution)/shard_map/ppermute | solution.py:507
  73.0 0.9 %last.1 = f32[4,8,4096]{2,1,0:T(8,128)} custom-call(f32[1,3,8,8,128]{4,3,2,1,0:T(8,128)S(1)} %get-tuple-element.45.refs_0_, f32[1,3,14,8,128]{4,3,2,1,0:T(8,128)S(1)} %get-tuple-element.51.refs_1_, f32[1,3,10,8,128]{4,3,2,1,0:T(8,128)S(1)} %get-tuple-element.56.refs_2_, f32[56,8,128]{2,1,0:T(8,128)S(1)} %collective-permute-done.9.rest_1_.refs_3_, ...), custom_call_target="tpu_custom_call" | custom-call | tf_op jit(solution)/shard_map/last/pallas_call | solution.py:495
  (16 shorter events, 0.2 us)
Async XLA Ops:
  8.6 9.7 %collective-permute-start = (f32[4,32,8,128]{3,2,1,0:T(8,128)S(1)}, f32[4,32,8,128]{3,2,1,0:T(8,128)S(1)}, u32[]{:S(2)}, u32[]{:S(2)}) collective-permute-start(f32[4,32,8,128]{3,2,1,0:T(8,128)S(1)} %get-tuple-element.35), channel_id=1, source_target_pairs={{0,1},{1,0},{2,3},{3,2},{4,5},{5,4},{6,7},{7,6},{8,9},{9,8},{10,11... | collective-permute-start | bytes 1572872 | tf_op jit(solution)/shard_map/ppermute | solution.py:507
  9.1 14.8 %collective-permute-start.3 = (f32[8,4096]{1,0:T(8,128)S(1)}, f32[8,4096]{1,0:T(8,128)S(1)}, u32[]{:S(2)}, u32[]{:S(2)}) collective-permute-start(f32[8,4096]{1,0:T(8,128)S(1)} %get-tuple-element.37), channel_id=1, source_target_pairs={{0,24},{1,25},{2,26},{3,27},{4,28},{5,29},{6,30},{7,31}} | collective-permute-start | bytes 393224 | tf_op jit(solution)/shard_map/ppermute | solution.py:513
  14.5 9.4 %collective-permute-start.2 = (f32[8,4096]{1,0:T(8,128)S(1)}, f32[8,4096]{1,0:T(8,128)S(1)}, u32[]{:S(2)}, u32[]{:S(2)}) collective-permute-start(f32[8,4096]{1,0:T(8,128)S(1)} %get-tuple-element.37), channel_id=1, source_target_pairs={{0,16},{8,24},{1,17},{9,25},{2,18},{10,26},{3,19},{11,27},{4,20},{... | collective-permute-start | bytes 393224 | tf_op jit(solution)/shard_map/ppermute | solution.py:513
  15.8 8.1 %collective-permute-start.1 = (f32[8,4096]{1,0:T(8,128)S(1)}, f32[8,4096]{1,0:T(8,128)S(1)}, u32[]{:S(2)}, u32[]{:S(2)}) collective-permute-start(f32[8,4096]{1,0:T(8,128)S(1)} %get-tuple-element.37), channel_id=1, source_target_pairs={{0,8},{8,16},{16,24},{1,9},{9,17},{17,25},{2,10},{10,18},{18,26},{... | collective-permute-start | bytes 393224 | tf_op jit(solution)/shard_map/ppermute | solution.py:513
  18.4 8.2 %collective-permute-start.5 = (f32[2,32,8,128]{3,2,1,0:T(8,128)S(1)}, f32[2,32,8,128]{3,2,1,0:T(8,128)S(1)}, u32[]{:S(2)}, u32[]{:S(2)}) collective-permute-start(f32[2,32,8,128]{3,2,1,0:T(8,128)S(1)} %get-tuple-element.36.rest_0_), channel_id=1, source_target_pairs={{0,2},{1,3},{2,0},{3,1},{4,6},{5,7},{6,4},{7,5},{8,10},{9,11},{10,... | collective-permute-start | bytes 786440 | tf_op jit(solution)/shard_map/ppermute | solution.py:507
  20.0 3.9 %copy-start = (f32[4,3]{1,0:T(4,128)S(1)}, f32[4,3]{1,0:T(4,128)}, u32[]{:S(2)}) copy-start(f32[4,3]{1,0:T(4,128)} %tint_ref.5) | copy-start | bytes 148
  20.0 3.9 %copy-start.1 = (s32[4]{0:T(128)S(1)}, s32[4]{0:T(128)}, u32[]{:S(2)}) copy-start(s32[4]{0:T(128)} %code_ref.5) | copy-start | bytes 52
  25.7 1.8 %collective-permute-start.4 = (f32[4,3,8,8,128]{4,3,2,1,0:T(8,128)S(1)}, f32[4,3,8,8,128]{4,3,2,1,0:T(8,128)S(1)}, u32[]{:S(2)}, u32[]{:S(2)}) collective-permute-start(f32[4,3,8,8,128]{4,3,2,1,0:T(8,128)S(1)} %get-tuple-element.39.rest_0_), channel_id=1, source_target_pairs={{0,1},{1,0},{2,3},{3,2},{4,5},{5,4},{6,7},{7,6},{8,9},{9,8},{10,11... | collective-permute-start | bytes 1179656 | tf_op jit(solution)/shard_map/ppermute | solution.py:507
  27.5 9.7 %collective-permute-start.6 = (f32[2,3,8,8,128]{4,3,2,1,0:T(8,128)S(1)}, f32[2,3,8,8,128]{4,3,2,1,0:T(8,128)S(1)}, u32[]{:S(2)}, u32[]{:S(2)}) collective-permute-start(f32[2,3,8,8,128]{4,3,2,1,0:T(8,128)S(1)} %get-tuple-element.43.rest_3_), channel_id=1, source_target_pairs={{0,2},{1,3},{2,0},{3,1},{4,6},{5,7},{6,4},{7,5},{8,10},{9,11},{10,... | collective-permute-start | bytes 589832 | tf_op jit(solution)/shard_map/ppermute | solution.py:507
  37.1 2.8 %collective-permute-start.7 = (f32[4,3,14,8,128]{4,3,2,1,0:T(8,128)S(1)}, f32[4,3,14,8,128]{4,3,2,1,0:T(8,128)S(1)}, u32[]{:S(2)}, u32[]{:S(2)}) collective-permute-start(f32[4,3,14,8,128]{4,3,2,1,0:T(8,128)S(1)} %get-tuple-element.44.rest_1_), channel_id=1, source_target_pairs={{0,1},{1,0},{2,3},{3,2},{4,5},{5,4},{6,7},{7,6},{8,9},{9,8},{10,11... | collective-permute-start | bytes 2064392 | tf_op jit(solution)/shard_map/ppermute | solution.py:507
  37.3 14.0 %collective-permute-start.9 = (f32[56,8,128]{2,1,0:T(8,128)S(1)}, f32[56,8,128]{2,1,0:T(8,128)S(1)}, u32[]{:S(2)}, u32[]{:S(2)}) collective-permute-start(f32[56,8,128]{2,1,0:T(8,128)S(1)} %get-tuple-element.47.rest_0_), channel_id=1, source_target_pairs={{0,4},{1,5},{2,6},{3,7},{4,0},{5,1},{6,2},{7,3},{8,12},{9,13},{10,... | collective-permute-start | bytes 688136 | tf_op jit(solution)/shard_map/ppermute | solution.py:507
  40.1 14.4 %collective-permute-start.8 = (f32[2,3,14,8,128]{4,3,2,1,0:T(8,128)S(1)}, f32[2,3,14,8,128]{4,3,2,1,0:T(8,128)S(1)}, u32[]{:S(2)}, u32[]{:S(2)}) collective-permute-start(f32[2,3,14,8,128]{4,3,2,1,0:T(8,128)S(1)} %get-tuple-element.49.rest_3_), channel_id=1, source_target_pairs={{0,2},{1,3},{2,0},{3,1},{4,6},{5,7},{6,4},{7,5},{8,10},{9,11},{10,... | collective-permute-start | bytes 1032200 | tf_op jit(solution)/shard_map/ppermute | solution.py:507
  47.9 6.6 %collective-permute-start.10 = (f32[4,3,10,8,128]{4,3,2,1,0:T(8,128)S(1)}, f32[4,3,10,8,128]{4,3,2,1,0:T(8,128)S(1)}, u32[]{:S(2)}, u32[]{:S(2)}) collective-permute-start(f32[4,3,10,8,128]{4,3,2,1,0:T(8,128)S(1)} %get-tuple-element.50.rest_0_), channel_id=1, source_target_pairs={{0,1},{1,0},{2,3},{3,2},{4,5},{5,4},{6,7},{7,6},{8,9},{9,8},{10,11... | collective-permute-start | bytes 1474568 | tf_op jit(solution)/shard_map/ppermute | solution.py:507
  54.6 11.0 %collective-permute-start.11 = (f32[2,3,10,8,128]{4,3,2,1,0:T(8,128)S(1)}, f32[2,3,10,8,128]{4,3,2,1,0:T(8,128)S(1)}, u32[]{:S(2)}, u32[]{:S(2)}) collective-permute-start(f32[2,3,10,8,128]{4,3,2,1,0:T(8,128)S(1)} %get-tuple-element.55), channel_id=1, source_target_pairs={{0,2},{1,3},{2,0},{3,1},{4,6},{5,7},{6,4},{7,5},{8,10},{9,11},{10,... | collective-permute-start | bytes 737288 | tf_op jit(solution)/shard_map/ppermute | solution.py:507
  55.6 8.7 %collective-permute-start.12 = (f32[1,3,14,8,128]{4,3,2,1,0:T(8,128)S(1)}, f32[1,3,14,8,128]{4,3,2,1,0:T(8,128)S(1)}, u32[]{:S(2)}, u32[]{:S(2)}) collective-permute-start(f32[1,3,14,8,128]{4,3,2,1,0:T(8,128)S(1)} %get-tuple-element.53.rest_0_), channel_id=1, source_target_pairs={{0,4},{1,5},{2,6},{3,7},{4,0},{5,1},{6,2},{7,3},{8,12},{9,13},{10,... | collective-permute-start | bytes 516104 | tf_op jit(solution)/shard_map/ppermute | solution.py:507
  65.6 7.4 %collective-permute-start.13 = (f32[1,3,10,8,128]{4,3,2,1,0:T(8,128)S(1)}, f32[1,3,10,8,128]{4,3,2,1,0:T(8,128)S(1)}, u32[]{:S(2)}, u32[]{:S(2)}) collective-permute-start(f32[1,3,10,8,128]{4,3,2,1,0:T(8,128)S(1)} %get-tuple-element.57), channel_id=1, source_target_pairs={{0,4},{1,5},{2,6},{3,7},{4,0},{5,1},{6,2},{7,3},{8,12},{9,13},{10,... | collective-permute-start | bytes 368648 | tf_op jit(solution)/shard_map/ppermute | solution.py:507

commit v3 on v2

--- a/solution.py
+++ b/solution.py
@@ -1,8 +1,8 @@
 import functools
-import math
 
 import jax
 import jax.numpy as jnp
+import numpy as np
 from jax import lax
 from jax.experimental import pallas as pl
 from jax.experimental.pallas import tpu as pltpu
@@ -11,8 +11,8 @@
 LANE = 128
 SUB = 8
 DRIFTS = (-1, 0, 1)
-VMEM_LIMIT = 24 * 2**20
-STREAM_LIMIT = 44 * 2**20
+VMEM_LIMIT = 16 * 2**20
+STREAM_LIMIT = 36 * 2**20
 F32 = jnp.float32
 
 
@@ -49,9 +49,19 @@
         coef[4 * q + 3] = step[SUB:]
 
 
+def threshold_of(knots):
+    edge = np.float32(SUB / (knots - 1.0))
+    scale = np.float32(knots - 1.0)
+    while edge * scale >= SUB:
+        edge = np.nextafter(edge, np.float32(0.0))
+    while edge * scale < SUB:
+        edge = np.nextafter(edge, np.float32(1.0))
+    return float(edge)
+
+
 def place_of(cells, knots):
     knot = (cells * (knots - 1.0)).astype(jnp.int32)
-    return knot & (SUB - 1), knot >= SUB
+    return knot & (SUB - 1), cells >= threshold_of(knots)
 
 
 def value_at(table, place, cells):
@@ -72,9 +82,9 @@
 
 def sums_kernel(sigma_scale, ratio, bits, split, table_ref, density_ref, *rest):
     if split:
-        leaving_ref, cells_ref, coef, send_ref, keep_ref, clear, sems = rest
+        leaving_ref, cells_ref, sigma_ref, coef, send_ref, keep_ref, clear, sems = rest
     else:
-        leaving_ref, cells_ref, coef, sems = rest
+        leaving_ref, cells_ref, sigma_ref, coef, sems = rest
     tiles, layers, slices, _ = cells_ref.shape
     knots = table_ref.shape[1]
 
@@ -94,15 +104,18 @@
         for block in range(slices // SUB):
             through = jnp.zeros((SUB, LANE), F32)
             for b in range(layers):
-                cells = cells_ref[tile, b, block * SUB : block * SUB + SUB]
-                sigma = value_at(table, place_of(cells, knots), cells)
+                rows = slice(block * SUB, block * SUB + SUB)
+                cells = cells_ref[tile, b, rows]
+                place = place_of(cells, knots)
+                sigma = value_at(table, place, cells)
+                sigma_ref[tile, b, rows] = sigma
                 through = through + sigma
                 down[b] = down[b] + sigma
             if split:
-                clear[block] = jnp.exp2(through)
+                clear[block] = jnp.exp(through)
         columns = pl.ds(pl.multiple_of(tile * LANE, LANE), LANE)
         for b in range(layers):
-            leaving_ref[b : b + 1, columns] = jnp.exp2(
+            leaving_ref[b : b + 1, columns] = jnp.exp(
                 jnp.sum(down[b], axis=0, keepdims=True) * ratio
             )
         if split:
@@ -152,16 +165,17 @@
         lighting[k] = shade[:, LANE : LANE + width]
 
 
-def weights_of(coef, cells_ref, tile, b, ahead, ratio, knots):
+def weights_of(cell_refs, tile, b, ahead, ratio, knots):
     steps = len(ahead)
     sublane = lax.broadcasted_iota(jnp.int32, (SUB, LANE), 0)
-    table = table_of(coef, 0)
+    cells_ref, sigma_ref = cell_refs
     cells, places, sigma = [], [], []
     before, running = [], None
     for j in range(steps):
-        cells.append(cells_ref[tile, b, pl.ds(j, SUB, stride=steps), :])
+        rows = pl.ds(j, SUB, stride=steps)
+        cells.append(cells_ref[tile, b, rows, :])
         places.append(place_of(cells[j], knots))
-        sigma.append(value_at(table, places[j], cells[j]))
+        sigma.append(sigma_ref[tile, b, rows, :])
         before.append(running)
         running = sigma[j] if running is None else running + sigma[j]
     earlier = running
@@ -171,8 +185,8 @@
     weights = []
     for j in range(steps):
         inside = earlier if j == 0 else earlier + before[j]
-        shadow = jnp.exp2(inside * ratio)
-        passed = jnp.exp2(sigma[j])
+        shadow = jnp.exp(inside * ratio)
+        passed = jnp.exp(sigma[j])
         if ahead[j] is None:
             after = passed
             weights.append((1.0 - passed) * shadow)
@@ -194,15 +208,16 @@
 
 def shade_kernel(
     ratio, knots, first, total, bits, pieces, far, late, whole_out,
-    code_ref, tint_ref, coef, cells_ref, *rest,
+    code_ref, tint_ref, coef, *rest,
 ):
+    cell_refs, rest = rest[:2], rest[2:]
     brick_refs = [rest[at * len(pieces) : (at + 1) * len(pieces)] for at in range(far)]
     rest = rest[far * len(pieces) + late :]
     if whole_out:
         out_ref, lighting, sums = rest
     else:
         send_ref, keep_ref, lighting, sums = rest
-    layers, slices = cells_ref.shape[1:3]
+    layers, slices = cell_refs[0].shape[1:3]
     steps = slices // SUB
     channels = lighting.shape[0]
     fill_lighting(pieces, brick_refs, code_ref, tint_ref, lighting, first, total)
@@ -213,7 +228,7 @@
         ahead = [None] * steps
         for b in range(layers):
             cells, places, weights = weights_of(
-                coef, cells_ref, first // LANE + tile, b, ahead, ratio, knots
+                cell_refs, first // LANE + tile, b, ahead, ratio, knots
             )
             for k in range(channels):
                 lit = jnp.broadcast_to(lighting[k, b : b + 1, columns], (SUB, LANE))
@@ -238,8 +253,8 @@
             put_halves(send_ref, keep_ref, sums, tile, bits)
 
 
-def unlit_kernel(ratio, knots, first, late, coef, cells_ref, *rest):
-    out_ref = rest[late]
+def unlit_kernel(ratio, knots, first, late, coef, *rest):
+    cell_refs, out_ref = rest[:2], rest[2 + late]
     tiles, layers, channels, slices, _ = out_ref.shape
     steps = slices // SUB
 
@@ -248,7 +263,7 @@
         ahead = [None] * steps
         for b in range(layers):
             cells, places, weights = weights_of(
-                coef, cells_ref, first // LANE + tile, b, ahead, ratio, knots
+                cell_refs, first // LANE + tile, b, ahead, ratio, knots
             )
             for k in range(channels):
                 table = table_of(coef, k + 1)
@@ -302,6 +317,7 @@
     half = (1 << bits) // 2
     outs = [
         shape(layers, total),
+        shape(tiles, layers, slices, LANE),
         shape(tiles, layers, slices, LANE),
         shape(4 * table.shape[0], SUB, LANE),
     ]
@@ -324,7 +340,7 @@
 
 
 def shade(coef, cells, knots, code, tint, bricks, pieces, low, high, ratio, bits, whole_out, after=()):
-    tiles, layers, slices, _ = cells.shape
+    tiles, layers, slices, _ = cells[0].shape
     channels = tint.shape[1]
     half = (1 << bits) // 2
     if whole_out:
@@ -337,7 +353,7 @@
             shade_kernel, ratio, knots, low, tiles * LANE, bits, pieces, len(bricks), len(after),
             whole_out,
         ),
-        in_specs=[SMEM()] * 2 + [VMEM()] * (2 + len(operands)) + [ANY()] * len(after),
+        in_specs=[SMEM()] * 2 + [VMEM()] * (3 + len(operands)) + [ANY()] * len(after),
         out_specs=[VMEM()] * len(outs),
         out_shape=outs,
         scratch_shapes=[
@@ -345,22 +361,22 @@
             pltpu.VMEM((channels + 1, slices, LANE), F32),
         ],
         compiler_params=params(),
-        cost_estimate=cost(cells, high - low, 10000),
+        cost_estimate=cost(cells[0], high - low, 10000),
         name="shade",
-    )(code, tint, coef, cells, *operands, *after)
+    )(code, tint, coef, *cells, *operands, *after)
 
 
 def unlit(coef, cells, knots, channels, low, high, ratio, after=()):
-    layers, slices = cells.shape[1:3]
+    layers, slices = cells[0].shape[1:3]
     return pl.pallas_call(
         functools.partial(unlit_kernel, ratio, knots, low, len(after)),
-        in_specs=[VMEM()] * 2 + [ANY()] * len(after),
+        in_specs=[VMEM()] * 3 + [ANY()] * len(after),
         out_specs=VMEM(),
         out_shape=shape((high - low) // LANE, layers, channels, slices, LANE),
         compiler_params=params(),
-        cost_estimate=cost(cells, high - low, 10000),
+        cost_estimate=cost(cells[0], high - low, 10000),
         name="unlit",
-    )(coef, cells, *after)
+    )(coef, *cells, *after)
 
 
 def lit(cells, code, tint, bricks, pieces, low, high, total, bits, after=()):
@@ -406,81 +422,76 @@
     )(own, other, *after)
 
 
-def merge_kernel(bit, start, joined, own_ref, other_ref, own_clear_ref, other_clear_ref, *rest):
+def merge_kernel(bit, start, parts, *refs):
+    owns, others = refs[:parts], refs[parts : 2 * parts]
+    own_clear_ref, other_clear_ref, *rest = refs[2 * parts :]
     send_ref, keep_ref = rest[-2:]
-    half, channels, count = keep_ref.shape[:3]
-    tiles = pl.ds(start, count)
+    half, channels = keep_ref.shape[:2]
     me = lax.axis_index("view")
     mine = me >> bit + 1 & 1
 
-    def merged(front_ref, back_ref, clear_ref):
-        for at in range(half):
-            for to_ref, side in ((send_ref, 1 - mine), (keep_ref, mine)):
-                source = side * half + at
-                clear = clear_ref[source, tiles]
-                for k in range(channels):
-                    value = front_ref[source, k] + clear * back_ref[source, k]
-                    if joined and to_ref is send_ref:
-                        send_ref[k * count : (k + 1) * count] = value
-                    else:
-                        to_ref[at, k] = value
+    def merged(fronts, backs, clear_ref):
+        offset = 0
+        for front_ref, back_ref in zip(fronts, backs):
+            count = front_ref.shape[2]
+            tiles, to = pl.ds(start + offset, count), pl.ds(offset, count)
+            for at in range(half):
+                for to_ref, side in ((send_ref, 1 - mine), (keep_ref, mine)):
+                    source = side * half + at
+                    clear = clear_ref[source, tiles]
+                    for k in range(channels):
+                        value = front_ref[source, k] + clear * back_ref[source, k]
+                        to_ref[at, k, to] = value
+            offset += count
 
     upper = me >> bit & 1 == 1
 
     @pl.when(upper)
     def _():
-        merged(other_ref, own_ref, other_clear_ref)
+        merged(others, owns, other_clear_ref)
 
     @pl.when(jnp.logical_not(upper))
     def _():
-        merged(own_ref, other_ref, own_clear_ref)
-
-    if joined:
-        send_ref[channels * count :] = rest[0][0]
-
-
-def merge(own, other, own_clear, other_clear, bit, low, joined=(), after=()):
-    count, channels, tiles = own.shape[:3]
-    half = shape(count // 2, *own.shape[1:])
+        merged(owns, others, own_clear_ref)
+
+
+def merge(owns, others, own_clear, other_clear, bit, low, after=()):
+    count, channels = owns[0].shape[:2]
+    tiles = sum(own.shape[2] for own in owns)
+    half = shape(count // 2, channels, tiles, SUB, LANE)
     outs = [half] * 2
-    if joined:
-        outs = [shape(channels * tiles + joined[0].shape[1], SUB, LANE), half]
     return pl.pallas_call(
-        functools.partial(merge_kernel, bit, low // LANE, bool(joined)),
-        in_specs=[VMEM()] * (4 + len(joined)) + [ANY()] * len(after),
+        functools.partial(merge_kernel, bit, low // LANE, len(owns)),
+        in_specs=[VMEM()] * (2 * len(owns) + 2) + [ANY()] * len(after),
         out_specs=[VMEM()] * len(outs),
         out_shape=outs,
         compiler_params=params(),
         cost_estimate=MERGE_COST,
         name="merge",
-    )(own, other, own_clear, other_clear, *joined, *after)
+    )(*owns, *others, own_clear, other_clear, *after)
 
 
 def last_kernel(bit, firsts, *refs):
     chunks = len(firsts)
     owns, others = refs[:chunks], refs[chunks : 2 * chunks]
-    own_clear_ref, image_ref = refs[2 * chunks :]
-    channels, joined_tiles = owns[0].shape[1:3]
+    own_clear_ref, other_clear_ref, image_ref = refs[2 * chunks :]
+    channels = owns[0].shape[1]
     upper = lax.axis_index("view") >> bit & 1 == 1
-
-    def other_clear(tile):
-        return others[0][channels * joined_tiles + tile]
 
     def merged(swapped):
         for at, first in enumerate(firsts):
             for tile in range(owns[at].shape[2]):
                 columns = slice(first + tile * LANE, first + tile * LANE + LANE)
                 whole = first // LANE + tile
-                clear = other_clear(whole) if swapped else own_clear_ref[0, whole]
+                clear = (other_clear_ref if swapped else own_clear_ref)[0, whole]
                 for k in range(channels):
-                    own = owns[at][0, k, tile]
-                    other = others[at][k * joined_tiles + tile] if at == 0 else others[at][0, k, tile]
+                    own, other = owns[at][0, k, tile], others[at][0, k, tile]
                     front, back = (other, own) if swapped else (own, other)
                     image_ref[k, :, columns] = front + clear * back
 
     for tile in range(own_clear_ref.shape[1]):
         columns = slice(tile * LANE, tile * LANE + LANE)
-        image_ref[channels, :, columns] = own_clear_ref[0, tile] * other_clear(tile)
+        image_ref[channels, :, columns] = own_clear_ref[0, tile] * other_clear_ref[0, tile]
 
     @pl.when(upper)
     def _():
@@ -491,15 +502,15 @@
         merged(False)
 
 
-def last(owns, others, own_clear, bit, firsts, total):
+def last(owns, others, own_clear, other_clear, bit, firsts, total):
     return pl.pallas_call(
         functools.partial(last_kernel, bit, firsts),
-        in_specs=[VMEM()] * (2 * len(owns) + 1),
+        in_specs=[VMEM()] * (2 * len(owns) + 2),
         out_specs=VMEM(),
         out_shape=shape(owns[0].shape[1] + 1, SUB, total),
         compiler_params=params(),
         name="last",
-    )(*owns, *others, own_clear)
+    )(*owns, *others, own_clear, other_clear)
 
 
 def swap(block, bit):
@@ -522,7 +533,7 @@
 
 def plain(density, table, light_code, light_tint, sigma_scale, ratio, bits):
     slices, total = density.shape[1:]
-    leaving, cells, coef = sums(density, table, sigma_scale, ratio, 0, False)
+    leaving, *cells, coef = sums(density, table, sigma_scale, ratio, 0, False)
     bricks = [[row] for row in from_earlier(leaving)]
     parts = shade(
         coef, cells, table.shape[1], light_code, light_tint, bricks, [(0, total)], 0, total, ratio,
@@ -541,64 +552,76 @@
     return current.reshape(depth, rows, total)
 
 
-CUTS = (0.25, 0.6875)
-
-
-def ranges(cuts, total):
-    ends = [0] + [round(total * cut / LANE) * LANE for cut in cuts] + [total]
-    return list(zip(ends[:-1], ends[1:]))
+PARTS = ((11,), (12,), (9,))
+
+
+def ranges(total):
+    whole = sum(sum(parts) for parts in PARTS)
+    result, done = [], 0
+    for parts in PARTS:
+        result.append([])
+        for part in parts:
+            low = total * done // (whole * LANE) * LANE
+            done += part
+            result[-1].append((low, total * done // (whole * LANE) * LANE))
+    return result
 
 
 def local(density, tables, table_index, light_code, light_tint):
     layers, slices, total = density.shape
     views = lax.axis_size("view")
     bits = views.bit_length() - 1
-    sigma_scale = -math.log2(math.e) / (layers * views)
+    sigma_scale = -1.0 / (layers * views)
     ratio = layers * views / (slices * lax.axis_size("light"))
-    chosen = jnp.arange(tables.shape[0], dtype=jnp.int32) == table_index[0, 0]
-    table = jnp.sum(jnp.where(chosen[:, None, None], tables, 0.0), axis=0)
+    chosen = lax.broadcasted_iota(jnp.int32, (tables.shape[0], 1), 0) == table_index
+    table = jnp.sum(jnp.where(chosen[:, :, None], tables, 0.0), axis=0)
     if views * SUB != slices or bits != 3:
         return plain(density, table, light_code, light_tint, sigma_scale, ratio, bits)
     pieces = [(0, total)]
-    chunks = ranges(CUTS, total)
+    chunks = ranges(total)
     knots = table.shape[1]
-    leaving, cells, coef, send, keep = sums(
+    leaving, *cells, coef, send, keep = sums(
         density, table, sigma_scale, ratio, bits, True
     )
     bricks = [[row] for row in from_earlier(leaving)]
     clear = [(keep, swap(send, 0))]
     send, keep = merge_clear(*clear[0], 0)
     clear.append((keep, swap(send, 1)))
-    first = unlit(coef, cells, knots, light_tint.shape[1], *chunks[0], ratio, after=(send,))
-    state = [lit(first, light_code, light_tint, bricks, pieces, *chunks[0], total, bits)]
-    clear_send, own_clear = merge_clear(*clear[1], 1, after=(state[0][0],))
+    first = unlit(coef, cells, knots, light_tint.shape[1], *chunks[0][0], ratio, after=(send,))
+    done = lit(first, light_code, light_tint, bricks, pieces, *chunks[0][0], total, bits)
+    halves = [(done[1], swap(done[0], 0))]
+    clear_send, own_clear = merge_clear(*clear[1], 1, after=(done[0],))
+    clear.append((own_clear, swap(clear_send, 2)))
     done = clear_send
-    for at, (low, high) in enumerate(chunks):
-        if at:
-            state.append(
-                shade(
+    state = []
+
+    def forward(after):
+        at = len(state) - 1
+        settled = state[at - 1][1] if at else clear[2][1]
+        send, keep = merge(
+            [state[at][0]], [state[at][1]], *clear[1], 1, chunks[at][0][0], after=(after, settled)
+        )
+        state[at] = (keep, swap(send, 2))
+        return send
+
+    for at, parts in enumerate(chunks):
+        for number, (low, high) in enumerate(parts):
+            if at:
+                send, keep = shade(
                     coef, cells, knots, light_code, light_tint, bricks, pieces, low, high, ratio,
                     bits, False, after=(done,),
                 )
-            )
-            done = state[at][0]
-        send, keep = state[at]
-        arrived = swap(send, 0)
-        if at:
-            settled = (done,) if at == 1 else (done, state[at - 2][1])
-            late = merge(
-                *state[at - 1], *clear[1], 1, chunks[at - 1][0],
-                joined=(clear_send,) if at == 1 else (), after=settled,
-            )
-            state[at - 1] = (late[1], swap(late[0], 2))
-            done = late[0]
-        send, keep = merge(keep, arrived, *clear[0], 0, low, after=(done,))
+                halves.append((keep, swap(send, 0)))
+                done = send
+                if number == 0:
+                    done = forward(done)
+        send, keep = merge(*zip(*halves), *clear[0], 0, parts[0][0], after=(done,))
+        halves = []
         done = send
-        state[at] = (keep, swap(send, 1))
-    late = merge(*state[-1], *clear[1], 1, chunks[-1][0], after=(state[-2][1],))
-    state[-1] = (late[1], swap(late[0], 2))
+        state.append((keep, swap(send, 1)))
+    forward(done)
     owns, others = zip(*state)
-    return last(owns, others, own_clear, 2, [low for low, _ in chunks], total)
+    return last(owns, others, *clear[2], 2, [parts[0][0] for parts in chunks], total)
 
 
 def solution(mesh):

time: 74.2 us -> 68.6 us (0.925)
  waiting for transfers between devices: 20.7 us -> 17.4 us
  Pallas kernels: 29.4 us -> 27.5 us
    ppermute x11 -> x12, waiting for transfers between devices: 20.7 us -> 17.4 us  [swap(): lax.ppermute(block, 'view', [(at, at ^ 1 << bit) for at in range(count)])]
    pallas_call x2, Pallas kernels: 15.3 us -> 12.4 us  [shade(): pl.pallas_call(functools.partial(shade_kernel, ratio, knots, low, tiles *...]
    pallas_call x1, Pallas kernels: 3.85 us -> 4.65 us  [unlit(): pl.pallas_call(functools.partial(unlit_kernel, ratio, knots, low, len(aft...]
    ppermute x11 -> x12, starting transfers between devices: 13 us -> 12.6 us  [swap(): lax.ppermute(block, 'view', [(at, at ^ 1 << bit) for at in range(count)])]
  transfers between devices with their start and end apart: 14 -> 15, of which waited for: 7 -> 6; matrix products, arithmetic and copies ran while one was open for 0% -> 0% of each run, Pallas kernels for 29% -> 28%
where the time goes in v3:
time: 68.6 us; the launch traced here: 68.3 us
  Pallas kernels  27.5 us (40%)
  starting transfers between devices  21.8 us (32%)
  waiting for transfers between devices  17.4 us (25%)
  between operations  0.85 us (1%)
  other arithmetic  0.81 us (1%)
    ppermute x12, waiting for transfers between devices, swap(): lax.ppermute(block, 'view', [(at, at ^ 1 << bit) for at in range(count)])  17.4 us
    ppermute x12, starting transfers between devices, swap(): lax.ppermute(block, 'view', [(at, at ^ 1 << bit) for at in range(count)])  12.6 us
    pallas_call x2, Pallas kernels, shade(): pl.pallas_call(functools.partial(shade_kernel, ratio, knots, low, tiles *...  12.4 us
    ppermute x3, starting transfers between devices, from_earlier(): lax.ppermute(leaving, 'light', [(at, at + apart) for at in range(count -...  9.15 us
    pallas_call x1, Pallas kernels, sums(): pl.pallas_call(functools.partial(sums_kernel, sigma_scale, ratio, bits, s...  7.17 us
    pallas_call x1, Pallas kernels, unlit(): pl.pallas_call(functools.partial(unlit_kernel, ratio, knots, low, len(aft...  4.65 us
    pallas_call x1, Pallas kernels, lit(): pl.pallas_call(functools.partial(lit_kernel, low, total, bits, pieces, le...  1.93 us
  transfers between devices with their start and end apart: 15, of which 6 were waited for; matrix products, arithmetic and copies ran while one was open for 0% of the time, Pallas kernels for 28%

profile of v3, /device:TPU:0, one launch (start us, length us, event | category | flops | bytes accessed | tf_op | source)
XLA Modules:
  0.0 68.3 jit_solution(7211946499388924424)
XLA Ops:
  0.7 0.8 %select_reduce_fusion.table_ref = f32[4,16]{1,0:T(4,128)S(1)} fusion(f32[8,4,16]{2,1,0:T(4,128)} %param.6, pred[8]{0:T(512)(128)(4,1)S(1)} %iota_compare_fusion), kind=kLoop, calls=%fused_computation | loop fusion | flops 960 | bytes 2312 | tf_op jit(solution)/shard_map/reduce_sum | solution.py:577
  1.5 7.2 %sums.1 = (f32[8,4096]{1,0:T(8,128)S(1)}, f32[32,8,64,128]{3,2,1,0:T(8,128)S(1)}, f32[32,8,64,128]{3,2,1,0:T(8,128)S(1)}, f32[16,8,128]{2,1,0:T(8,128)S(1)}, f32...) custom-call(f32[4,16]{1,0:T(4,128)S(1)} %select_reduce_fusion.table_ref, f32[8,64,4096]{2,1,0:T(8,128)} %density_ref.1), custom_call_target="tpu_custom_call" | custom-call | flops 8388608000 | bytes 8388608 | tf_op jit(solution)/shard_map/sums/pallas_call | solution.py:330
  8.6 0.5 collective-permute-start
  9.1 5.4 %collective-permute-start.3 = (f32[8,4096]{1,0:T(8,128)S(1)}, f32[8,4096]{1,0:T(8,128)S(1)}, u32[]{:S(2)}, u32[]{:S(2)}) collective-permute-start(f32[8,4096]{1,0:T(8,128)S(1)} %get-tuple-element.39), channel_id=1, source_target_pairs={{0,24},{1,25},{2,26},{3,27},{4,28},{5,29},{6,30},{7,31}} | collective-permute-start | bytes 393224 | tf_op jit(solution)/shard_map/ppermute | solution.py:524
  14.5 1.3 %collective-permute-start.2 = (f32[8,4096]{1,0:T(8,128)S(1)}, f32[8,4096]{1,0:T(8,128)S(1)}, u32[]{:S(2)}, u32[]{:S(2)}) collective-permute-start(f32[8,4096]{1,0:T(8,128)S(1)} %get-tuple-element.39), channel_id=1, source_target_pairs={{0,16},{8,24},{1,17},{9,25},{2,18},{10,26},{3,19},{11,27},{4,20},{... | collective-permute-start | bytes 393224 | tf_op jit(solution)/shard_map/ppermute | solution.py:524
  15.8 2.5 %collective-permute-start.1 = (f32[8,4096]{1,0:T(8,128)S(1)}, f32[8,4096]{1,0:T(8,128)S(1)}, u32[]{:S(2)}, u32[]{:S(2)}) collective-permute-start(f32[8,4096]{1,0:T(8,128)S(1)} %get-tuple-element.39), channel_id=1, source_target_pairs={{0,8},{8,16},{16,24},{1,9},{9,17},{17,25},{2,10},{10,18},{18,26},{... | collective-permute-start | bytes 393224 | tf_op jit(solution)/shard_map/ppermute | solution.py:524
  18.3 0.1 merge_clear.2
  18.4 1.6 %collective-permute-start.5 = (f32[2,32,8,128]{3,2,1,0:T(8,128)S(1)}, f32[2,32,8,128]{3,2,1,0:T(8,128)S(1)}, u32[]{:S(2)}, u32[]{:S(2)}) collective-permute-start(f32[2,32,8,128]{3,2,1,0:T(8,128)S(1)} %get-tuple-element.38.rest_2_), channel_id=1, source_target_pairs={{0,2},{1,3},{2,0},{3,1},{4,6},{5,7},{6,4},{7,5},{8,10},{9,11},{10,... | collective-permute-start | bytes 786440 | tf_op jit(solution)/shard_map/ppermute | solution.py:518
  20.1 4.6 %unlit.1.unlit_ref = f32[11,8,3,64,128]{4,3,2,1,0:T(8,128)S(1)} custom-call(f32[16,8,128]{2,1,0:T(8,128)S(1)} %get-tuple-element.33.coef, f32[32,8,64,128]{3,2,1,0:T(8,128)S(1)} %get-tuple-element.34.rest_0_, f32[32,8,64,128]{3,2,1,0:T(8,128)S(1)} %get-tuple-element.35.rest_1_, f32[2,32,8,128]{3,2,1,0:T(8,128)S(1)} %get-tuple-element.38.rest_2_), custom_call_target="tpu_custom_call" | custom-call | flops 7208960000 | bytes 2883584 | tf_op jit(solution)/shard_map/unlit/pallas_call | solution.py:371
  24.8 1.9 %lit.1 = (f32[4,3,11,8,128]{4,3,2,1,0:T(8,128)S(1)}, f32[4,3,11,8,128]{4,3,2,1,0:T(8,128)S(1)}) custom-call(s32[4]{0:T(128)S(1)} %copy-done.1, f32[4,3]{1,0:T(4,128)S(1)} %copy-done, f32[11,8,3,64,128]{4,3,2,1,0:T(8,128)S(1)} %unlit.1.unlit_ref, f32[8,4096]{1,0:T(8,128)S(1)} %collective-permute-done.1.rest_0_.rest_2_, ...), custom_call_target="tpu_custom_call" | custom-call | tf_op jit(solution)/shard_map/lit/pallas_call | solution.py:386
  26.7 0.1 collective-permute-start.4
  26.8 2.7 %collective-permute-start.7 = (f32[1,32,8,128]{3,2,1,0:T(8,128)S(1)}, f32[1,32,8,128]{3,2,1,0:T(8,128)S(1)}, u32[]{:S(2)}, u32[]{:S(2)}) collective-permute-start(f32[1,32,8,128]{3,2,1,0:T(8,128)S(1)} %get-tuple-element.43.refs_4_), channel_id=1, source_target_pairs={{0,4},{1,5},{2,6},{3,7},{4,0},{5,1},{6,2},{7,3},{8,12},{9,13},{10,... | collective-permute-start | bytes 393224 | tf_op jit(solution)/shard_map/ppermute | solution.py:518
  29.5 0.1 merge.6
  29.6 1.5 %collective-permute-start.6 = (f32[2,3,11,8,128]{4,3,2,1,0:T(8,128)S(1)}, f32[2,3,11,8,128]{4,3,2,1,0:T(8,128)S(1)}, u32[]{:S(2)}, u32[]{:S(2)}) collective-permute-start(f32[2,3,11,8,128]{4,3,2,1,0:T(8,128)S(1)} %get-tuple-element.45.rest_5_), channel_id=1, source_target_pairs={{0,2},{1,3},{2,0},{3,1},{4,6},{5,7},{6,4},{7,5},{8,10},{9,11},{10,... | collective-permute-start | bytes 811016 | tf_op jit(solution)/shard_map/ppermute | solution.py:518
  31.0 7.0 %shade.2 = (f32[4,3,12,8,128]{4,3,2,1,0:T(8,128)S(1)}, f32[4,3,12,8,128]{4,3,2,1,0:T(8,128)S(1)}) custom-call(s32[4]{0:T(128)S(1)} %copy-done.1, f32[4,3]{1,0:T(4,128)S(1)} %copy-done, f32[16,8,128]{2,1,0:T(8,128)S(1)} %get-tuple-element.33.coef, f32[32,8,64,128]{3,2,1,0:T(8,128)S(1)} %get-tuple-element.34.rest_0_, ...), custom_call_target="tpu_custom_call" | custom-call | flops 7864320000 | bytes 3145728 | tf_op jit(solution)/shard_map/shade/pallas_call | solution.py:351
  38.0 0.1 collective-permute-start.8
  38.1 2.8 %collective-permute-done.6.refs_1_ = f32[2,3,11,8,128]{4,3,2,1,0:T(8,128)S(1)} collective-permute-done((f32[2,3,11,8,128]{4,3,2,1,0:T(8,128)S(1)}, f32[2,3,11,8,128]{4,3,2,1,0:T(8,128)S(1)}, u32[]{:S(2)}, u32[]{:S(2)}) %collective-permute-start.6) | collective-permute-done | bytes 270368 | tf_op jit(solution)/shard_map/ppermute | solution.py:518
  41.0 0.1 collective-permute-start.10
  41.1 0.1 merge.8
  41.2 1.6 %collective-permute-start.9 = (f32[2,3,12,8,128]{4,3,2,1,0:T(8,128)S(1)}, f32[2,3,12,8,128]{4,3,2,1,0:T(8,128)S(1)}, u32[]{:S(2)}, u32[]{:S(2)}) collective-permute-start(f32[2,3,12,8,128]{4,3,2,1,0:T(8,128)S(1)} %get-tuple-element.51.rest_5_), channel_id=1, source_target_pairs={{0,2},{1,3},{2,0},{3,1},{4,6},{5,7},{6,4},{7,5},{8,10},{9,11},{10,... | collective-permute-start | bytes 884744 | tf_op jit(solution)/shard_map/ppermute | solution.py:518
  42.8 5.5 %shade.3 = (f32[4,3,9,8,128]{4,3,2,1,0:T(8,128)S(1)}, f32[4,3,9,8,128]{4,3,2,1,0:T(8,128)S(1)}) custom-call(s32[4]{0:T(128)S(1)} %copy-done.1, f32[4,3]{1,0:T(4,128)S(1)} %copy-done, f32[16,8,128]{2,1,0:T(8,128)S(1)} %get-tuple-element.33.coef, f32[32,8,64,128]{3,2,1,0:T(8,128)S(1)} %get-tuple-element.34.rest_0_, ...), custom_call_target="tpu_custom_call" | custom-call | flops 5898240000 | bytes 2359296 | tf_op jit(solution)/shard_map/shade/pallas_call | solution.py:351
  48.2 0.1 collective-permute-start.11
  48.3 1.5 %collective-permute-done.10.refs_5_.refs_3_ = f32[1,3,11,8,128]{4,3,2,1,0:T(8,128)S(1)} collective-permute-done((f32[1,3,11,8,128]{4,3,2,1,0:T(8,128)S(1)}, f32[1,3,11,8,128]{4,3,2,1,0:T(8,128)S(1)}, u32[]{:S(2)}, u32[]{:S(2)}) %collective-permute-start.10) | collective-permute-done | bytes 135200 | tf_op jit(solution)/shard_map/ppermute | solution.py:518
  49.8 2.6 %collective-permute-done.9.refs_1_ = f32[2,3,12,8,128]{4,3,2,1,0:T(8,128)S(1)} collective-permute-done((f32[2,3,12,8,128]{4,3,2,1,0:T(8,128)S(1)}, f32[2,3,12,8,128]{4,3,2,1,0:T(8,128)S(1)}, u32[]{:S(2)}, u32[]{:S(2)}) %collective-permute-start.9) | collective-permute-done | bytes 294944 | tf_op jit(solution)/shard_map/ppermute | solution.py:518
  52.5 0.1 merge.10
  52.6 0.2 collective-permute-start.12
  52.8 3.0 %collective-permute-start.13 = (f32[1,3,12,8,128]{4,3,2,1,0:T(8,128)S(1)}, f32[1,3,12,8,128]{4,3,2,1,0:T(8,128)S(1)}, u32[]{:S(2)}, u32[]{:S(2)}) collective-permute-start(f32[1,3,12,8,128]{4,3,2,1,0:T(8,128)S(1)} %get-tuple-element.55.refs_4_), channel_id=1, source_target_pairs={{0,4},{1,5},{2,6},{3,7},{4,0},{5,1},{6,2},{7,3},{8,12},{9,13},{10,... | collective-permute-start | bytes 442376 | tf_op jit(solution)/shard_map/ppermute | solution.py:518
  55.8 4.6 %collective-permute-done.13.refs_5_.refs_4_ = f32[1,3,12,8,128]{4,3,2,1,0:T(8,128)S(1)} collective-permute-done((f32[1,3,12,8,128]{4,3,2,1,0:T(8,128)S(1)}, f32[1,3,12,8,128]{4,3,2,1,0:T(8,128)S(1)}, u32[]{:S(2)}, u32[]{:S(2)}) %collective-permute-start.13) | collective-permute-done | bytes 147488 | tf_op jit(solution)/shard_map/ppermute | solution.py:518
  60.4 1.3 %collective-permute-done.12.refs_1_ = f32[2,3,9,8,128]{4,3,2,1,0:T(8,128)S(1)} collective-permute-done((f32[2,3,9,8,128]{4,3,2,1,0:T(8,128)S(1)}, f32[2,3,9,8,128]{4,3,2,1,0:T(8,128)S(1)}, u32[]{:S(2)}, u32[]{:S(2)}) %collective-permute-start.12) | collective-permute-done | bytes 221216 | tf_op jit(solution)/shard_map/ppermute | solution.py:518
  61.7 1.3 %collective-permute-start.14 = (f32[1,3,9,8,128]{4,3,2,1,0:T(8,128)S(1)}, f32[1,3,9,8,128]{4,3,2,1,0:T(8,128)S(1)}, u32[]{:S(2)}, u32[]{:S(2)}) collective-permute-start(f32[1,3,9,8,128]{4,3,2,1,0:T(8,128)S(1)} %get-tuple-element.59), channel_id=1, source_target_pairs={{0,4},{1,5},{2,6},{3,7},{4,0},{5,1},{6,2},{7,3},{8,12},{9,13},{10,... | collective-permute-start | bytes 331784 | tf_op jit(solution)/shard_map/ppermute | solution.py:518
  63.0 4.5 %collective-permute-done.14.refs_5_ = f32[1,3,9,8,128]{4,3,2,1,0:T(8,128)S(1)} collective-permute-done((f32[1,3,9,8,128]{4,3,2,1,0:T(8,128)S(1)}, f32[1,3,9,8,128]{4,3,2,1,0:T(8,128)S(1)}, u32[]{:S(2)}, u32[]{:S(2)}) %collective-permute-start.14) | collective-permute-done | bytes 110624 | tf_op jit(solution)/shard_map/ppermute | solution.py:518
  67.5 0.9 %last.1 = f32[4,8,4096]{2,1,0:T(8,128)} custom-call(f32[1,3,11,8,128]{4,3,2,1,0:T(8,128)S(1)} %get-tuple-element.47.refs_0_, f32[1,3,12,8,128]{4,3,2,1,0:T(8,128)S(1)} %get-tuple-element.53.refs_1_, f32[1,3,9,8,128]{4,3,2,1,0:T(8,128)S(1)} %get-tuple-element.58.refs_2_, f32[1,3,11,8,128]{4,3,2,1,0:T(8,128)S(1)} %collective-permute-done.10.refs_5_.refs_3_, ...), custom_call_target="tpu_custom_call" | custom-call | tf_op jit(solution)/shard_map/last/pallas_call | solution.py:506
  (18 shorter events, 0.2 us)
Async XLA Ops:
  8.6 9.7 %collective-permute-start = (f32[4,32,8,128]{3,2,1,0:T(8,128)S(1)}, f32[4,32,8,128]{3,2,1,0:T(8,128)S(1)}, u32[]{:S(2)}, u32[]{:S(2)}) collective-permute-start(f32[4,32,8,128]{3,2,1,0:T(8,128)S(1)} %get-tuple-element.37), channel_id=1, source_target_pairs={{0,1},{1,0},{2,3},{3,2},{4,5},{5,4},{6,7},{7,6},{8,9},{9,8},{10,11... | collective-permute-start | bytes 1572872 | tf_op jit(solution)/shard_map/ppermute | solution.py:518
  9.1 15.6 %collective-permute-start.3 = (f32[8,4096]{1,0:T(8,128)S(1)}, f32[8,4096]{1,0:T(8,128)S(1)}, u32[]{:S(2)}, u32[]{:S(2)}) collective-permute-start(f32[8,4096]{1,0:T(8,128)S(1)} %get-tuple-element.39), channel_id=1, source_target_pairs={{0,24},{1,25},{2,26},{3,27},{4,28},{5,29},{6,30},{7,31}} | collective-permute-start | bytes 393224 | tf_op jit(solution)/shard_map/ppermute | solution.py:524
  14.5 10.2 %collective-permute-start.2 = (f32[8,4096]{1,0:T(8,128)S(1)}, f32[8,4096]{1,0:T(8,128)S(1)}, u32[]{:S(2)}, u32[]{:S(2)}) collective-permute-start(f32[8,4096]{1,0:T(8,128)S(1)} %get-tuple-element.39), channel_id=1, source_target_pairs={{0,16},{8,24},{1,17},{9,25},{2,18},{10,26},{3,19},{11,27},{4,20},{... | collective-permute-start | bytes 393224 | tf_op jit(solution)/shard_map/ppermute | solution.py:524
  15.8 8.9 %collective-permute-start.1 = (f32[8,4096]{1,0:T(8,128)S(1)}, f32[8,4096]{1,0:T(8,128)S(1)}, u32[]{:S(2)}, u32[]{:S(2)}) collective-permute-start(f32[8,4096]{1,0:T(8,128)S(1)} %get-tuple-element.39), channel_id=1, source_target_pairs={{0,8},{8,16},{16,24},{1,9},{9,17},{17,25},{2,10},{10,18},{18,26},{... | collective-permute-start | bytes 393224 | tf_op jit(solution)/shard_map/ppermute | solution.py:524
  18.4 8.4 %collective-permute-start.5 = (f32[2,32,8,128]{3,2,1,0:T(8,128)S(1)}, f32[2,32,8,128]{3,2,1,0:T(8,128)S(1)}, u32[]{:S(2)}, u32[]{:S(2)}) collective-permute-start(f32[2,32,8,128]{3,2,1,0:T(8,128)S(1)} %get-tuple-element.38.rest_2_), channel_id=1, source_target_pairs={{0,2},{1,3},{2,0},{3,1},{4,6},{5,7},{6,4},{7,5},{8,10},{9,11},{10,... | collective-permute-start | bytes 786440 | tf_op jit(solution)/shard_map/ppermute | solution.py:518
  20.1 4.7 %copy-start = (f32[4,3]{1,0:T(4,128)S(1)}, f32[4,3]{1,0:T(4,128)}, u32[]{:S(2)}) copy-start(f32[4,3]{1,0:T(4,128)} %tint_ref.5) | copy-start | bytes 148
  20.1 4.7 %copy-start.1 = (s32[4]{0:T(128)S(1)}, s32[4]{0:T(128)}, u32[]{:S(2)}) copy-start(s32[4]{0:T(128)} %code_ref.5) | copy-start | bytes 52
  26.7 2.8 %collective-permute-start.4 = (f32[4,3,11,8,128]{4,3,2,1,0:T(8,128)S(1)}, f32[4,3,11,8,128]{4,3,2,1,0:T(8,128)S(1)}, u32[]{:S(2)}, u32[]{:S(2)}) collective-permute-start(f32[4,3,11,8,128]{4,3,2,1,0:T(8,128)S(1)} %get-tuple-element.41.rest_0_), channel_id=1, source_target_pairs={{0,1},{1,0},{2,3},{3,2},{4,5},{5,4},{6,7},{7,6},{8,9},{9,8},{10,11... | collective-permute-start | bytes 1622024 | tf_op jit(solution)/shard_map/ppermute | solution.py:518
  26.8 11.3 %collective-permute-start.7 = (f32[1,32,8,128]{3,2,1,0:T(8,128)S(1)}, f32[1,32,8,128]{3,2,1,0:T(8,128)S(1)}, u32[]{:S(2)}, u32[]{:S(2)}) collective-permute-start(f32[1,32,8,128]{3,2,1,0:T(8,128)S(1)} %get-tuple-element.43.refs_4_), channel_id=1, source_target_pairs={{0,4},{1,5},{2,6},{3,7},{4,0},{5,1},{6,2},{7,3},{8,12},{9,13},{10,... | collective-permute-start | bytes 393224 | tf_op jit(solution)/shard_map/ppermute | solution.py:518
  29.6 11.4 %collective-permute-start.6 = (f32[2,3,11,8,128]{4,3,2,1,0:T(8,128)S(1)}, f32[2,3,11,8,128]{4,3,2,1,0:T(8,128)S(1)}, u32[]{:S(2)}, u32[]{:S(2)}) collective-permute-start(f32[2,3,11,8,128]{4,3,2,1,0:T(8,128)S(1)} %get-tuple-element.45.rest_5_), channel_id=1, source_target_pairs={{0,2},{1,3},{2,0},{3,1},{4,6},{5,7},{6,4},{7,5},{8,10},{9,11},{10,... | collective-permute-start | bytes 811016 | tf_op jit(solution)/shard_map/ppermute | solution.py:518
  38.0 3.1 %collective-permute-start.8 = (f32[4,3,12,8,128]{4,3,2,1,0:T(8,128)S(1)}, f32[4,3,12,8,128]{4,3,2,1,0:T(8,128)S(1)}, u32[]{:S(2)}, u32[]{:S(2)}) collective-permute-start(f32[4,3,12,8,128]{4,3,2,1,0:T(8,128)S(1)} %get-tuple-element.46.refs_4_), channel_id=1, source_target_pairs={{0,1},{1,0},{2,3},{3,2},{4,5},{5,4},{6,7},{7,6},{8,9},{9,8},{10,11... | collective-permute-start | bytes 1769480 | tf_op jit(solution)/shard_map/ppermute | solution.py:518
  41.0 8.8 %collective-permute-start.10 = (f32[1,3,11,8,128]{4,3,2,1,0:T(8,128)S(1)}, f32[1,3,11,8,128]{4,3,2,1,0:T(8,128)S(1)}, u32[]{:S(2)}, u32[]{:S(2)}) collective-permute-start(f32[1,3,11,8,128]{4,3,2,1,0:T(8,128)S(1)} %get-tuple-element.49.refs_4_), channel_id=1, source_target_pairs={{0,4},{1,5},{2,6},{3,7},{4,0},{5,1},{6,2},{7,3},{8,12},{9,13},{10,... | collective-permute-start | bytes 405512 | tf_op jit(solution)/shard_map/ppermute | solution.py:518
  41.2 11.2 %collective-permute-start.9 = (f32[2,3,12,8,128]{4,3,2,1,0:T(8,128)S(1)}, f32[2,3,12,8,128]{4,3,2,1,0:T(8,128)S(1)}, u32[]{:S(2)}, u32[]{:S(2)}) collective-permute-start(f32[2,3,12,8,128]{4,3,2,1,0:T(8,128)S(1)} %get-tuple-element.51.rest_5_), channel_id=1, source_target_pairs={{0,2},{1,3},{2,0},{3,1},{4,6},{5,7},{6,4},{7,5},{8,10},{9,11},{10,... | collective-permute-start | bytes 884744 | tf_op jit(solution)/shard_map/ppermute | solution.py:518
  48.2 4.2 %collective-permute-start.11 = (f32[4,3,9,8,128]{4,3,2,1,0:T(8,128)S(1)}, f32[4,3,9,8,128]{4,3,2,1,0:T(8,128)S(1)}, u32[]{:S(2)}, u32[]{:S(2)}) collective-permute-start(f32[4,3,9,8,128]{4,3,2,1,0:T(8,128)S(1)} %get-tuple-element.52.refs_4_), channel_id=1, source_target_pairs={{0,1},{1,0},{2,3},{3,2},{4,5},{5,4},{6,7},{7,6},{8,9},{9,8},{10,11... | collective-permute-start | bytes 1327112 | tf_op jit(solution)/shard_map/ppermute | solution.py:518
  52.6 9.1 %collective-permute-start.12 = (f32[2,3,9,8,128]{4,3,2,1,0:T(8,128)S(1)}, f32[2,3,9,8,128]{4,3,2,1,0:T(8,128)S(1)}, u32[]{:S(2)}, u32[]{:S(2)}) collective-permute-start(f32[2,3,9,8,128]{4,3,2,1,0:T(8,128)S(1)} %get-tuple-element.57.refs_4_), channel_id=1, source_target_pairs={{0,2},{1,3},{2,0},{3,1},{4,6},{5,7},{6,4},{7,5},{8,10},{9,11},{10,... | collective-permute-start | bytes 663560 | tf_op jit(solution)/shard_map/ppermute | solution.py:518
  52.8 7.6 %collective-permute-start.13 = (f32[1,3,12,8,128]{4,3,2,1,0:T(8,128)S(1)}, f32[1,3,12,8,128]{4,3,2,1,0:T(8,128)S(1)}, u32[]{:S(2)}, u32[]{:S(2)}) collective-permute-start(f32[1,3,12,8,128]{4,3,2,1,0:T(8,128)S(1)} %get-tuple-element.55.refs_4_), channel_id=1, source_target_pairs={{0,4},{1,5},{2,6},{3,7},{4,0},{5,1},{6,2},{7,3},{8,12},{9,13},{10,... | collective-permute-start | bytes 442376 | tf_op jit(solution)/shard_map/ppermute | solution.py:518
  61.7 5.7 %collective-permute-start.14 = (f32[1,3,9,8,128]{4,3,2,1,0:T(8,128)S(1)}, f32[1,3,9,8,128]{4,3,2,1,0:T(8,128)S(1)}, u32[]{:S(2)}, u32[]{:S(2)}) collective-permute-start(f32[1,3,9,8,128]{4,3,2,1,0:T(8,128)S(1)} %get-tuple-element.59), channel_id=1, source_target_pairs={{0,4},{1,5},{2,6},{3,7},{4,0},{5,1},{6,2},{7,3},{8,12},{9,13},{10,... | collective-permute-start | bytes 331784 | tf_op jit(solution)/shard_map/ppermute | solution.py:518

commit v4 on v3

--- a/solution.py
+++ b/solution.py
@@ -28,8 +28,11 @@
     return jnp.take_along_axis(table, index, axis=0, mode="promise_in_bounds")
 
 
-def fill_coefficients(table_ref, coef, sigma_scale):
-    rows = table_ref[...]
+def fill_coefficients(index_ref, tables_ref, coef, sigma_scale):
+    rows = jnp.zeros(tables_ref.shape[1:], F32)
+    for at in range(tables_ref.shape[0]):
+        chosen = jnp.broadcast_to(index_ref[...], rows.shape) == at
+        rows = jnp.where(chosen, tables_ref[at], rows)
     knots = rows.shape[1]
     at_row = lax.broadcasted_iota(jnp.int32, (2 * SUB, knots), 0)
     at_col = lax.broadcasted_iota(jnp.int32, (2 * SUB, knots), 1)
@@ -80,19 +83,19 @@
     return pltpu.make_async_copy(density_ref.at[:, :, columns], cells_ref.at[tile], sems.at[tile])
 
 
-def sums_kernel(sigma_scale, ratio, bits, split, table_ref, density_ref, *rest):
+def sums_kernel(sigma_scale, ratio, bits, split, index_ref, tables_ref, density_ref, *rest):
     if split:
         leaving_ref, cells_ref, sigma_ref, coef, send_ref, keep_ref, clear, sems = rest
     else:
         leaving_ref, cells_ref, sigma_ref, coef, sems = rest
     tiles, layers, slices, _ = cells_ref.shape
-    knots = table_ref.shape[1]
+    knots = tables_ref.shape[2]
 
     @pl.loop(0, tiles)
     def _(tile):
         fetch_tile(density_ref, cells_ref, sems, tile).start()
 
-    fill_coefficients(table_ref, coef, sigma_scale)
+    fill_coefficients(index_ref, tables_ref, coef, sigma_scale)
     mine = lax.axis_index("view") & 1 if split else 0
     half = (1 << bits) // 2
 
@@ -147,12 +150,13 @@
         leaving = jnp.concatenate(parts, axis=1)
         active = mine >= apart
         result = []
-        shared = None
         for drift, front in zip(DRIFTS, fronts):
-            if shared is None or apart < len(brick_refs):
-                row = front * leaving
-                shared = 0.5 * row + 0.25 * (pltpu.roll(row, 1, 1) + pltpu.roll(row, wide - 1, 1))
-            moved = shared if drift == 0 else pltpu.roll(shared, drift % wide, 1)
+            row = front * leaving
+            taps = [
+                row if hop % wide == 0 else pltpu.roll(row, hop % wide, 1)
+                for hop in (drift - 1, drift, drift + 1)
+            ]
+            moved = 0.5 * taps[1] + 0.25 * (taps[0] + taps[2])
             result.append(jnp.where(active, moved * inside, front))
         fronts = result
     for k in range(lighting.shape[0]):
@@ -311,7 +315,7 @@
 MERGE_COST = pl.CostEstimate(flops=2 * 10**10, bytes_accessed=2**20, transcendentals=0)
 
 
-def sums(density, table, sigma_scale, ratio, bits, split):
+def sums(density, tables, index, sigma_scale, ratio, bits, split):
     layers, slices, total = density.shape
     tiles = total // LANE
     half = (1 << bits) // 2
@@ -319,7 +323,7 @@
         shape(layers, total),
         shape(tiles, layers, slices, LANE),
         shape(tiles, layers, slices, LANE),
-        shape(4 * table.shape[0], SUB, LANE),
+        shape(4 * tables.shape[1], SUB, LANE),
     ]
     cells_shape = outs[1]
     scratch = []
@@ -329,14 +333,14 @@
     scratch.append(pltpu.SemaphoreType.DMA((tiles,)))
     return pl.pallas_call(
         functools.partial(sums_kernel, sigma_scale, ratio, bits, split),
-        in_specs=[VMEM(), HBM()],
+        in_specs=[VMEM(), VMEM(), HBM()],
         out_specs=[VMEM()] * len(outs),
         out_shape=outs,
         scratch_shapes=scratch,
         compiler_params=params(STREAM_LIMIT),
         cost_estimate=cost(cells_shape, total, 4000),
         name="sums",
-    )(table, density)
+    )(index, tables, density)
 
 
 def shade(coef, cells, knots, code, tint, bricks, pieces, low, high, ratio, bits, whole_out, after=()):
@@ -531,12 +535,12 @@
     return jnp.concatenate([front[:-1] + clear * back[:-1], clear * back[-1:]])
 
 
-def plain(density, table, light_code, light_tint, sigma_scale, ratio, bits):
+def plain(density, tables, index, light_code, light_tint, sigma_scale, ratio, bits):
     slices, total = density.shape[1:]
-    leaving, *cells, coef = sums(density, table, sigma_scale, ratio, 0, False)
+    leaving, *cells, coef = sums(density, tables, index, sigma_scale, ratio, 0, False)
     bricks = [[row] for row in from_earlier(leaving)]
     parts = shade(
-        coef, cells, table.shape[1], light_code, light_tint, bricks, [(0, total)], 0, total, ratio,
+        coef, cells, tables.shape[2], light_code, light_tint, bricks, [(0, total)], 0, total, ratio,
         0, True,
     )[0]
     rows = slices >> bits
@@ -573,15 +577,15 @@
     bits = views.bit_length() - 1
     sigma_scale = -1.0 / (layers * views)
     ratio = layers * views / (slices * lax.axis_size("light"))
-    chosen = lax.broadcasted_iota(jnp.int32, (tables.shape[0], 1), 0) == table_index
-    table = jnp.sum(jnp.where(chosen[:, :, None], tables, 0.0), axis=0)
     if views * SUB != slices or bits != 3:
-        return plain(density, table, light_code, light_tint, sigma_scale, ratio, bits)
+        return plain(
+            density, tables, table_index, light_code, light_tint, sigma_scale, ratio, bits
+        )
     pieces = [(0, total)]
     chunks = ranges(total)
-    knots = table.shape[1]
+    knots = tables.shape[2]
     leaving, *cells, coef, send, keep = sums(
-        density, table, sigma_scale, ratio, bits, True
+        density, tables, table_index, sigma_scale, ratio, bits, True
     )
     bricks = [[row] for row in from_earlier(leaving)]
     clear = [(keep, swap(send, 0))]

time: 68.6 us -> 68.3 us (level)
  other arithmetic: 0.81 us -> 0 us
  local copies, waits for them, and re-layouts: 0.01 us -> 0.72 us
    reduce_sum x1 -> x0, other arithmetic: 0.8 us -> none  [local(): table = jnp.sum(jnp.where(chosen[:, :, None], tables, 0.0), axis=0)]
    unnamed x4 -> x6, local copies, waits for them, and re-layouts: 0.01 us -> 0.72 us
where the time goes in v4:
time: 68.3 us; the launch traced here: 68 us
  Pallas kernels  27 us (40%)
  starting transfers between devices  22.2 us (33%)
  waiting for transfers between devices  17.3 us (25%)
  between operations  0.84 us (1%)
  local copies, waits for them, and re-layouts  0.72 us (1%)
    ppermute x12, waiting for transfers between devices, swap(): lax.ppermute(block, 'view', [(at, at ^ 1 << bit) for at in range(count)])  17.3 us
    ppermute x12, starting transfers between devices, swap(): lax.ppermute(block, 'view', [(at, at ^ 1 << bit) for at in range(count)])  13 us
    pallas_call x2, Pallas kernels, shade(): pl.pallas_call(functools.partial(shade_kernel, ratio, knots, low, tiles *...  12.1 us
    ppermute x3, starting transfers between devices, from_earlier(): lax.ppermute(leaving, 'light', [(at, at + apart) for at in range(count -...  9.15 us
    pallas_call x1, Pallas kernels, sums(): pl.pallas_call(functools.partial(sums_kernel, sigma_scale, ratio, bits, s...  7.16 us
    pallas_call x1, Pallas kernels, unlit(): pl.pallas_call(functools.partial(unlit_kernel, ratio, knots, low, len(aft...  4.65 us
    pallas_call x1, Pallas kernels, lit(): pl.pallas_call(functools.partial(lit_kernel, low, total, bits, pieces, le...  1.75 us
  transfers between devices with their start and end apart: 15, of which 6 were waited for; matrix products, arithmetic and copies ran while one was open for 0% of the time, Pallas kernels for 28%

profile of v4, /device:TPU:0, one launch (start us, length us, event | category | flops | bytes accessed | tf_op | source)
XLA Modules:
  0.0 68.0 jit_solution(3970177429245408810)
XLA Ops:
  0.7 0.7 %copy-done.2 = f32[8,4,16]{2,1,0:T(4,128)S(1)} copy-done((f32[8,4,16]{2,1,0:T(4,128)S(1)}, f32[8,4,16]{2,1,0:T(4,128)}, u32[]{:S(2)}) %copy-start.2) | copy-done | bytes 2072
  1.4 7.2 %sums.1 = (f32[8,4096]{1,0:T(8,128)S(1)}, f32[32,8,64,128]{3,2,1,0:T(8,128)S(1)}, f32[32,8,64,128]{3,2,1,0:T(8,128)S(1)}, f32[16,8,128]{2,1,0:T(8,128)S(1)}, f32...) custom-call(s32[1,1]{1,0:T(1,128)S(6)} %copy.6.index_ref, f32[8,4,16]{2,1,0:T(4,128)S(1)} %copy-done.2, ...), custom_call_target="tpu_custom_call" | custom-call | flops 8388608000 | bytes 8388608 | tf_op jit(solution)/shard_map/sums/pallas_call | solution.py:334
  8.5 0.5 collective-permute-start
  9.0 5.4 %collective-permute-start.3 = (f32[8,4096]{1,0:T(8,128)S(1)}, f32[8,4096]{1,0:T(8,128)S(1)}, u32[]{:S(2)}, u32[]{:S(2)}) collective-permute-start(f32[8,4096]{1,0:T(8,128)S(1)} %get-tuple-element.39), channel_id=1, source_target_pairs={{0,24},{1,25},{2,26},{3,27},{4,28},{5,29},{6,30},{7,31}} | collective-permute-start | bytes 393224 | tf_op jit(solution)/shard_map/ppermute | solution.py:528
  14.4 1.3 %collective-permute-start.2 = (f32[8,4096]{1,0:T(8,128)S(1)}, f32[8,4096]{1,0:T(8,128)S(1)}, u32[]{:S(2)}, u32[]{:S(2)}) collective-permute-start(f32[8,4096]{1,0:T(8,128)S(1)} %get-tuple-element.39), channel_id=1, source_target_pairs={{0,16},{8,24},{1,17},{9,25},{2,18},{10,26},{3,19},{11,27},{4,20},{... | collective-permute-start | bytes 393224 | tf_op jit(solution)/shard_map/ppermute | solution.py:528
  15.7 2.5 %collective-permute-start.1 = (f32[8,4096]{1,0:T(8,128)S(1)}, f32[8,4096]{1,0:T(8,128)S(1)}, u32[]{:S(2)}, u32[]{:S(2)}) collective-permute-start(f32[8,4096]{1,0:T(8,128)S(1)} %get-tuple-element.39), channel_id=1, source_target_pairs={{0,8},{8,16},{16,24},{1,9},{9,17},{17,25},{2,10},{10,18},{18,26},{... | collective-permute-start | bytes 393224 | tf_op jit(solution)/shard_map/ppermute | solution.py:528
  18.2 0.1 merge_clear.2
  18.3 1.6 %collective-permute-start.5 = (f32[2,32,8,128]{3,2,1,0:T(8,128)S(1)}, f32[2,32,8,128]{3,2,1,0:T(8,128)S(1)}, u32[]{:S(2)}, u32[]{:S(2)}) collective-permute-start(f32[2,32,8,128]{3,2,1,0:T(8,128)S(1)} %get-tuple-element.38.rest_2_), channel_id=1, source_target_pairs={{0,2},{1,3},{2,0},{3,1},{4,6},{5,7},{6,4},{7,5},{8,10},{9,11},{10,... | collective-permute-start | bytes 786440 | tf_op jit(solution)/shard_map/ppermute | solution.py:522
  20.0 4.6 %unlit.1.unlit_ref = f32[11,8,3,64,128]{4,3,2,1,0:T(8,128)S(1)} custom-call(f32[16,8,128]{2,1,0:T(8,128)S(1)} %get-tuple-element.33.coef, f32[32,8,64,128]{3,2,1,0:T(8,128)S(1)} %get-tuple-element.34.rest_0_, f32[32,8,64,128]{3,2,1,0:T(8,128)S(1)} %get-tuple-element.35.rest_1_, f32[2,32,8,128]{3,2,1,0:T(8,128)S(1)} %get-tuple-element.38.rest_2_), custom_call_target="tpu_custom_call" | custom-call | flops 7208960000 | bytes 2883584 | tf_op jit(solution)/shard_map/unlit/pallas_call | solution.py:375
  24.7 1.7 %lit.1 = (f32[4,3,11,8,128]{4,3,2,1,0:T(8,128)S(1)}, f32[4,3,11,8,128]{4,3,2,1,0:T(8,128)S(1)}) custom-call(s32[4]{0:T(128)S(1)} %copy-done.1, f32[4,3]{1,0:T(4,128)S(1)} %copy-done, f32[11,8,3,64,128]{4,3,2,1,0:T(8,128)S(1)} %unlit.1.unlit_ref, f32[8,4096]{1,0:T(8,128)S(1)} %collective-permute-done.1.rest_0_.rest_2_, ...), custom_call_target="tpu_custom_call" | custom-call | tf_op jit(solution)/shard_map/lit/pallas_call | solution.py:390
  26.4 0.1 collective-permute-start.4
  26.5 2.7 %collective-permute-start.7 = (f32[1,32,8,128]{3,2,1,0:T(8,128)S(1)}, f32[1,32,8,128]{3,2,1,0:T(8,128)S(1)}, u32[]{:S(2)}, u32[]{:S(2)}) collective-permute-start(f32[1,32,8,128]{3,2,1,0:T(8,128)S(1)} %get-tuple-element.43.refs_4_), channel_id=1, source_target_pairs={{0,4},{1,5},{2,6},{3,7},{4,0},{5,1},{6,2},{7,3},{8,12},{9,13},{10,... | collective-permute-start | bytes 393224 | tf_op jit(solution)/shard_map/ppermute | solution.py:522
  29.2 0.1 merge.6
  29.3 1.6 %collective-permute-start.6 = (f32[2,3,11,8,128]{4,3,2,1,0:T(8,128)S(1)}, f32[2,3,11,8,128]{4,3,2,1,0:T(8,128)S(1)}, u32[]{:S(2)}, u32[]{:S(2)}) collective-permute-start(f32[2,3,11,8,128]{4,3,2,1,0:T(8,128)S(1)} %get-tuple-element.45.rest_5_), channel_id=1, source_target_pairs={{0,2},{1,3},{2,0},{3,1},{4,6},{5,7},{6,4},{7,5},{8,10},{9,11},{10,... | collective-permute-start | bytes 811016 | tf_op jit(solution)/shard_map/ppermute | solution.py:522
  30.9 6.8 %shade.2 = (f32[4,3,12,8,128]{4,3,2,1,0:T(8,128)S(1)}, f32[4,3,12,8,128]{4,3,2,1,0:T(8,128)S(1)}) custom-call(s32[4]{0:T(128)S(1)} %copy-done.1, f32[4,3]{1,0:T(4,128)S(1)} %copy-done, f32[16,8,128]{2,1,0:T(8,128)S(1)} %get-tuple-element.33.coef, f32[32,8,64,128]{3,2,1,0:T(8,128)S(1)} %get-tuple-element.34.rest_0_, ...), custom_call_target="tpu_custom_call" | custom-call | flops 7864320000 | bytes 3145728 | tf_op jit(solution)/shard_map/shade/pallas_call | solution.py:355
  37.7 0.1 collective-permute-start.8
  37.8 2.7 %collective-permute-done.6.refs_1_ = f32[2,3,11,8,128]{4,3,2,1,0:T(8,128)S(1)} collective-permute-done((f32[2,3,11,8,128]{4,3,2,1,0:T(8,128)S(1)}, f32[2,3,11,8,128]{4,3,2,1,0:T(8,128)S(1)}, u32[]{:S(2)}, u32[]{:S(2)}) %collective-permute-start.6) | collective-permute-done | bytes 270368 | tf_op jit(solution)/shard_map/ppermute | solution.py:522
  40.6 0.1 collective-permute-start.10
  40.7 0.1 merge.8
  40.8 1.7 %collective-permute-start.9 = (f32[2,3,12,8,128]{4,3,2,1,0:T(8,128)S(1)}, f32[2,3,12,8,128]{4,3,2,1,0:T(8,128)S(1)}, u32[]{:S(2)}, u32[]{:S(2)}) collective-permute-start(f32[2,3,12,8,128]{4,3,2,1,0:T(8,128)S(1)} %get-tuple-element.51.rest_5_), channel_id=1, source_target_pairs={{0,2},{1,3},{2,0},{3,1},{4,6},{5,7},{6,4},{7,5},{8,10},{9,11},{10,... | collective-permute-start | bytes 884744 | tf_op jit(solution)/shard_map/ppermute | solution.py:522
  42.5 5.3 %shade.3 = (f32[4,3,9,8,128]{4,3,2,1,0:T(8,128)S(1)}, f32[4,3,9,8,128]{4,3,2,1,0:T(8,128)S(1)}) custom-call(s32[4]{0:T(128)S(1)} %copy-done.1, f32[4,3]{1,0:T(4,128)S(1)} %copy-done, f32[16,8,128]{2,1,0:T(8,128)S(1)} %get-tuple-element.33.coef, f32[32,8,64,128]{3,2,1,0:T(8,128)S(1)} %get-tuple-element.34.rest_0_, ...), custom_call_target="tpu_custom_call" | custom-call | flops 5898240000 | bytes 2359296 | tf_op jit(solution)/shard_map/shade/pallas_call | solution.py:355
  47.8 0.1 collective-permute-start.11
  47.8 1.6 %collective-permute-done.10.refs_5_.refs_3_ = f32[1,3,11,8,128]{4,3,2,1,0:T(8,128)S(1)} collective-permute-done((f32[1,3,11,8,128]{4,3,2,1,0:T(8,128)S(1)}, f32[1,3,11,8,128]{4,3,2,1,0:T(8,128)S(1)}, u32[]{:S(2)}, u32[]{:S(2)}) %collective-permute-start.10) | collective-permute-done | bytes 135200 | tf_op jit(solution)/shard_map/ppermute | solution.py:522
  49.4 2.6 %collective-permute-done.9.refs_1_ = f32[2,3,12,8,128]{4,3,2,1,0:T(8,128)S(1)} collective-permute-done((f32[2,3,12,8,128]{4,3,2,1,0:T(8,128)S(1)}, f32[2,3,12,8,128]{4,3,2,1,0:T(8,128)S(1)}, u32[]{:S(2)}, u32[]{:S(2)}) %collective-permute-start.9) | collective-permute-done | bytes 294944 | tf_op jit(solution)/shard_map/ppermute | solution.py:522
  52.1 0.1 merge.10
  52.2 0.2 collective-permute-start.12
  52.3 3.1 %collective-permute-start.13 = (f32[1,3,12,8,128]{4,3,2,1,0:T(8,128)S(1)}, f32[1,3,12,8,128]{4,3,2,1,0:T(8,128)S(1)}, u32[]{:S(2)}, u32[]{:S(2)}) collective-permute-start(f32[1,3,12,8,128]{4,3,2,1,0:T(8,128)S(1)} %get-tuple-element.55.refs_4_), channel_id=1, source_target_pairs={{0,4},{1,5},{2,6},{3,7},{4,0},{5,1},{6,2},{7,3},{8,12},{9,13},{10,... | collective-permute-start | bytes 442376 | tf_op jit(solution)/shard_map/ppermute | solution.py:522
  55.5 4.5 %collective-permute-done.13.refs_5_.refs_4_ = f32[1,3,12,8,128]{4,3,2,1,0:T(8,128)S(1)} collective-permute-done((f32[1,3,12,8,128]{4,3,2,1,0:T(8,128)S(1)}, f32[1,3,12,8,128]{4,3,2,1,0:T(8,128)S(1)}, u32[]{:S(2)}, u32[]{:S(2)}) %collective-permute-start.13) | collective-permute-done | bytes 147488 | tf_op jit(solution)/shard_map/ppermute | solution.py:522
  60.0 1.4 %collective-permute-done.12.refs_1_ = f32[2,3,9,8,128]{4,3,2,1,0:T(8,128)S(1)} collective-permute-done((f32[2,3,9,8,128]{4,3,2,1,0:T(8,128)S(1)}, f32[2,3,9,8,128]{4,3,2,1,0:T(8,128)S(1)}, u32[]{:S(2)}, u32[]{:S(2)}) %collective-permute-start.12) | collective-permute-done | bytes 221216 | tf_op jit(solution)/shard_map/ppermute | solution.py:522
  61.4 1.3 %collective-permute-start.14 = (f32[1,3,9,8,128]{4,3,2,1,0:T(8,128)S(1)}, f32[1,3,9,8,128]{4,3,2,1,0:T(8,128)S(1)}, u32[]{:S(2)}, u32[]{:S(2)}) collective-permute-start(f32[1,3,9,8,128]{4,3,2,1,0:T(8,128)S(1)} %get-tuple-element.59), channel_id=1, source_target_pairs={{0,4},{1,5},{2,6},{3,7},{4,0},{5,1},{6,2},{7,3},{8,12},{9,13},{10,... | collective-permute-start | bytes 331784 | tf_op jit(solution)/shard_map/ppermute | solution.py:522
  62.7 4.5 %collective-permute-done.14.refs_5_ = f32[1,3,9,8,128]{4,3,2,1,0:T(8,128)S(1)} collective-permute-done((f32[1,3,9,8,128]{4,3,2,1,0:T(8,128)S(1)}, f32[1,3,9,8,128]{4,3,2,1,0:T(8,128)S(1)}, u32[]{:S(2)}, u32[]{:S(2)}) %collective-permute-start.14) | collective-permute-done | bytes 110624 | tf_op jit(solution)/shard_map/ppermute | solution.py:522
  67.2 0.9 %last.1 = f32[4,8,4096]{2,1,0:T(8,128)} custom-call(f32[1,3,11,8,128]{4,3,2,1,0:T(8,128)S(1)} %get-tuple-element.47.refs_0_, f32[1,3,12,8,128]{4,3,2,1,0:T(8,128)S(1)} %get-tuple-element.53.refs_1_, f32[1,3,9,8,128]{4,3,2,1,0:T(8,128)S(1)} %get-tuple-element.58.refs_2_, f32[1,3,11,8,128]{4,3,2,1,0:T(8,128)S(1)} %collective-permute-done.10.refs_5_.refs_3_, ...), custom_call_target="tpu_custom_call" | custom-call | tf_op jit(solution)/shard_map/last/pallas_call | solution.py:510
  (18 shorter events, 0.2 us)
Async XLA Ops:
  0.7 0.7 %copy-start.2 = (f32[8,4,16]{2,1,0:T(4,128)S(1)}, f32[8,4,16]{2,1,0:T(4,128)}, u32[]{:S(2)}) copy-start(f32[8,4,16]{2,1,0:T(4,128)} %tables_ref.1) | copy-start | bytes 6148
  8.5 9.7 %collective-permute-start = (f32[4,32,8,128]{3,2,1,0:T(8,128)S(1)}, f32[4,32,8,128]{3,2,1,0:T(8,128)S(1)}, u32[]{:S(2)}, u32[]{:S(2)}) collective-permute-start(f32[4,32,8,128]{3,2,1,0:T(8,128)S(1)} %get-tuple-element.37), channel_id=1, source_target_pairs={{0,1},{1,0},{2,3},{3,2},{4,5},{5,4},{6,7},{7,6},{8,9},{9,8},{10,11... | collective-permute-start | bytes 1572872 | tf_op jit(solution)/shard_map/ppermute | solution.py:522
  9.0 15.6 %collective-permute-start.3 = (f32[8,4096]{1,0:T(8,128)S(1)}, f32[8,4096]{1,0:T(8,128)S(1)}, u32[]{:S(2)}, u32[]{:S(2)}) collective-permute-start(f32[8,4096]{1,0:T(8,128)S(1)} %get-tuple-element.39), channel_id=1, source_target_pairs={{0,24},{1,25},{2,26},{3,27},{4,28},{5,29},{6,30},{7,31}} | collective-permute-start | bytes 393224 | tf_op jit(solution)/shard_map/ppermute | solution.py:528
  14.4 10.2 %collective-permute-start.2 = (f32[8,4096]{1,0:T(8,128)S(1)}, f32[8,4096]{1,0:T(8,128)S(1)}, u32[]{:S(2)}, u32[]{:S(2)}) collective-permute-start(f32[8,4096]{1,0:T(8,128)S(1)} %get-tuple-element.39), channel_id=1, source_target_pairs={{0,16},{8,24},{1,17},{9,25},{2,18},{10,26},{3,19},{11,27},{4,20},{... | collective-permute-start | bytes 393224 | tf_op jit(solution)/shard_map/ppermute | solution.py:528
  15.7 8.9 %collective-permute-start.1 = (f32[8,4096]{1,0:T(8,128)S(1)}, f32[8,4096]{1,0:T(8,128)S(1)}, u32[]{:S(2)}, u32[]{:S(2)}) collective-permute-start(f32[8,4096]{1,0:T(8,128)S(1)} %get-tuple-element.39), channel_id=1, source_target_pairs={{0,8},{8,16},{16,24},{1,9},{9,17},{17,25},{2,10},{10,18},{18,26},{... | collective-permute-start | bytes 393224 | tf_op jit(solution)/shard_map/ppermute | solution.py:528
  18.3 8.2 %collective-permute-start.5 = (f32[2,32,8,128]{3,2,1,0:T(8,128)S(1)}, f32[2,32,8,128]{3,2,1,0:T(8,128)S(1)}, u32[]{:S(2)}, u32[]{:S(2)}) collective-permute-start(f32[2,32,8,128]{3,2,1,0:T(8,128)S(1)} %get-tuple-element.38.rest_2_), channel_id=1, source_target_pairs={{0,2},{1,3},{2,0},{3,1},{4,6},{5,7},{6,4},{7,5},{8,10},{9,11},{10,... | collective-permute-start | bytes 786440 | tf_op jit(solution)/shard_map/ppermute | solution.py:522
  20.0 4.7 %copy-start = (f32[4,3]{1,0:T(4,128)S(1)}, f32[4,3]{1,0:T(4,128)}, u32[]{:S(2)}) copy-start(f32[4,3]{1,0:T(4,128)} %tint_ref.5) | copy-start | bytes 148
  20.0 4.7 %copy-start.1 = (s32[4]{0:T(128)S(1)}, s32[4]{0:T(128)}, u32[]{:S(2)}) copy-start(s32[4]{0:T(128)} %code_ref.5) | copy-start | bytes 52
  26.4 2.8 %collective-permute-start.4 = (f32[4,3,11,8,128]{4,3,2,1,0:T(8,128)S(1)}, f32[4,3,11,8,128]{4,3,2,1,0:T(8,128)S(1)}, u32[]{:S(2)}, u32[]{:S(2)}) collective-permute-start(f32[4,3,11,8,128]{4,3,2,1,0:T(8,128)S(1)} %get-tuple-element.41.rest_0_), channel_id=1, source_target_pairs={{0,1},{1,0},{2,3},{3,2},{4,5},{5,4},{6,7},{7,6},{8,9},{9,8},{10,11... | collective-permute-start | bytes 1622024 | tf_op jit(solution)/shard_map/ppermute | solution.py:522
  26.5 11.3 %collective-permute-start.7 = (f32[1,32,8,128]{3,2,1,0:T(8,128)S(1)}, f32[1,32,8,128]{3,2,1,0:T(8,128)S(1)}, u32[]{:S(2)}, u32[]{:S(2)}) collective-permute-start(f32[1,32,8,128]{3,2,1,0:T(8,128)S(1)} %get-tuple-element.43.refs_4_), channel_id=1, source_target_pairs={{0,4},{1,5},{2,6},{3,7},{4,0},{5,1},{6,2},{7,3},{8,12},{9,13},{10,... | collective-permute-start | bytes 393224 | tf_op jit(solution)/shard_map/ppermute | solution.py:522
  29.3 11.2 %collective-permute-start.6 = (f32[2,3,11,8,128]{4,3,2,1,0:T(8,128)S(1)}, f32[2,3,11,8,128]{4,3,2,1,0:T(8,128)S(1)}, u32[]{:S(2)}, u32[]{:S(2)}) collective-permute-start(f32[2,3,11,8,128]{4,3,2,1,0:T(8,128)S(1)} %get-tuple-element.45.rest_5_), channel_id=1, source_target_pairs={{0,2},{1,3},{2,0},{3,1},{4,6},{5,7},{6,4},{7,5},{8,10},{9,11},{10,... | collective-permute-start | bytes 811016 | tf_op jit(solution)/shard_map/ppermute | solution.py:522
  37.7 2.9 %collective-permute-start.8 = (f32[4,3,12,8,128]{4,3,2,1,0:T(8,128)S(1)}, f32[4,3,12,8,128]{4,3,2,1,0:T(8,128)S(1)}, u32[]{:S(2)}, u32[]{:S(2)}) collective-permute-start(f32[4,3,12,8,128]{4,3,2,1,0:T(8,128)S(1)} %get-tuple-element.46.refs_4_), channel_id=1, source_target_pairs={{0,1},{1,0},{2,3},{3,2},{4,5},{5,4},{6,7},{7,6},{8,9},{9,8},{10,11... | collective-permute-start | bytes 1769480 | tf_op jit(solution)/shard_map/ppermute | solution.py:522
  40.6 8.8 %collective-permute-start.10 = (f32[1,3,11,8,128]{4,3,2,1,0:T(8,128)S(1)}, f32[1,3,11,8,128]{4,3,2,1,0:T(8,128)S(1)}, u32[]{:S(2)}, u32[]{:S(2)}) collective-permute-start(f32[1,3,11,8,128]{4,3,2,1,0:T(8,128)S(1)} %get-tuple-element.49.refs_4_), channel_id=1, source_target_pairs={{0,4},{1,5},{2,6},{3,7},{4,0},{5,1},{6,2},{7,3},{8,12},{9,13},{10,... | collective-permute-start | bytes 405512 | tf_op jit(solution)/shard_map/ppermute | solution.py:522
  40.8 11.2 %collective-permute-start.9 = (f32[2,3,12,8,128]{4,3,2,1,0:T(8,128)S(1)}, f32[2,3,12,8,128]{4,3,2,1,0:T(8,128)S(1)}, u32[]{:S(2)}, u32[]{:S(2)}) collective-permute-start(f32[2,3,12,8,128]{4,3,2,1,0:T(8,128)S(1)} %get-tuple-element.51.rest_5_), channel_id=1, source_target_pairs={{0,2},{1,3},{2,0},{3,1},{4,6},{5,7},{6,4},{7,5},{8,10},{9,11},{10,... | collective-permute-start | bytes 884744 | tf_op jit(solution)/shard_map/ppermute | solution.py:522
  47.8 4.3 %collective-permute-start.11 = (f32[4,3,9,8,128]{4,3,2,1,0:T(8,128)S(1)}, f32[4,3,9,8,128]{4,3,2,1,0:T(8,128)S(1)}, u32[]{:S(2)}, u32[]{:S(2)}) collective-permute-start(f32[4,3,9,8,128]{4,3,2,1,0:T(8,128)S(1)} %get-tuple-element.52.refs_4_), channel_id=1, source_target_pairs={{0,1},{1,0},{2,3},{3,2},{4,5},{5,4},{6,7},{7,6},{8,9},{9,8},{10,11... | collective-permute-start | bytes 1327112 | tf_op jit(solution)/shard_map/ppermute | solution.py:522
  52.2 9.2 %collective-permute-start.12 = (f32[2,3,9,8,128]{4,3,2,1,0:T(8,128)S(1)}, f32[2,3,9,8,128]{4,3,2,1,0:T(8,128)S(1)}, u32[]{:S(2)}, u32[]{:S(2)}) collective-permute-start(f32[2,3,9,8,128]{4,3,2,1,0:T(8,128)S(1)} %get-tuple-element.57.refs_4_), channel_id=1, source_target_pairs={{0,2},{1,3},{2,0},{3,1},{4,6},{5,7},{6,4},{7,5},{8,10},{9,11},{10,... | collective-permute-start | bytes 663560 | tf_op jit(solution)/shard_map/ppermute | solution.py:522
  52.3 7.7 %collective-permute-start.13 = (f32[1,3,12,8,128]{4,3,2,1,0:T(8,128)S(1)}, f32[1,3,12,8,128]{4,3,2,1,0:T(8,128)S(1)}, u32[]{:S(2)}, u32[]{:S(2)}) collective-permute-start(f32[1,3,12,8,128]{4,3,2,1,0:T(8,128)S(1)} %get-tuple-element.55.refs_4_), channel_id=1, source_target_pairs={{0,4},{1,5},{2,6},{3,7},{4,0},{5,1},{6,2},{7,3},{8,12},{9,13},{10,... | collective-permute-start | bytes 442376 | tf_op jit(solution)/shard_map/ppermute | solution.py:522
  61.4 5.7 %collective-permute-start.14 = (f32[1,3,9,8,128]{4,3,2,1,0:T(8,128)S(1)}, f32[1,3,9,8,128]{4,3,2,1,0:T(8,128)S(1)}, u32[]{:S(2)}, u32[]{:S(2)}) collective-permute-start(f32[1,3,9,8,128]{4,3,2,1,0:T(8,128)S(1)} %get-tuple-element.59), channel_id=1, source_target_pairs={{0,4},{1,5},{2,6},{3,7},{4,0},{5,1},{6,2},{7,3},{8,12},{9,13},{10,... | collective-permute-start | bytes 331784 | tf_op jit(solution)/shard_map/ppermute | solution.py:522

commit v5 on v4

--- a/solution.py
+++ b/solution.py
@@ -133,6 +133,7 @@
     wide = width + 2 * LANE
     place = lax.broadcasted_iota(jnp.int32, (layers, wide), 1) + (first - LANE)
     inside = jnp.logical_and(place >= 0, place < total).astype(F32)
+    within = first >= LANE and first + width + LANE <= total
     mine = lax.axis_index("light")
     fronts = [inside] * len(DRIFTS)
     for apart in range(len(brick_refs), 0, -1):
@@ -157,7 +158,7 @@
                 for hop in (drift - 1, drift, drift + 1)
             ]
             moved = 0.5 * taps[1] + 0.25 * (taps[0] + taps[2])
-            result.append(jnp.where(active, moved * inside, front))
+            result.append(jnp.where(active, moved if within else moved * inside, front))
         fronts = result
     for k in range(lighting.shape[0]):
         shade = jnp.zeros((layers, wide), F32)

time: 68.3 us -> 68.3 us (level)
  no operation moved by 1% of the time
where the time goes in v5:
time: 68.3 us; the launch traced here: 68 us
  Pallas kernels  27 us (40%)
  starting transfers between devices  22.2 us (33%)
  waiting for transfers between devices  17.3 us (25%)
  between operations  0.84 us (1%)
  local copies, waits for them, and re-layouts  0.72 us (1%)
    ppermute x12, waiting for transfers between devices, swap(): lax.ppermute(block, 'view', [(at, at ^ 1 << bit) for at in range(count)])  17.3 us
    ppermute x12, starting transfers between devices, swap(): lax.ppermute(block, 'view', [(at, at ^ 1 << bit) for at in range(count)])  13 us
    pallas_call x2, Pallas kernels, shade(): pl.pallas_call(functools.partial(shade_kernel, ratio, knots, low, tiles *...  12.1 us
    ppermute x3, starting transfers between devices, from_earlier(): lax.ppermute(leaving, 'light', [(at, at + apart) for at in range(count -...  9.15 us
    pallas_call x1, Pallas kernels, sums(): pl.pallas_call(functools.partial(sums_kernel, sigma_scale, ratio, bits, s...  7.16 us
    pallas_call x1, Pallas kernels, unlit(): pl.pallas_call(functools.partial(unlit_kernel, ratio, knots, low, len(aft...  4.65 us
    pallas_call x1, Pallas kernels, lit(): pl.pallas_call(functools.partial(lit_kernel, low, total, bits, pieces, le...  1.75 us
  transfers between devices with their start and end apart: 15, of which 6 were waited for; matrix products, arithmetic and copies ran while one was open for 0% of the time, Pallas kernels for 28%

profile of v5, /device:TPU:0, one launch (start us, length us, event | category | flops | bytes accessed | tf_op | source)
XLA Modules:
  0.0 68.0 jit_solution(3970177429245408810)
XLA Ops:
  0.7 0.7 %copy-done.2 = f32[8,4,16]{2,1,0:T(4,128)S(1)} copy-done((f32[8,4,16]{2,1,0:T(4,128)S(1)}, f32[8,4,16]{2,1,0:T(4,128)}, u32[]{:S(2)}) %copy-start.2) | copy-done | bytes 2072
  1.4 7.2 %sums.1 = (f32[8,4096]{1,0:T(8,128)S(1)}, f32[32,8,64,128]{3,2,1,0:T(8,128)S(1)}, f32[32,8,64,128]{3,2,1,0:T(8,128)S(1)}, f32[16,8,128]{2,1,0:T(8,128)S(1)}, f32...) custom-call(s32[1,1]{1,0:T(1,128)S(6)} %copy.6.index_ref, f32[8,4,16]{2,1,0:T(4,128)S(1)} %copy-done.2, ...), custom_call_target="tpu_custom_call" | custom-call | flops 8388608000 | bytes 8388608 | tf_op jit(solution)/shard_map/sums/pallas_call | solution.py:335
  8.5 0.5 collective-permute-start
  9.0 5.4 %collective-permute-start.3 = (f32[8,4096]{1,0:T(8,128)S(1)}, f32[8,4096]{1,0:T(8,128)S(1)}, u32[]{:S(2)}, u32[]{:S(2)}) collective-permute-start(f32[8,4096]{1,0:T(8,128)S(1)} %get-tuple-element.39), channel_id=1, source_target_pairs={{0,24},{1,25},{2,26},{3,27},{4,28},{5,29},{6,30},{7,31}} | collective-permute-start | bytes 393224 | tf_op jit(solution)/shard_map/ppermute | solution.py:529
  14.4 1.3 %collective-permute-start.2 = (f32[8,4096]{1,0:T(8,128)S(1)}, f32[8,4096]{1,0:T(8,128)S(1)}, u32[]{:S(2)}, u32[]{:S(2)}) collective-permute-start(f32[8,4096]{1,0:T(8,128)S(1)} %get-tuple-element.39), channel_id=1, source_target_pairs={{0,16},{8,24},{1,17},{9,25},{2,18},{10,26},{3,19},{11,27},{4,20},{... | collective-permute-start | bytes 393224 | tf_op jit(solution)/shard_map/ppermute | solution.py:529
  15.7 2.5 %collective-permute-start.1 = (f32[8,4096]{1,0:T(8,128)S(1)}, f32[8,4096]{1,0:T(8,128)S(1)}, u32[]{:S(2)}, u32[]{:S(2)}) collective-permute-start(f32[8,4096]{1,0:T(8,128)S(1)} %get-tuple-element.39), channel_id=1, source_target_pairs={{0,8},{8,16},{16,24},{1,9},{9,17},{17,25},{2,10},{10,18},{18,26},{... | collective-permute-start | bytes 393224 | tf_op jit(solution)/shard_map/ppermute | solution.py:529
  18.2 0.1 merge_clear.2
  18.3 1.6 %collective-permute-start.5 = (f32[2,32,8,128]{3,2,1,0:T(8,128)S(1)}, f32[2,32,8,128]{3,2,1,0:T(8,128)S(1)}, u32[]{:S(2)}, u32[]{:S(2)}) collective-permute-start(f32[2,32,8,128]{3,2,1,0:T(8,128)S(1)} %get-tuple-element.38.rest_2_), channel_id=1, source_target_pairs={{0,2},{1,3},{2,0},{3,1},{4,6},{5,7},{6,4},{7,5},{8,10},{9,11},{10,... | collective-permute-start | bytes 786440 | tf_op jit(solution)/shard_map/ppermute | solution.py:523
  20.0 4.6 %unlit.1.unlit_ref = f32[11,8,3,64,128]{4,3,2,1,0:T(8,128)S(1)} custom-call(f32[16,8,128]{2,1,0:T(8,128)S(1)} %get-tuple-element.33.coef, f32[32,8,64,128]{3,2,1,0:T(8,128)S(1)} %get-tuple-element.34.rest_0_, f32[32,8,64,128]{3,2,1,0:T(8,128)S(1)} %get-tuple-element.35.rest_1_, f32[2,32,8,128]{3,2,1,0:T(8,128)S(1)} %get-tuple-element.38.rest_2_), custom_call_target="tpu_custom_call" | custom-call | flops 7208960000 | bytes 2883584 | tf_op jit(solution)/shard_map/unlit/pallas_call | solution.py:376
  24.7 1.7 %lit.1 = (f32[4,3,11,8,128]{4,3,2,1,0:T(8,128)S(1)}, f32[4,3,11,8,128]{4,3,2,1,0:T(8,128)S(1)}) custom-call(s32[4]{0:T(128)S(1)} %copy-done.1, f32[4,3]{1,0:T(4,128)S(1)} %copy-done, f32[11,8,3,64,128]{4,3,2,1,0:T(8,128)S(1)} %unlit.1.unlit_ref, f32[8,4096]{1,0:T(8,128)S(1)} %collective-permute-done.1.rest_0_.rest_2_, ...), custom_call_target="tpu_custom_call" | custom-call | tf_op jit(solution)/shard_map/lit/pallas_call | solution.py:391
  26.4 0.1 collective-permute-start.4
  26.5 2.7 %collective-permute-start.7 = (f32[1,32,8,128]{3,2,1,0:T(8,128)S(1)}, f32[1,32,8,128]{3,2,1,0:T(8,128)S(1)}, u32[]{:S(2)}, u32[]{:S(2)}) collective-permute-start(f32[1,32,8,128]{3,2,1,0:T(8,128)S(1)} %get-tuple-element.43.refs_4_), channel_id=1, source_target_pairs={{0,4},{1,5},{2,6},{3,7},{4,0},{5,1},{6,2},{7,3},{8,12},{9,13},{10,... | collective-permute-start | bytes 393224 | tf_op jit(solution)/shard_map/ppermute | solution.py:523
  29.2 0.1 merge.6
  29.3 1.6 %collective-permute-start.6 = (f32[2,3,11,8,128]{4,3,2,1,0:T(8,128)S(1)}, f32[2,3,11,8,128]{4,3,2,1,0:T(8,128)S(1)}, u32[]{:S(2)}, u32[]{:S(2)}) collective-permute-start(f32[2,3,11,8,128]{4,3,2,1,0:T(8,128)S(1)} %get-tuple-element.45.rest_5_), channel_id=1, source_target_pairs={{0,2},{1,3},{2,0},{3,1},{4,6},{5,7},{6,4},{7,5},{8,10},{9,11},{10,... | collective-permute-start | bytes 811016 | tf_op jit(solution)/shard_map/ppermute | solution.py:523
  30.9 6.8 %shade.2 = (f32[4,3,12,8,128]{4,3,2,1,0:T(8,128)S(1)}, f32[4,3,12,8,128]{4,3,2,1,0:T(8,128)S(1)}) custom-call(s32[4]{0:T(128)S(1)} %copy-done.1, f32[4,3]{1,0:T(4,128)S(1)} %copy-done, f32[16,8,128]{2,1,0:T(8,128)S(1)} %get-tuple-element.33.coef, f32[32,8,64,128]{3,2,1,0:T(8,128)S(1)} %get-tuple-element.34.rest_0_, ...), custom_call_target="tpu_custom_call" | custom-call | flops 7864320000 | bytes 3145728 | tf_op jit(solution)/shard_map/shade/pallas_call | solution.py:356
  37.7 0.1 collective-permute-start.8
  37.8 2.7 %collective-permute-done.6.refs_1_ = f32[2,3,11,8,128]{4,3,2,1,0:T(8,128)S(1)} collective-permute-done((f32[2,3,11,8,128]{4,3,2,1,0:T(8,128)S(1)}, f32[2,3,11,8,128]{4,3,2,1,0:T(8,128)S(1)}, u32[]{:S(2)}, u32[]{:S(2)}) %collective-permute-start.6) | collective-permute-done | bytes 270368 | tf_op jit(solution)/shard_map/ppermute | solution.py:523
  40.6 0.1 collective-permute-start.10
  40.7 0.1 merge.8
  40.8 1.7 %collective-permute-start.9 = (f32[2,3,12,8,128]{4,3,2,1,0:T(8,128)S(1)}, f32[2,3,12,8,128]{4,3,2,1,0:T(8,128)S(1)}, u32[]{:S(2)}, u32[]{:S(2)}) collective-permute-start(f32[2,3,12,8,128]{4,3,2,1,0:T(8,128)S(1)} %get-tuple-element.51.rest_5_), channel_id=1, source_target_pairs={{0,2},{1,3},{2,0},{3,1},{4,6},{5,7},{6,4},{7,5},{8,10},{9,11},{10,... | collective-permute-start | bytes 884744 | tf_op jit(solution)/shard_map/ppermute | solution.py:523
  42.5 5.3 %shade.3 = (f32[4,3,9,8,128]{4,3,2,1,0:T(8,128)S(1)}, f32[4,3,9,8,128]{4,3,2,1,0:T(8,128)S(1)}) custom-call(s32[4]{0:T(128)S(1)} %copy-done.1, f32[4,3]{1,0:T(4,128)S(1)} %copy-done, f32[16,8,128]{2,1,0:T(8,128)S(1)} %get-tuple-element.33.coef, f32[32,8,64,128]{3,2,1,0:T(8,128)S(1)} %get-tuple-element.34.rest_0_, ...), custom_call_target="tpu_custom_call" | custom-call | flops 5898240000 | bytes 2359296 | tf_op jit(solution)/shard_map/shade/pallas_call | solution.py:356
  47.8 0.1 collective-permute-start.11
  47.8 1.6 %collective-permute-done.10.refs_5_.refs_3_ = f32[1,3,11,8,128]{4,3,2,1,0:T(8,128)S(1)} collective-permute-done((f32[1,3,11,8,128]{4,3,2,1,0:T(8,128)S(1)}, f32[1,3,11,8,128]{4,3,2,1,0:T(8,128)S(1)}, u32[]{:S(2)}, u32[]{:S(2)}) %collective-permute-start.10) | collective-permute-done | bytes 135200 | tf_op jit(solution)/shard_map/ppermute | solution.py:523
  49.4 2.6 %collective-permute-done.9.refs_1_ = f32[2,3,12,8,128]{4,3,2,1,0:T(8,128)S(1)} collective-permute-done((f32[2,3,12,8,128]{4,3,2,1,0:T(8,128)S(1)}, f32[2,3,12,8,128]{4,3,2,1,0:T(8,128)S(1)}, u32[]{:S(2)}, u32[]{:S(2)}) %collective-permute-start.9) | collective-permute-done | bytes 294944 | tf_op jit(solution)/shard_map/ppermute | solution.py:523
  52.1 0.1 merge.10
  52.2 0.2 collective-permute-start.12
  52.3 3.1 %collective-permute-start.13 = (f32[1,3,12,8,128]{4,3,2,1,0:T(8,128)S(1)}, f32[1,3,12,8,128]{4,3,2,1,0:T(8,128)S(1)}, u32[]{:S(2)}, u32[]{:S(2)}) collective-permute-start(f32[1,3,12,8,128]{4,3,2,1,0:T(8,128)S(1)} %get-tuple-element.55.refs_4_), channel_id=1, source_target_pairs={{0,4},{1,5},{2,6},{3,7},{4,0},{5,1},{6,2},{7,3},{8,12},{9,13},{10,... | collective-permute-start | bytes 442376 | tf_op jit(solution)/shard_map/ppermute | solution.py:523
  55.5 4.5 %collective-permute-done.13.refs_5_.refs_4_ = f32[1,3,12,8,128]{4,3,2,1,0:T(8,128)S(1)} collective-permute-done((f32[1,3,12,8,128]{4,3,2,1,0:T(8,128)S(1)}, f32[1,3,12,8,128]{4,3,2,1,0:T(8,128)S(1)}, u32[]{:S(2)}, u32[]{:S(2)}) %collective-permute-start.13) | collective-permute-done | bytes 147488 | tf_op jit(solution)/shard_map/ppermute | solution.py:523
  60.0 1.4 %collective-permute-done.12.refs_1_ = f32[2,3,9,8,128]{4,3,2,1,0:T(8,128)S(1)} collective-permute-done((f32[2,3,9,8,128]{4,3,2,1,0:T(8,128)S(1)}, f32[2,3,9,8,128]{4,3,2,1,0:T(8,128)S(1)}, u32[]{:S(2)}, u32[]{:S(2)}) %collective-permute-start.12) | collective-permute-done | bytes 221216 | tf_op jit(solution)/shard_map/ppermute | solution.py:523
  61.4 1.3 %collective-permute-start.14 = (f32[1,3,9,8,128]{4,3,2,1,0:T(8,128)S(1)}, f32[1,3,9,8,128]{4,3,2,1,0:T(8,128)S(1)}, u32[]{:S(2)}, u32[]{:S(2)}) collective-permute-start(f32[1,3,9,8,128]{4,3,2,1,0:T(8,128)S(1)} %get-tuple-element.59), channel_id=1, source_target_pairs={{0,4},{1,5},{2,6},{3,7},{4,0},{5,1},{6,2},{7,3},{8,12},{9,13},{10,... | collective-permute-start | bytes 331784 | tf_op jit(solution)/shard_map/ppermute | solution.py:523
  62.7 4.5 %collective-permute-done.14.refs_5_ = f32[1,3,9,8,128]{4,3,2,1,0:T(8,128)S(1)} collective-permute-done((f32[1,3,9,8,128]{4,3,2,1,0:T(8,128)S(1)}, f32[1,3,9,8,128]{4,3,2,1,0:T(8,128)S(1)}, u32[]{:S(2)}, u32[]{:S(2)}) %collective-permute-start.14) | collective-permute-done | bytes 110624 | tf_op jit(solution)/shard_map/ppermute | solution.py:523
  67.2 0.9 %last.1 = f32[4,8,4096]{2,1,0:T(8,128)} custom-call(f32[1,3,11,8,128]{4,3,2,1,0:T(8,128)S(1)} %get-tuple-element.47.refs_0_, f32[1,3,12,8,128]{4,3,2,1,0:T(8,128)S(1)} %get-tuple-element.53.refs_1_, f32[1,3,9,8,128]{4,3,2,1,0:T(8,128)S(1)} %get-tuple-element.58.refs_2_, f32[1,3,11,8,128]{4,3,2,1,0:T(8,128)S(1)} %collective-permute-done.10.refs_5_.refs_3_, ...), custom_call_target="tpu_custom_call" | custom-call | tf_op jit(solution)/shard_map/last/pallas_call | solution.py:511
  (18 shorter events, 0.2 us)
Async XLA Ops:
  0.7 0.7 %copy-start.2 = (f32[8,4,16]{2,1,0:T(4,128)S(1)}, f32[8,4,16]{2,1,0:T(4,128)}, u32[]{:S(2)}) copy-start(f32[8,4,16]{2,1,0:T(4,128)} %tables_ref.1) | copy-start | bytes 6148
  8.5 9.7 %collective-permute-start = (f32[4,32,8,128]{3,2,1,0:T(8,128)S(1)}, f32[4,32,8,128]{3,2,1,0:T(8,128)S(1)}, u32[]{:S(2)}, u32[]{:S(2)}) collective-permute-start(f32[4,32,8,128]{3,2,1,0:T(8,128)S(1)} %get-tuple-element.37), channel_id=1, source_target_pairs={{0,1},{1,0},{2,3},{3,2},{4,5},{5,4},{6,7},{7,6},{8,9},{9,8},{10,11... | collective-permute-start | bytes 1572872 | tf_op jit(solution)/shard_map/ppermute | solution.py:523
  9.0 15.6 %collective-permute-start.3 = (f32[8,4096]{1,0:T(8,128)S(1)}, f32[8,4096]{1,0:T(8,128)S(1)}, u32[]{:S(2)}, u32[]{:S(2)}) collective-permute-start(f32[8,4096]{1,0:T(8,128)S(1)} %get-tuple-element.39), channel_id=1, source_target_pairs={{0,24},{1,25},{2,26},{3,27},{4,28},{5,29},{6,30},{7,31}} | collective-permute-start | bytes 393224 | tf_op jit(solution)/shard_map/ppermute | solution.py:529
  14.4 10.2 %collective-permute-start.2 = (f32[8,4096]{1,0:T(8,128)S(1)}, f32[8,4096]{1,0:T(8,128)S(1)}, u32[]{:S(2)}, u32[]{:S(2)}) collective-permute-start(f32[8,4096]{1,0:T(8,128)S(1)} %get-tuple-element.39), channel_id=1, source_target_pairs={{0,16},{8,24},{1,17},{9,25},{2,18},{10,26},{3,19},{11,27},{4,20},{... | collective-permute-start | bytes 393224 | tf_op jit(solution)/shard_map/ppermute | solution.py:529
  15.7 8.9 %collective-permute-start.1 = (f32[8,4096]{1,0:T(8,128)S(1)}, f32[8,4096]{1,0:T(8,128)S(1)}, u32[]{:S(2)}, u32[]{:S(2)}) collective-permute-start(f32[8,4096]{1,0:T(8,128)S(1)} %get-tuple-element.39), channel_id=1, source_target_pairs={{0,8},{8,16},{16,24},{1,9},{9,17},{17,25},{2,10},{10,18},{18,26},{... | collective-permute-start | bytes 393224 | tf_op jit(solution)/shard_map/ppermute | solution.py:529
  18.3 8.2 %collective-permute-start.5 = (f32[2,32,8,128]{3,2,1,0:T(8,128)S(1)}, f32[2,32,8,128]{3,2,1,0:T(8,128)S(1)}, u32[]{:S(2)}, u32[]{:S(2)}) collective-permute-start(f32[2,32,8,128]{3,2,1,0:T(8,128)S(1)} %get-tuple-element.38.rest_2_), channel_id=1, source_target_pairs={{0,2},{1,3},{2,0},{3,1},{4,6},{5,7},{6,4},{7,5},{8,10},{9,11},{10,... | collective-permute-start | bytes 786440 | tf_op jit(solution)/shard_map/ppermute | solution.py:523
  20.0 4.7 %copy-start = (f32[4,3]{1,0:T(4,128)S(1)}, f32[4,3]{1,0:T(4,128)}, u32[]{:S(2)}) copy-start(f32[4,3]{1,0:T(4,128)} %tint_ref.5) | copy-start | bytes 148
  20.0 4.7 %copy-start.1 = (s32[4]{0:T(128)S(1)}, s32[4]{0:T(128)}, u32[]{:S(2)}) copy-start(s32[4]{0:T(128)} %code_ref.5) | copy-start | bytes 52
  26.4 2.8 %collective-permute-start.4 = (f32[4,3,11,8,128]{4,3,2,1,0:T(8,128)S(1)}, f32[4,3,11,8,128]{4,3,2,1,0:T(8,128)S(1)}, u32[]{:S(2)}, u32[]{:S(2)}) collective-permute-start(f32[4,3,11,8,128]{4,3,2,1,0:T(8,128)S(1)} %get-tuple-element.41.rest_0_), channel_id=1, source_target_pairs={{0,1},{1,0},{2,3},{3,2},{4,5},{5,4},{6,7},{7,6},{8,9},{9,8},{10,11... | collective-permute-start | bytes 1622024 | tf_op jit(solution)/shard_map/ppermute | solution.py:523
  26.5 11.3 %collective-permute-start.7 = (f32[1,32,8,128]{3,2,1,0:T(8,128)S(1)}, f32[1,32,8,128]{3,2,1,0:T(8,128)S(1)}, u32[]{:S(2)}, u32[]{:S(2)}) collective-permute-start(f32[1,32,8,128]{3,2,1,0:T(8,128)S(1)} %get-tuple-element.43.refs_4_), channel_id=1, source_target_pairs={{0,4},{1,5},{2,6},{3,7},{4,0},{5,1},{6,2},{7,3},{8,12},{9,13},{10,... | collective-permute-start | bytes 393224 | tf_op jit(solution)/shard_map/ppermute | solution.py:523
  29.3 11.2 %collective-permute-start.6 = (f32[2,3,11,8,128]{4,3,2,1,0:T(8,128)S(1)}, f32[2,3,11,8,128]{4,3,2,1,0:T(8,128)S(1)}, u32[]{:S(2)}, u32[]{:S(2)}) collective-permute-start(f32[2,3,11,8,128]{4,3,2,1,0:T(8,128)S(1)} %get-tuple-element.45.rest_5_), channel_id=1, source_target_pairs={{0,2},{1,3},{2,0},{3,1},{4,6},{5,7},{6,4},{7,5},{8,10},{9,11},{10,... | collective-permute-start | bytes 811016 | tf_op jit(solution)/shard_map/ppermute | solution.py:523
  37.7 2.9 %collective-permute-start.8 = (f32[4,3,12,8,128]{4,3,2,1,0:T(8,128)S(1)}, f32[4,3,12,8,128]{4,3,2,1,0:T(8,128)S(1)}, u32[]{:S(2)}, u32[]{:S(2)}) collective-permute-start(f32[4,3,12,8,128]{4,3,2,1,0:T(8,128)S(1)} %get-tuple-element.46.refs_4_), channel_id=1, source_target_pairs={{0,1},{1,0},{2,3},{3,2},{4,5},{5,4},{6,7},{7,6},{8,9},{9,8},{10,11... | collective-permute-start | bytes 1769480 | tf_op jit(solution)/shard_map/ppermute | solution.py:523
  40.6 8.8 %collective-permute-start.10 = (f32[1,3,11,8,128]{4,3,2,1,0:T(8,128)S(1)}, f32[1,3,11,8,128]{4,3,2,1,0:T(8,128)S(1)}, u32[]{:S(2)}, u32[]{:S(2)}) collective-permute-start(f32[1,3,11,8,128]{4,3,2,1,0:T(8,128)S(1)} %get-tuple-element.49.refs_4_), channel_id=1, source_target_pairs={{0,4},{1,5},{2,6},{3,7},{4,0},{5,1},{6,2},{7,3},{8,12},{9,13},{10,... | collective-permute-start | bytes 405512 | tf_op jit(solution)/shard_map/ppermute | solution.py:523
  40.8 11.2 %collective-permute-start.9 = (f32[2,3,12,8,128]{4,3,2,1,0:T(8,128)S(1)}, f32[2,3,12,8,128]{4,3,2,1,0:T(8,128)S(1)}, u32[]{:S(2)}, u32[]{:S(2)}) collective-permute-start(f32[2,3,12,8,128]{4,3,2,1,0:T(8,128)S(1)} %get-tuple-element.51.rest_5_), channel_id=1, source_target_pairs={{0,2},{1,3},{2,0},{3,1},{4,6},{5,7},{6,4},{7,5},{8,10},{9,11},{10,... | collective-permute-start | bytes 884744 | tf_op jit(solution)/shard_map/ppermute | solution.py:523
  47.8 4.3 %collective-permute-start.11 = (f32[4,3,9,8,128]{4,3,2,1,0:T(8,128)S(1)}, f32[4,3,9,8,128]{4,3,2,1,0:T(8,128)S(1)}, u32[]{:S(2)}, u32[]{:S(2)}) collective-permute-start(f32[4,3,9,8,128]{4,3,2,1,0:T(8,128)S(1)} %get-tuple-element.52.refs_4_), channel_id=1, source_target_pairs={{0,1},{1,0},{2,3},{3,2},{4,5},{5,4},{6,7},{7,6},{8,9},{9,8},{10,11... | collective-permute-start | bytes 1327112 | tf_op jit(solution)/shard_map/ppermute | solution.py:523
  52.2 9.2 %collective-permute-start.12 = (f32[2,3,9,8,128]{4,3,2,1,0:T(8,128)S(1)}, f32[2,3,9,8,128]{4,3,2,1,0:T(8,128)S(1)}, u32[]{:S(2)}, u32[]{:S(2)}) collective-permute-start(f32[2,3,9,8,128]{4,3,2,1,0:T(8,128)S(1)} %get-tuple-element.57.refs_4_), channel_id=1, source_target_pairs={{0,2},{1,3},{2,0},{3,1},{4,6},{5,7},{6,4},{7,5},{8,10},{9,11},{10,... | collective-permute-start | bytes 663560 | tf_op jit(solution)/shard_map/ppermute | solution.py:523
  52.3 7.7 %collective-permute-start.13 = (f32[1,3,12,8,128]{4,3,2,1,0:T(8,128)S(1)}, f32[1,3,12,8,128]{4,3,2,1,0:T(8,128)S(1)}, u32[]{:S(2)}, u32[]{:S(2)}) collective-permute-start(f32[1,3,12,8,128]{4,3,2,1,0:T(8,128)S(1)} %get-tuple-element.55.refs_4_), channel_id=1, source_target_pairs={{0,4},{1,5},{2,6},{3,7},{4,0},{5,1},{6,2},{7,3},{8,12},{9,13},{10,... | collective-permute-start | bytes 442376 | tf_op jit(solution)/shard_map/ppermute | solution.py:523
  61.4 5.7 %collective-permute-start.14 = (f32[1,3,9,8,128]{4,3,2,1,0:T(8,128)S(1)}, f32[1,3,9,8,128]{4,3,2,1,0:T(8,128)S(1)}, u32[]{:S(2)}, u32[]{:S(2)}) collective-permute-start(f32[1,3,9,8,128]{4,3,2,1,0:T(8,128)S(1)} %get-tuple-element.59), channel_id=1, source_target_pairs={{0,4},{1,5},{2,6},{3,7},{4,0},{5,1},{6,2},{7,3},{8,12},{9,13},{10,... | collective-permute-start | bytes 331784 | tf_op jit(solution)/shard_map/ppermute | solution.py:523
